TPU v7x, 256 devices: a whole 4x4x8 slice. The times are simulated.
256 devices in a mesh: section: 16 (over x, z_hi), tensor: 16 (over y, z_lo, core).
Axes of the slice: x: 4, y: 4, z: 8 (z_hi: 4, z_lo: 2; z = z_hi * 2 + z_lo), core: 2. Of those that a mesh axis runs over, the one named last changes fastest.
Arguments:
- weight_q: bfloat16 [16, 4096, 4096], P('section', None, 'tensor'), as said below
- weight_kv: bfloat16 [16, 4096, 4096], P('section', None, 'tensor'), as said below
- weight_o: bfloat16 [16, 4096, 4096], P('section', None, 'tensor'), as said below
- section_inputs: bfloat16 [2, 2, 16, 128, 4096], P(None, None, 'section', None, 'tensor')
- saved_q: bfloat16 [2, 2, 16, 128, 4096], P(None, None, 'section', None, 'tensor')
- saved_kv: bfloat16 [2, 2, 16, 128, 4096], P(None, None, 'section', None, 'tensor'), as said below
- out_grads: bfloat16 [2, 16, 128, 4096], P(None, 'section', None, 'tensor'), may hold values from -6 to 6
Outputs:
- input_grads: bfloat16 [2, 2, 16, 128, 4096], P(None, None, 'section', None, 'tensor')
- grad_query: bfloat16 [16, 2048, 4096], P('section', None, 'tensor')
- grad_kv: bfloat16 [16, 512, 4096], P('section', None, 'tensor')
- grad_output: bfloat16 [16, 2048, 4096], P('section', None, 'tensor')
Inputs may be any that keep to these rules, and one draw needn't show every extreme that they name: weight_q[s] equals weight_q[15 - s] for every s. weight_o[s] equals weight_o[15 - s] for every s. weight_kv[s] equals weight_kv[15 - s]; column blocks c and u (256 wide) are equal whenever c // 4 == u // 4. `saved_kv`: column blocks c and u (256 wide) are equal whenever c // 4 == u // 4.
All inputs are finite; a program needn't handle non-finite values.
Results may differ from a plain program's by a relative error of at most 0.018.
Values may be sent and summed in bfloat16 or wider, within the bound.
No kernel may reach another device: no remote copies, remote signals or barrier semaphores. Data moves between devices by JAX's collectives and lax.ppermute only.
A program may use at most 128 MiB of HBM per device.

v0:
```python
import jax
import jax.numpy as jnp
from jax import lax
from jax.sharding import PartitionSpec as P

KV = 4
HD = 128
TICKS = 2


def from_behind(block, axis, distance):
    devices = range(lax.axis_size(axis))
    route = [(i - distance, i) for i in devices if i - distance in devices]
    return lax.ppermute(block, axis, route)


def from_partner(x, axis, stride):
    return lax.ppermute(x, axis, [(i, i ^ 1 << stride) for i in range(lax.axis_size(axis))])


def lower_upper(matrix, upper_half):
    rows_half = matrix.shape[0] // 2
    kept = lax.dynamic_slice_in_dim(matrix, upper_half * rows_half, rows_half, 0)
    given = lax.dynamic_slice_in_dim(matrix, (1 - upper_half) * rows_half, rows_half, 0)
    return (kept, given)


def on_device(weight_q, weight_kv, weight_o, section_inputs, saved_q, saved_kv, out_grads):
    sections = lax.axis_size("section")
    tensors = lax.axis_size("tensor")
    position = lax.axis_index("section")
    column = lax.axis_index("tensor")
    w_query = weight_q[0]
    w_pairs = weight_kv[0]
    w_out = weight_o[0]
    width = w_query.shape[0]
    local_width = section_inputs.shape[-1]
    tokens = section_inputs.shape[3]
    heads_here = saved_q.shape[-1] // HD
    score_scale = HD ** (-0.5)
    causal = jnp.arange(tokens)[:, None] >= jnp.arange(tokens)[None, :]
    grad_here = out_grads[:, 0]
    acc_query = jnp.zeros(w_query.shape, jnp.float32)
    acc_pairs = jnp.zeros(w_pairs.shape, jnp.float32)
    acc_output = jnp.zeros(w_out.shape, jnp.float32)
    produced = []
    for tick_index in range(TICKS):
        rows_in, grad_full = (
            lax.all_gather(section_inputs[:, tick_index, 0], "tensor", axis=2, tiled=True),
            lax.all_gather(grad_here, "tensor", axis=2, tiled=True),
        )
        rows_f = rows_in.astype(jnp.float32)
        inverse = lax.rsqrt(jnp.mean(rows_f * rows_f, axis=-1, keepdims=True) + 1e-06)
        normed = rows_f * inverse
        normed_b = normed.astype(jnp.bfloat16)
        queries = saved_q[:, tick_index, 0].reshape(2, tokens, heads_here, HD)
        pair_rows = saved_kv[:, tick_index, 0]
        key_rows = pair_rows[..., :HD]
        value_rows = pair_rows[..., HD:]
        scores = (
            jnp.einsum("riae,rje->raij", queries, key_rows, preferred_element_type=jnp.float32)
            * score_scale
        )
        scores = jnp.where(causal, scores, -1e30)
        attention = jax.nn.softmax(scores, axis=-1)
        attention_b = attention.astype(jnp.bfloat16)
        attended = (
            jnp.einsum(
                "raij,rje->riae", attention_b, value_rows, preferred_element_type=jnp.float32
            )
            .astype(jnp.bfloat16)
            .reshape(2, tokens, heads_here * HD)
        )
        grad_attn = jnp.einsum(
            "rtd,dc->rtc", grad_full, w_out, preferred_element_type=jnp.float32
        ).astype(jnp.bfloat16)
        grad_heads = grad_attn.reshape(2, tokens, heads_here, HD)
        grad_probs = jnp.einsum(
            "riae,rje->raij", grad_heads, value_rows, preferred_element_type=jnp.float32
        )
        row_delta = jnp.sum(attention * grad_probs, axis=-1, keepdims=True)
        grad_scores = (attention * (grad_probs - row_delta) * score_scale).astype(jnp.bfloat16)
        query_grad = (
            jnp.einsum("raij,rje->riae", grad_scores, key_rows, preferred_element_type=jnp.float32)
            .astype(jnp.bfloat16)
            .reshape(2, tokens, heads_here * HD)
        )
        grad_key = jnp.einsum(
            "raij,riae->rje", grad_scores, queries, preferred_element_type=jnp.float32
        )
        grad_value = jnp.einsum(
            "raij,riae->rje", attention_b, grad_heads, preferred_element_type=jnp.float32
        )
        grad_pairs = jnp.concatenate([grad_key, grad_value], axis=-1).astype(jnp.bfloat16)
        partial_normed = jnp.einsum(
            "rtc,dc->rtd", query_grad, w_query, preferred_element_type=jnp.float32
        ) + jnp.einsum("rte,de->rtd", grad_pairs, w_pairs, preferred_element_type=jnp.float32)
        normed_here = lax.dynamic_slice_in_dim(normed, column * local_width, local_width, 2)
        grad_normed = lax.psum_scatter(partial_normed, "tensor", scatter_dimension=2, tiled=True)
        row_sums = lax.psum(jnp.sum(grad_normed * normed_here, axis=-1, keepdims=True), "tensor")
        grad_in = (
            grad_here.astype(jnp.float32) + inverse * (grad_normed - normed_here * row_sums / width)
        ).astype(jnp.bfloat16)
        produced.append(grad_in)
        acc_output = acc_output + jnp.einsum(
            "rtd,rtc->dc", grad_full, attended, preferred_element_type=jnp.float32
        )
        acc_query = acc_query + jnp.einsum(
            "rtd,rtc->dc", normed_b, query_grad, preferred_element_type=jnp.float32
        )
        acc_pairs = acc_pairs + jnp.einsum(
            "rtd,rte->de", normed_b, grad_pairs, preferred_element_type=jnp.float32
        )
        if tick_index + 1 < TICKS:
            from_above = from_behind(grad_in[0], "section", -1)
            from_below = from_behind(grad_in[1], "section", 1)
            grad_here = jnp.stack([from_above, from_below])
    group_size = tensors // KV
    member = column % group_size
    reduced = acc_pairs
    for bit_index in range(group_size.bit_length() - 2, -1, -1):
        rows_half = reduced.shape[0] // 2
        which_half = member // 2**bit_index % 2
        kept_rows = lax.dynamic_slice_in_dim(reduced, which_half * rows_half, rows_half, 0)
        given_rows = lax.dynamic_slice_in_dim(reduced, (1 - which_half) * rows_half, rows_half, 0)
        reduced = kept_rows + from_partner(given_rows, "tensor", bit_index)
    upper_half = (position >= sections // 2).astype(jnp.int32)
    keep_query, send_query = lower_upper(acc_query.astype(jnp.bfloat16), upper_half)
    keep_output, send_output = lower_upper(acc_output.astype(jnp.bfloat16), upper_half)
    keep_pairs, send_pairs = lower_upper(reduced.astype(jnp.bfloat16), upper_half)
    spread = (
        lax.all_to_all(
            send_query.reshape(sections, -1, send_query.shape[1]),
            "section",
            split_axis=0,
            concat_axis=0,
            tiled=True,
        ),
        lax.all_to_all(
            send_output.reshape(sections, -1, send_output.shape[1]),
            "section",
            split_axis=0,
            concat_axis=0,
            tiled=True,
        ),
        lax.all_to_all(
            send_pairs.reshape(sections, -1, send_pairs.shape[1]),
            "section",
            split_axis=0,
            concat_axis=0,
            tiled=True,
        ),
    )
    collected = (
        lax.all_to_all(jnp.flip(spread[0], 0), "section", split_axis=0, concat_axis=0, tiled=True),
        lax.all_to_all(jnp.flip(spread[1], 0), "section", split_axis=0, concat_axis=0, tiled=True),
        lax.all_to_all(jnp.flip(spread[2], 0), "section", split_axis=0, concat_axis=0, tiled=True),
    )
    received_query = collected[0].reshape(send_query.shape)
    received_output = collected[1].reshape(send_output.shape)
    received_pairs = collected[2].reshape(send_pairs.shape)
    query_total = (keep_query.astype(jnp.float32) + received_query.astype(jnp.float32)).astype(
        jnp.bfloat16
    )
    output_total = (keep_output.astype(jnp.float32) + received_output.astype(jnp.float32)).astype(
        jnp.bfloat16
    )
    pairs_total = (keep_pairs.astype(jnp.float32) + received_pairs.astype(jnp.float32)).astype(
        jnp.bfloat16
    )
    input_grads = jnp.stack(produced, axis=1)[:, :, None]
    return (input_grads, query_total[None], pairs_total[None], output_total[None])


def solution(mesh):
    placed = (
        P("section", None, "tensor"),
        P("section", None, "tensor"),
        P("section", None, "tensor"),
        P(None, None, "section", None, "tensor"),
        P(None, None, "section", None, "tensor"),
        P(None, None, "section", None, "tensor"),
        P(None, "section", None, "tensor"),
    )
    return jax.shard_map(
        on_device,
        mesh=mesh,
        in_specs=placed,
        out_specs=(
            P(None, None, "section", None, "tensor"),
            P("section", None, "tensor"),
            P("section", None, "tensor"),
            P("section", None, "tensor"),
        ),
        check_vma=False,
    )
```

profile of v0, /device:TPU:96, one launch (start us, length us, event | category | flops | bytes accessed | tf_op | source)
XLA Modules:
  0.0 538.9 jit_solution(15406723498126992042)
XLA Ops:
  8.0 1.7 slice_bitcast_fusion.1
  12.8 38.5 %all-gather.12.cloned.1.call-done = bf16[2,1,128,4096]{3,2,0,1:T(8,128)(2,1)} async-done(((bf16[2,1,128,256]{3,2,0,1:T(8,128)(2,1)}), bf16[2,1,128,4096]{3,2,0,1:T(8,128)(2,1)}) %all-gather.12.cloned.1.call-update) | async-done | bytes 2097168 | tf_op jit(solution)/shard_map/all_gather | solution.py:50
  51.3 2.9 fusion.41
  55.9 1.3 fusion.49
  59.1 2.7 convolution_add_fusion.1
  62.5 31.1 %all-gather.10.cloned.1.call-done = bf16[2,1,1,128,4096]{4,3,0,2,1:T(8,128)(2,1)} async-done(((bf16[2,1,1,128,256]{4,3,0,2,1:T(8,128)(2,1)}), bf16[2,1,1,128,4096]{4,3,0,2,1:T(8,128)(2,1)}) %all-gather.10.cloned.1.call-update) | async-done | bytes 2097168 | tf_op jit(solution)/shard_map/all_gather | solution.py:49
  93.6 2.2 fusion.9
  95.9 2.5 convert_multiply_fusion.2
  98.4 65.6 %reduce-scatter.3.cloned.1.call-done = f32[2,128,256]{2,1,0:T(8,128)} async-done(((f32[2,128,4096]{2,1,0:T(8,128)}), f32[2,128,256]{2,1,0:T(8,128)}) %reduce-scatter.3.cloned.1.call-update) | async-done | bytes 262160 | tf_op jit(solution)/shard_map/reduce_scatter | solution.py:99
  165.2 29.4 %psum.14 = f32[2,128]{1,0:T(2,128)S(1)} all-reduce(f32[2,128]{1,0:T(2,128)S(1)} %multiply_reduce_fusion.3), channel_id=1, replica_groups=mesh['section'=16,'tensor'=16] {'tensor'}, use_global_device_ids=true, to_apply=%region_6.7 | all-reduce | flops 256 | bytes 2048 | tf_op jit(solution)/shard_map/psum | solution.py:100
  195.8 4.8 collective-permute-start.1
  200.6 1.9 collective-permute-start
  203.0 6.7 %collective-permute-done = bf16[128,256]{1,0:T(8,128)(2,1)S(1)} collective-permute-done((bf16[128,256]{1,0:T(8,128)(2,1)S(1)}, bf16[128,256]{1,0:T(8,128)(2,1)S(1)}, u32[]{:S(2)}, u32[]{:S(2)}) %collective-permute-start) | collective-permute-done | bytes 65568 | tf_op jit(solution)/shard_map/ppermute | solution.py:14
  211.8 1.6 fusion.99
  213.4 2.1 fusion.10
  215.5 36.0 %all-gather.8.cloned.1.call-done = bf16[2,128,4096]{2,1,0:T(8,128)(2,1)} async-done(((bf16[2,128,256]{2,1,0:T(8,128)(2,1)}), bf16[2,128,4096]{2,1,0:T(8,128)(2,1)}) %all-gather.8.cloned.1.call-update) | async-done | bytes 2097168 | tf_op jit(solution)/shard_map/all_gather | solution.py:50
  251.5 2.9 fusion.46
  255.8 1.3 convolution_convert_fusion.2
  257.1 1.3 fusion.51
  258.4 2.8 convolution_bitcast_fusion.2
  262.4 1.4 constant_dynamic-slice_fusion.3
  263.8 1.3 copy-done.6
  268.2 1.4 copy-done.7
  270.6 9.6 %all-to-all-start = ((bf16[16,128,256]{2,1,0:T(8,128)(2,1)}), bf16[16,128,256]{2,1,0:T(8,128)(2,1)}, u32[]{:S(2)}, u32[]{:S(2)}) async-start(bf16[16,128,256]{2,1,0:T(8,128)(2,1)} %bitcast.55), calls=%async_computation.2 | async-start | bytes 2097152 | tf_op jit(solution)/shard_map/all_to_all | solution.py:132
  281.8 2.7 convolution_add_fusion
  288.5 1.6 copy.180
  290.1 2.3 copy.181
  292.4 80.9 %all-to-all-done = bf16[16,128,256]{2,1,0:T(8,128)(2,1)} async-done(((bf16[16,128,256]{2,1,0:T(8,128)(2,1)}), bf16[16,128,256]{2,1,0:T(8,128)(2,1)}, u32[]{:S(2)}, u32[]{:S(2)}) %all-to-all-start) | async-done | bytes 1048608 | tf_op jit(solution)/shard_map/all_to_all | solution.py:132
  373.3 5.5 %all-to-all-start.4 = ((bf16[16,128,256]{1,2,0:T(8,128)(2,1)}), bf16[16,128,256]{1,2,0:T(8,128)(2,1)S(1)}, u32[]{:S(2)}, u32[]{:S(2)}) async-start(bf16[16,128,256]{1,2,0:T(8,128)(2,1)} %copy.181), calls=%async_computation.6 | async-start | bytes 2097152 | tf_op jit(solution)/shard_map/all_to_all | solution.py:139
  378.9 2.5 dynamic-slice_add_fusion
  382.4 3.0 collective-permute-done.3
  385.4 1.3 add_convert_fusion
  388.3 17.2 %all-to-all-done.4 = bf16[16,128,256]{1,2,0:T(8,128)(2,1)S(1)} async-done(((bf16[16,128,256]{1,2,0:T(8,128)(2,1)}), bf16[16,128,256]{1,2,0:T(8,128)(2,1)S(1)}, u32[]{:S(2)}, u32[]{:S(2)}) %all-to-all-start.4) | async-done | bytes 1048608 | tf_op jit(solution)/shard_map/all_to_all | solution.py:139
  405.5 4.5 all-to-all-start.2
  411.1 9.8 %all-to-all-done.2 = bf16[16,32,256]{2,1,0:T(8,128)(2,1)S(1)} async-done(((bf16[16,32,256]{2,1,0:T(8,128)(2,1)}), bf16[16,32,256]{2,1,0:T(8,128)(2,1)S(1)}, u32[]{:S(2)}, u32[]{:S(2)}) %all-to-all-start.2) | async-done | bytes 262176 | tf_op jit(solution)/shard_map/all_to_all | solution.py:146
  420.8 6.7 %all-to-all-start.5 = ((bf16[16,128,256]{1,2,0:T(8,128)(2,1)}), bf16[16,128,256]{1,2,0:T(8,128)(2,1)S(1)}, u32[]{:S(2)}, u32[]{:S(2)}) async-start(bf16[16,128,256]{1,2,0:T(8,128)(2,1)} %rev.13), calls=%async_computation.7 | async-start | bytes 2097152 | tf_op jit(solution)/shard_map/all_to_all | solution.py:156
  427.6 2.4 rev.11
  430.0 21.3 %all-to-all-done.5 = bf16[16,128,256]{1,2,0:T(8,128)(2,1)S(1)} async-done(((bf16[16,128,256]{1,2,0:T(8,128)(2,1)}), bf16[16,128,256]{1,2,0:T(8,128)(2,1)S(1)}, u32[]{:S(2)}, u32[]{:S(2)}) %all-to-all-start.5) | async-done | bytes 1048608 | tf_op jit(solution)/shard_map/all_to_all | solution.py:156
  452.3 7.3 %all-to-all-start.1 = ((bf16[16,128,256]{2,1,0:T(8,128)(2,1)}), bf16[16,128,256]{2,1,0:T(8,128)(2,1)S(1)}, u32[]{:S(2)}, u32[]{:S(2)}) async-start(bf16[16,128,256]{2,1,0:T(8,128)(2,1)} %rev.11), calls=%async_computation.3 | async-start | bytes 2097152 | tf_op jit(solution)/shard_map/all_to_all | solution.py:155
  459.6 2.5 convert_multiply_fusion
  462.8 1.8 fusion.54
  464.6 1.3 copy.184
  465.9 14.4 %all-to-all-done.1 = bf16[16,128,256]{2,1,0:T(8,128)(2,1)S(1)} async-done(((bf16[16,128,256]{2,1,0:T(8,128)(2,1)}), bf16[16,128,256]{2,1,0:T(8,128)(2,1)S(1)}, u32[]{:S(2)}, u32[]{:S(2)}) %all-to-all-start.1) | async-done | bytes 1048608 | tf_op jit(solution)/shard_map/all_to_all | solution.py:155
  480.3 10.6 %all-to-all-start.3 = ((bf16[16,32,256]{2,1,0:T(8,128)(2,1)}), bf16[16,32,256]{2,1,0:T(8,128)(2,1)S(1)}, u32[]{:S(2)}, u32[]{:S(2)}) async-start(bf16[16,32,256]{2,1,0:T(8,128)(2,1)} %rev.12), calls=%async_computation.5 | async-start | bytes 524288 | tf_op jit(solution)/shard_map/all_to_all | solution.py:157
  490.9 2.7 fusion.53
  493.6 7.6 %all-to-all-done.3 = bf16[16,32,256]{2,1,0:T(8,128)(2,1)S(1)} async-done(((bf16[16,32,256]{2,1,0:T(8,128)(2,1)}), bf16[16,32,256]{2,1,0:T(8,128)(2,1)S(1)}, u32[]{:S(2)}, u32[]{:S(2)}) %all-to-all-start.3) | async-done | bytes 262176 | tf_op jit(solution)/shard_map/all_to_all | solution.py:157
  501.2 1.7 fusion.68
  504.1 26.1 %psum.15 = f32[2,128]{1,0:T(2,128)S(1)} all-reduce(f32[2,128]{1,0:T(2,128)S(1)} %multiply_reduce_fusion.2), channel_id=1, replica_groups=mesh['section'=16,'tensor'=16] {'tensor'}, use_global_device_ids=true, to_apply=%region_13.14 | all-reduce | flops 256 | bytes 2048 | tf_op jit(solution)/shard_map/psum | solution.py:100
  (92 shorter events, 33.3 us)
Async XLA Ops:
  7.2 50.4 %copy-start = (bf16[1,4096,256]{2,1,0:T(8,128)(2,1)S(1)}, bf16[1,4096,256]{2,1,0:T(8,128)(2,1)}, u32[]{:S(2)}) copy-start(bf16[1,4096,256]{2,1,0:T(8,128)(2,1)} %param.7) | copy-start | bytes 6291460
  7.2 44.2 %all-gather.12.cloned.1.call-start = ((), (), s32[]{:S(2)}) async-start(), calls=%async_computation.12 | async-start | bytes 2228224 | tf_op jit(solution)/shard_map/all_gather | solution.py:50
  7.9 85.7 %all-gather.10.cloned.1.call-start = ((), (), s32[]{:S(2)}) async-start(), calls=%async_computation.11 | async-start | bytes 2228224 | tf_op jit(solution)/shard_map/all_gather | solution.py:49
  9.7 154.4 %reduce-scatter.3.cloned.1.call-start = ((), (), s32[]{:S(2)}) async-start(), calls=%async_computation.8 | async-start | bytes 4456448 | tf_op jit(solution)/shard_map/reduce_scatter | solution.py:99
  10.9 46.3 %copy-start.18 = (pred[128,128]{0,1:T(8,128)(4,1)}, pred[128,128]{0,1:T(8,128)(4,1)S(1)}, u32[]{:S(2)}) copy-start(pred[128,128]{0,1:T(8,128)(4,1)S(1)} %iota_compare_fusion) | copy-start | bytes 49156
  57.6 1.6 copy-start.9
  61.9 151.5 %all-gather.14.cloned.1.call-start = ((), (), s32[]{:S(2)}) async-start(), calls=%async_computation.13 | async-start | bytes 2228224 | tf_op jit(solution)/shard_map/all_gather | solution.py:49
  62.5 189.0 %all-gather.8.cloned.1.call-start = ((), (), s32[]{:S(2)}) async-start(), calls=%async_computation.9 | async-start | bytes 2228224 | tf_op jit(solution)/shard_map/all_gather | solution.py:50
  93.6 2.2 copy-start.4
  95.9 98.7 %copy-start.15 = (bf16[2,1,128,256]{3,2,1,0:T(8,128)(2,1)S(1)}, bf16[2,1,128,256]{3,2,1,0:T(8,128)(2,1)}, u32[]{:S(2)}) copy-start(bf16[2,1,128,256]{3,2,1,0:T(8,128)(2,1)} %param.13) | copy-start | bytes 393220
  195.8 7.2 %collective-permute-start.1 = (bf16[128,256]{1,0:T(8,128)(2,1)S(1)}, bf16[128,256]{1,0:T(8,128)(2,1)S(1)}, u32[]{:S(2)}, u32[]{:S(2)}) collective-permute-start(bf16[128,256]{1,0:T(8,128)(2,1)S(1)} %get-tuple-element.27), channel_id=1, source_target_pairs={{0,16},{16,32},{32,48},{48,64},{64,80},{80,96},{96,112},{112,128},... | collective-permute-start | bytes 196616 | tf_op jit(solution)/shard_map/ppermute | solution.py:14
  200.6 9.1 %collective-permute-start = (bf16[128,256]{1,0:T(8,128)(2,1)S(1)}, bf16[128,256]{1,0:T(8,128)(2,1)S(1)}, u32[]{:S(2)}, u32[]{:S(2)}) collective-permute-start(bf16[128,256]{1,0:T(8,128)(2,1)S(1)} %get-tuple-element.26), channel_id=1, source_target_pairs={{16,0},{32,16},{48,32},{64,48},{80,64},{96,80},{112,96},{128,112},... | collective-permute-start | bytes 196616 | tf_op jit(solution)/shard_map/ppermute | solution.py:14
  203.0 12.5 %copy-start.16 = (bf16[128,256]{1,0:T(8,128)(2,1)}, bf16[128,256]{1,0:T(8,128)(2,1)S(1)}, u32[]{:S(2)}) copy-start(bf16[128,256]{1,0:T(8,128)(2,1)S(1)} %collective-permute-done.1) | copy-start | bytes 196612
  209.7 5.8 %copy-start.17 = (bf16[128,256]{1,0:T(8,128)(2,1)}, bf16[128,256]{1,0:T(8,128)(2,1)S(1)}, u32[]{:S(2)}) copy-start(bf16[128,256]{1,0:T(8,128)(2,1)S(1)} %collective-permute-done) | copy-start | bytes 196612
  258.4 2.8 copy-start.5
  262.3 2.8 copy-start.6
  262.4 3.6 copy-start.2
  265.1 113.7 %collective-permute-start.2 = (f32[2048,256]{1,0:T(8,128)}, f32[2048,256]{1,0:T(8,128)}, u32[]{:S(2)}, u32[]{:S(2)}) collective-permute-start(f32[2048,256]{1,0:T(8,128)} %constant_dynamic-slice_fusion.3), channel_id=1, source_target_pairs={{0,2},{1,3},{2,0},{3,1},{4,6},{5,7},{6,4},{7,5},{8,10},{9,11},{10,... | collective-permute-start | bytes 6291464 | tf_op jit(solution)/shard_map/ppermute | solution.py:18
  268.2 1.4 copy-start.7
  270.6 102.8 %all-to-all-start = ((bf16[16,128,256]{2,1,0:T(8,128)(2,1)}), bf16[16,128,256]{2,1,0:T(8,128)(2,1)}, u32[]{:S(2)}, u32[]{:S(2)}) async-start(bf16[16,128,256]{2,1,0:T(8,128)(2,1)} %bitcast.55), calls=%async_computation.2 | async-start | bytes 2097152 | tf_op jit(solution)/shard_map/all_to_all | solution.py:132
  280.1 222.8 %reduce-scatter.5.cloned.1.call-start = ((), (), s32[]{:S(2)}) async-start(), calls=%async_computation.10 | async-start | bytes 4456448 | tf_op jit(solution)/shard_map/reduce_scatter | solution.py:99
  280.2 1.6 copy-start.10
  284.5 1.6 copy-start.12
  286.1 1.6 copy-start.14
  288.4 1.7 copy-start.8
  373.3 32.1 %all-to-all-start.4 = ((bf16[16,128,256]{1,2,0:T(8,128)(2,1)}), bf16[16,128,256]{1,2,0:T(8,128)(2,1)S(1)}, u32[]{:S(2)}, u32[]{:S(2)}) async-start(bf16[16,128,256]{1,2,0:T(8,128)(2,1)} %copy.181), calls=%async_computation.6 | async-start | bytes 2097152 | tf_op jit(solution)/shard_map/all_to_all | solution.py:139
  382.4 3.0 collective-permute-start.3
  386.7 0.8 copy-start.13
  405.5 15.4 %all-to-all-start.2 = ((bf16[16,32,256]{2,1,0:T(8,128)(2,1)}), bf16[16,32,256]{2,1,0:T(8,128)(2,1)S(1)}, u32[]{:S(2)}, u32[]{:S(2)}) async-start(bf16[16,32,256]{2,1,0:T(8,128)(2,1)} %bitcast.60), calls=%async_computation.4 | async-start | bytes 524288 | tf_op jit(solution)/shard_map/all_to_all | solution.py:146
  420.8 30.5 %all-to-all-start.5 = ((bf16[16,128,256]{1,2,0:T(8,128)(2,1)}), bf16[16,128,256]{1,2,0:T(8,128)(2,1)S(1)}, u32[]{:S(2)}, u32[]{:S(2)}) async-start(bf16[16,128,256]{1,2,0:T(8,128)(2,1)} %rev.13), calls=%async_computation.7 | async-start | bytes 2097152 | tf_op jit(solution)/shard_map/all_to_all | solution.py:156
  427.6 32.0 %copy-start.3 = (bf16[2,1,1,128,4096]{4,3,0,2,1:T(8,128)(2,1)S(1)}, bf16[2,1,1,128,4096]{4,3,0,2,1:T(8,128)(2,1)}, u32[]{:S(2)}) copy-start(bf16[2,1,1,128,4096]{4,3,0,2,1:T(8,128)(2,1)} %all-gather.14.cloned.1.call-done) | copy-start | bytes 6291460
  451.3 1.0 copy-start.11
  452.3 28.1 %all-to-all-start.1 = ((bf16[16,128,256]{2,1,0:T(8,128)(2,1)}), bf16[16,128,256]{2,1,0:T(8,128)(2,1)S(1)}, u32[]{:S(2)}, u32[]{:S(2)}) async-start(bf16[16,128,256]{2,1,0:T(8,128)(2,1)} %rev.11), calls=%async_computation.3 | async-start | bytes 2097152 | tf_op jit(solution)/shard_map/all_to_all | solution.py:155
  480.3 20.9 %all-to-all-start.3 = ((bf16[16,32,256]{2,1,0:T(8,128)(2,1)}), bf16[16,32,256]{2,1,0:T(8,128)(2,1)S(1)}, u32[]{:S(2)}, u32[]{:S(2)}) async-start(bf16[16,32,256]{2,1,0:T(8,128)(2,1)} %rev.12), calls=%async_computation.5 | async-start | bytes 524288 | tf_op jit(solution)/shard_map/all_to_all | solution.py:157
  490.9 41.2 %copy-start.1 = (bf16[1,4096,256]{2,1,0:T(8,128)(2,1)S(1)}, bf16[1,4096,256]{2,1,0:T(8,128)(2,1)}, u32[]{:S(2)}) copy-start(bf16[1,4096,256]{2,1,0:T(8,128)(2,1)} %param.7) | copy-start | bytes 6291460
Sparse Core Ops, SparseCore 0:
  9.8 41.5 all-gather.11
  53.7 39.9 all-gather.9
  96.2 67.8 reduce-scatter.2
  166.2 43.2 all-gather.13
  211.8 39.6 all-gather.7
  284.6 104.8 reduce-scatter.4
where the time goes:
time: 547 us; the launch traced here: 539 us
  waiting for transfers between devices  334 us (61%)
  blocking collectives  55.5 us (10%)
  starting transfers between devices  52 us (10%)
  matrix products  32.3 us (6%)
  local copies, waits for them, and re-layouts  25.9 us (5%)
  other arithmetic  24.7 us (5%)
  between operations  14.6 us (3%)
    all_to_all x1, waiting for transfers between devices, on_device(): lax.all_to_all(send_query.reshape(sections, -1, send_query.shape[1]), 'se...  80.9 us
    all_gather x2, waiting for transfers between devices, on_device(): lax.all_gather(grad_here, 'tensor', axis=2, tiled=True)  74.5 us
    reduce_scatter x2, waiting for transfers between devices, on_device(): lax.psum_scatter(partial_normed, 'tensor', scatter_dimension=2, tiled=True)  65.6 us
    psum x2, blocking collectives, on_device(): lax.psum(jnp.sum(grad_normed * normed_here, axis=-1, keepdims=True), 'ten...  55.5 us
    all_gather x2, waiting for transfers between devices, on_device(): lax.all_gather(section_inputs[:, tick_index, 0], 'tensor', axis=2, tiled=...  31.1 us
    all_to_all x1, waiting for transfers between devices, on_device(): lax.all_to_all(jnp.flip(spread[1], 0), 'section', split_axis=0, concat_ax...  21.3 us
    all_to_all x1, waiting for transfers between devices, on_device(): lax.all_to_all(send_output.reshape(sections, -1, send_output.shape[1]), '...  17.2 us
    all_to_all x1, waiting for transfers between devices, on_device(): lax.all_to_all(jnp.flip(spread[0], 0), 'section', split_axis=0, concat_ax...  14.4 us
  transfers between devices with their start and end apart: 16, of which 13 were waited for; matrix products, arithmetic and copies ran while one was open for 11% of the time, Pallas kernels for 0%

commit v1 on v0

v1 whole, which is shorter than its diff:
```python
import jax
import jax.numpy as jnp
from jax import lax
from jax.sharding import PartitionSpec as P

HD = 128
TICKS = 2
BF = jnp.bfloat16
F32 = jnp.float32

SAME_CORE = [[core + 2 * chip for chip in range(8)] for core in range(2)]


def all_pairs(route):
    pairs = []
    for section in range(16):
        for tensor in range(16):
            target = route(section, tensor)
            if target is not None:
                pairs.append((section * 16 + tensor, target[0] * 16 + target[1]))
    return pairs


def send(x, route):
    return lax.ppermute(x, ("section", "tensor"), all_pairs(route))


def swap_core(x):
    return lax.ppermute(x, "tensor", [(i, i ^ 1) for i in range(16)])


def swap_z(x):
    return lax.ppermute(x, "tensor", [(i, i ^ 2) for i in range(16)])


def mirror(x):
    return lax.ppermute(x, "section", [(i, 15 - i) for i in range(16)])


def mirror_other(x):
    return send(x, lambda s, c: (15 - s, c ^ 1))


def next_section(x):
    def route(s, c):
        target = s - 1 if c % 2 == 0 else s + 1
        return (target, c) if 0 <= target < 16 else None

    return send(x, route)


def exchange8(x):
    return lax.all_to_all(x, "tensor", 0, 0, axis_index_groups=SAME_CORE, tiled=True)


def exchange16(x):
    return lax.all_to_all(x, "tensor", 0, 0, tiled=True)


def gather8_now(x):
    out = exchange8(jnp.broadcast_to(x[None], (8,) + x.shape))
    return out.reshape((8 * x.shape[0],) + x.shape[1:])


def gather8(x):
    return lax.all_gather(x, "tensor", axis_index_groups=SAME_CORE, axis=0, tiled=True)


def dot(a, b):
    return jnp.dot(a, b, preferred_element_type=F32)


def dot_nt(a, b):
    return lax.dot_general(a, b, (((1,), (1,)), ((), ())), preferred_element_type=F32)


def dot_tn(a, b):
    return lax.dot_general(a, b, (((0,), (0,)), ((), ())), preferred_element_type=F32)


def spread(own, partner, extra=None):
    own_full = own if extra is None else jnp.concatenate([own, extra], -1)
    partner_full = partner if extra is None else jnp.concatenate([partner, extra], -1)
    return own_full, mirror(own_full), swap_core(partner_full), mirror_other(partner_full)


def on_device(weight_q, weight_kv, weight_o, section_inputs, saved_q, saved_kv, out_grads):
    position = lax.axis_index("section")
    column = lax.axis_index("tensor")
    core = column % 2
    z_low = column // 2 % 2
    half = (position >= 8).astype(jnp.int32)
    w_q, w_kv, w_o = weight_q[0], weight_kv[0], weight_o[0]
    width = w_q.shape[0]
    half_width = width // 2
    inputs = section_inputs[:, :, 0]
    grads = out_grads[:, 0]
    scale = HD ** (-0.5)

    def pick(x, index):
        return lax.dynamic_index_in_dim(x, index, 0, keepdims=False)

    def features_of(x, which):
        return lax.dynamic_slice_in_dim(x, which * half_width, half_width, x.ndim - 1)

    mixed = jnp.concatenate([grads[:, None], inputs], 1)
    mixed = mixed.reshape(2, 3, 8, 16, 256).transpose(2, 0, 1, 3, 4).reshape(16, 48, 256)
    rows = exchange16(mixed).transpose(1, 0, 2).reshape(3, 16, width)
    grad_rows = rows[0]

    w_o_both = jnp.concatenate([w_o, swap_core(w_o)], -1)
    w_q_both = jnp.concatenate([w_q, swap_core(w_q)], -1)
    queries = saved_q[:, :, 0]
    queries = jnp.concatenate([pick(queries, core), swap_core(pick(queries, 1 - core))], -1)
    pairs = pick(saved_kv[:, :, 0], core)
    keys, values = pairs[..., :HD], pairs[..., HD:]

    rows_f = rows[1:].astype(F32)
    inverse = lax.rsqrt(jnp.mean(rows_f * rows_f, axis=-1, keepdims=True) + 1e-06)
    normed = rows_f * inverse
    normed_b = normed.astype(BF)

    causal = jnp.arange(128)[:, None] >= jnp.arange(128)[None, :]
    query_heads = queries.reshape(TICKS, 128, 4, HD).transpose(0, 2, 1, 3)
    scores = jnp.einsum("taie,tje->taij", query_heads, keys, preferred_element_type=F32) * scale
    attention = jax.nn.softmax(jnp.where(causal, scores, -1e30), axis=-1)
    attention_b = attention.astype(BF)
    attended = jnp.einsum("taij,tje->tiae", attention_b, values, preferred_element_type=F32)
    attended = attended.astype(BF).reshape(TICKS, 128, 512)

    produced = []
    acc_q = acc_o = acc_kv = 0.0
    for t in range(TICKS):
        grad_full = gather8_now(grad_rows)
        grad_attn = dot(grad_full, w_o_both).astype(BF)
        grad_heads = grad_attn.reshape(128, 4, HD).transpose(1, 0, 2)
        grad_probs = jnp.einsum("aie,je->aij", grad_heads, values[t], preferred_element_type=F32)
        row_delta = jnp.sum(attention[t] * grad_probs, axis=-1, keepdims=True)
        grad_scores = (attention[t] * (grad_probs - row_delta) * scale).astype(BF)
        query_grad = jnp.einsum("aij,je->iae", grad_scores, keys[t], preferred_element_type=F32)
        query_grad = query_grad.astype(BF).reshape(128, 512)
        grad_key = jnp.einsum("aij,aie->je", grad_scores, query_heads[t], preferred_element_type=F32)
        grad_value = jnp.einsum("aij,aie->je", attention_b[t], grad_heads, preferred_element_type=F32)
        grad_pairs = jnp.concatenate([grad_key, grad_value], -1).astype(BF)
        partial = (dot_nt(query_grad, w_q_both) + dot_nt(grad_pairs, w_kv)).astype(BF)
        terms = exchange8(partial.reshape(8, 16, width))
        grad_normed = jnp.sum(terms.astype(F32), axis=0)
        row_sums = jnp.sum(grad_normed * normed[t], axis=-1, keepdims=True)
        grad_in = (
            grad_rows.astype(F32) + inverse[t] * (grad_normed - normed[t] * row_sums / width)
        ).astype(BF)
        blocks = exchange16(grad_in.reshape(16, 16, 256).transpose(1, 0, 2))
        produced.append(blocks.reshape(8, 2, 16, 256).transpose(1, 0, 2, 3).reshape(2, 128, 256))

        sent_normed = features_of(normed_b[t], 1 - half)
        sent_grad = features_of(grad_rows, 1 - half)
        far = mirror(jnp.concatenate([sent_normed, sent_grad], 0))
        x_here = gather8(jnp.concatenate([features_of(normed_b[t], half), far[:16]], 0))
        x_there = swap_core(x_here)
        g_here = jnp.concatenate([features_of(grad_full, half), gather8(far[16:])], 0)
        g_there = swap_core(g_here)
        out_parts = spread(attended[t][:, :256], attended[t][:, 256:])
        pairs_sum = (grad_pairs.astype(F32) + swap_z(grad_pairs).astype(F32)).astype(BF)
        in_parts = spread(query_grad[:, :256], query_grad[:, 256:], pairs_sum)

        acc_o = acc_o + dot_tn(g_here, jnp.concatenate(out_parts[:2], 0))
        acc_o = acc_o + dot_tn(g_there, jnp.concatenate(out_parts[2:], 0))

        def interleave(parts):
            return jnp.stack([part.reshape(8, 16, 512) for part in parts], 1).reshape(256, 512)

        in_here, in_there = interleave(in_parts[:2]), interleave(in_parts[2:])
        acc_q = acc_q + dot_tn(x_here, in_here[:, :256])
        acc_q = acc_q + dot_tn(x_there, in_there[:, :256])
        x_kv_here = lax.dynamic_slice_in_dim(x_here, core * 1024, 1024, 1)
        x_kv_there = lax.dynamic_slice_in_dim(x_there, core * 1024, 1024, 1)
        acc_kv = acc_kv + dot_tn(x_kv_here, in_here[:, 256:])
        acc_kv = acc_kv + dot_tn(x_kv_there, in_there[:, 256:])
        if t + 1 < TICKS:
            grad_rows = next_section(grad_in)

    acc_kv = acc_kv.astype(BF)
    kept = lax.dynamic_slice_in_dim(acc_kv, half * 512, 512, 0)
    given = lax.dynamic_slice_in_dim(acc_kv, (1 - half) * 512, 512, 0)
    taken = send(given, lambda s, c: (15 - s, c) if c // 2 % 2 == s // 8 else None)
    grad_kv = jnp.where(z_low == half, kept, taken)
    input_grads = jnp.stack(produced, axis=1)[:, :, None]
    return (input_grads, acc_q.astype(BF)[None], grad_kv[None], acc_o.astype(BF)[None])


def solution(mesh):
    placed = (
        P("section", None, "tensor"),
        P("section", None, "tensor"),
        P("section", None, "tensor"),
        P(None, None, "section", None, "tensor"),
        P(None, None, "section", None, "tensor"),
        P(None, None, "section", None, "tensor"),
        P(None, "section", None, "tensor"),
    )
    return jax.shard_map(
        on_device,
        mesh=mesh,
        in_specs=placed,
        out_specs=(
            P(None, None, "section", None, "tensor"),
            P("section", None, "tensor"),
            P("section", None, "tensor"),
            P("section", None, "tensor"),
        ),
        check_vma=False,
    )
```

time: 547 us -> 335 us (0.61)
  waiting for transfers between devices: 334 us -> 44.9 us
  starting transfers between devices: 52 us -> 87.7 us
  matrix products: 32.3 us -> 64.7 us
  blocking collectives: 55.5 us -> 64.1 us
  local copies, waits for them, and re-layouts: 25.9 us -> 32.5 us
    all_to_all x6 -> x7, waiting for transfers between devices: 151 us -> 2.22 us  [the longest x3 2.21 us: exchange16(): return lax.all_to_all(x, 'tensor', 0, 0, tiled=True)]
    all_gather x4 -> x2, waiting for transfers between devices: 106 us -> 0.02 us  [gather8(): lax.all_gather(x, 'tensor', axis_index_groups=SAME_CORE, axis=0, tiled=True)]
    reduce_scatter x2 -> x0, waiting for transfers between devices: 65.6 us -> none  [on_device(): lax.psum_scatter(partial_normed, 'tensor', scatter_dimension=2, tiled=True)]
    all_gather x0 -> x2, blocking collectives: none -> 64.1 us  [gather8(): lax.all_gather(x, 'tensor', axis_index_groups=SAME_CORE, axis=0, tiled=True)]
    psum x2 -> x0, blocking collectives: 55.5 us -> none  [on_device(): lax.psum(jnp.sum(grad_normed * normed_here, axis=-1, keepdims=True), 'ten...]
    ppermute x4 -> x25, starting transfers between devices: 7.51 us -> 43.8 us  [the longest x6 20.4 us: send(): return lax.ppermute(x, ('section', 'tensor'), all_pairs(route))]
    dot_general x22 -> x27, matrix products: 29.7 us -> 64.3 us  [the longest x12 31 us: dot_tn(): lax.dot_general(a, b, (((0,), (0,)), ((), ())), preferred_element_type=F32)]
    ppermute x4 -> x25, waiting for transfers between devices: 10.1 us -> 42.6 us  [the longest x6 29.6 us: mirror(): return lax.ppermute(x, 'section', [(i, 15 - i) for i in range(16)])]
  transfers between devices with their start and end apart: 16 -> 34, of which waited for: 13 -> 9; matrix products, arithmetic and copies ran while one was open for 11% -> 34% of each run, Pallas kernels for 0% -> 0%
where the time goes in v1:
time: 335 us; the launch traced here: 330 us
  starting transfers between devices  87.7 us (26%)
  matrix products  64.7 us (19%)
  blocking collectives  64.1 us (19%)
  waiting for transfers between devices  44.9 us (13%)
  local copies, waits for them, and re-layouts  32.5 us (10%)
  other arithmetic  21.4 us (6%)
  between operations  14.8 us (4%)
    all_gather x2, blocking collectives, gather8(): lax.all_gather(x, 'tensor', axis_index_groups=SAME_CORE, axis=0, tiled=True)  64.1 us
    dot_general x12, matrix products, dot_tn(): lax.dot_general(a, b, (((0,), (0,)), ((), ())), preferred_element_type=F32)  31 us
    ppermute x6, waiting for transfers between devices, mirror(): return lax.ppermute(x, 'section', [(i, 15 - i) for i in range(16)])  29.6 us
    all_to_all x4, starting transfers between devices, exchange8(): lax.all_to_all(x, 'tensor', 0, 0, axis_index_groups=SAME_CORE, tiled=True)  22.6 us
    all_to_all x3, starting transfers between devices, exchange16(): return lax.all_to_all(x, 'tensor', 0, 0, tiled=True)  21.4 us
    ppermute x6, starting transfers between devices, send(): return lax.ppermute(x, ('section', 'tensor'), all_pairs(route))  20.4 us
    ppermute x6, starting transfers between devices, mirror(): return lax.ppermute(x, 'section', [(i, 15 - i) for i in range(16)])  14.9 us
    dot_general x4, matrix products, dot_nt(): lax.dot_general(a, b, (((1,), (1,)), ((), ())), preferred_element_type=F32)  11.7 us
  transfers between devices with their start and end apart: 34, of which 9 were waited for; matrix products, arithmetic and copies ran while one was open for 34% of the time, Pallas kernels for 0%

profile of v1, /device:TPU:96, one launch (start us, length us, event | category | flops | bytes accessed | tf_op | source)
XLA Modules:
  0.0 330.0 jit_solution(16667490487278925466)
XLA Ops:
  9.2 5.9 %all-to-all-start = ((bf16[16,48,256]{2,1,0:T(8,128)(2,1)}), bf16[16,48,256]{2,1,0:T(8,128)(2,1)S(1)}, u32[]{:S(2)}, u32[]{:S(2)}) async-start(bf16[16,48,256]{2,1,0:T(8,128)(2,1)} %bitcast.4), calls=%async_computation | async-start | bytes 786432 | tf_op jit(solution)/shard_map/all_to_all | solution.py:57
  16.4 3.2 collective-permute-done
  22.9 5.5 %collective-permute-start.20 = (bf16[128,256]{0,1:T(8,128)(2,1)}, bf16[128,256]{0,1:T(8,128)(2,1)}, u32[]{:S(2)}, u32[]{:S(2)}) collective-permute-start(bf16[128,256]{0,1:T(8,128)(2,1)} %get-tuple-element.19), channel_id=1, source_target_pairs={{0,241},{1,240},{2,243},{3,242},{4,245},{5,244},{6,247},{7,246},{8... | collective-permute-start | bytes 196616 | tf_op jit(solution)/shard_map/ppermute | solution.py:25
  32.1 5.7 %all-to-all-start.1 = ((bf16[8,16,4096]{2,1,0:T(8,128)(2,1)}), bf16[8,16,4096]{2,1,0:T(8,128)(2,1)}, u32[]{:S(2)}, u32[]{:S(2)}) async-start(bf16[8,16,4096]{2,1,0:T(8,128)(2,1)} %broadcast_in_dim.45), calls=%async_computation.1 | async-start | bytes 2097152 | tf_op jit(solution)/shard_map/all_to_all | solution.py:53
  40.5 13.1 %collective-permute-done.4 = bf16[32,2048]{1,0:T(8,128)(2,1)S(1)} collective-permute-done((bf16[32,2048]{1,0:T(8,128)(2,1)S(1)}, bf16[32,2048]{1,0:T(8,128)(2,1)S(1)}, u32[]{:S(2)}, u32[]{:S(2)}) %collective-permute-start.4) | collective-permute-done | bytes 131104 | tf_op jit(solution)/shard_map/ppermute | solution.py:37
  55.0 30.8 %all_gather.14 = bf16[128,2048]{1,0:T(8,128)(2,1)S(1)} all-gather(bf16[16,2048]{1,0:T(8,128)(2,1)} %get-tuple-element.20), channel_id=1, replica_groups={{0,2,4,6,8,10,12,14},{1,3,5,7,9,11,13,15},{16,18,20,22,24,26,28,30},{17..., dimensions={0}, use_global_device_ids=true | all-gather | bytes 589824 | tf_op jit(solution)/shard_map/all_gather | solution.py:66
  85.8 4.0 %fusion.30 = bf16[128,512]{1,0:T(8,128)(2,1)} fusion(bf16[128,4096]{1,0:T(8,128)(2,1)} %bitcast.16, bf16[4096,256]{1,0:T(8,128)(2,1)} %collective-permute-done.1, bf16[4096,256]{1,0:T(8,128)(2,1)} %bitcast.292), kind=kOutput, calls=%fused_computation.45 | convolution fusion | flops 545325056 | bytes 5373952 | tf_op jit(solution)/shard_map/dot_general | solution.py:70
  91.4 1.8 fusion.89
  93.2 2.1 convolution_convert_fusion.2
  95.4 2.1 fusion.32
  98.7 1.7 fusion.15
  100.4 4.1 %fusion.3 = bf16[128,4096]{1,0:T(8,128)(2,1)} fusion(f32[128,4096]{1,0:T(8,128)S(1)} %fusion.15, bf16[128,512]{0,1:T(8,128)(2,1)S(1)} %bitcast.286, bf16[4096,256]{1,0:T(8,128)(2,1)} %collective-permute-done.2, bf16[4096,256]{1,0:T(8,128)(2,1)S(1)} %bitcast.295), kind=kOutput, calls=%fused_computation.5 | convolution fusion | flops 546308096 | bytes 7471104 | tf_op jit(solution)/shard_map/dot_general | solution.py:74
  104.5 5.5 %all-to-all-start.2 = ((bf16[8,16,4096]{2,1,0:T(8,128)(2,1)}), bf16[8,16,4096]{2,1,0:T(8,128)(2,1)}, u32[]{:S(2)}, u32[]{:S(2)}) async-start(bf16[8,16,4096]{2,1,0:T(8,128)(2,1)} %bitcast.260), calls=%async_computation.2 | async-start | bytes 2097152 | tf_op jit(solution)/shard_map/all_to_all | solution.py:53
  114.0 5.1 %collective-permute-done.5 = bf16[128,256]{0,1:T(8,128)(2,1)S(1)} collective-permute-done((bf16[128,256]{0,1:T(8,128)(2,1)S(1)}, bf16[128,256]{0,1:T(8,128)(2,1)S(1)}, u32[]{:S(2)}, u32[]{:S(2)}) %collective-permute-start.5) | collective-permute-done | bytes 65568 | tf_op jit(solution)/shard_map/ppermute | solution.py:33
  120.5 4.1 %collective-permute-start.8 = (bf16[128,512]{0,1:T(8,128)(2,1)}, bf16[128,512]{0,1:T(8,128)(2,1)}, u32[]{:S(2)}, u32[]{:S(2)}) collective-permute-start(bf16[128,512]{0,1:T(8,128)(2,1)} %get-tuple-element.37), channel_id=1, source_target_pairs={{0,1},{1,0},{2,3},{3,2},{4,5},{5,4},{6,7},{7,6},{8,9},{9,8},{10,11... | collective-permute-start | bytes 393224 | tf_op jit(solution)/shard_map/ppermute | solution.py:29
  128.7 6.0 %collective-permute-done.6 = bf16[128,512]{0,1:T(8,128)(2,1)} collective-permute-done((bf16[128,512]{0,1:T(8,128)(2,1)}, bf16[128,512]{0,1:T(8,128)(2,1)}, u32[]{:S(2)}, u32[]{:S(2)}) %collective-permute-start.6) | collective-permute-done | bytes 131104 | tf_op jit(solution)/shard_map/ppermute | solution.py:37
  138.0 5.9 %collective-permute-start.24 = (bf16[128,256]{0,1:T(8,128)(2,1)}, bf16[128,256]{0,1:T(8,128)(2,1)}, u32[]{:S(2)}, u32[]{:S(2)}) collective-permute-start(bf16[128,256]{0,1:T(8,128)(2,1)} %get-tuple-element.23), channel_id=1, source_target_pairs={{0,241},{1,240},{2,243},{3,242},{4,245},{5,244},{6,247},{7,246},{8... | collective-permute-start | bytes 196616 | tf_op jit(solution)/shard_map/ppermute | solution.py:25
  147.7 2.4 fusion.39
  151.9 3.1 fusion.72
  156.6 1.7 fusion.57
  158.3 6.9 %collective-permute-start.3 = (bf16[16,4096]{1,0:T(8,128)(2,1)}, bf16[16,4096]{1,0:T(8,128)(2,1)}, u32[]{:S(2)}, u32[]{:S(2)}) collective-permute-start(bf16[16,4096]{1,0:T(8,128)(2,1)} %fusion.57), channel_id=1, source_target_pairs={{1,17},{3,19},{5,21},{7,23},{9,25},{11,27},{13,29},{15,31},{16,0},... | collective-permute-start | bytes 393224 | tf_op jit(solution)/shard_map/ppermute | solution.py:25
  166.0 5.7 %all-to-all-start.3 = ((bf16[16,16,256]{2,1,0:T(8,128)(2,1)}), bf16[16,16,256]{2,1,0:T(8,128)(2,1)S(1)}, u32[]{:S(2)}, u32[]{:S(2)}) async-start(bf16[16,16,256]{2,1,0:T(8,128)(2,1)} %fusion.59), calls=%async_computation.3 | async-start | bytes 262144 | tf_op jit(solution)/shard_map/all_to_all | solution.py:57
  171.8 3.1 fusion.66
  174.9 2.1 all-to-all-done.3
  177.0 2.0 broadcast_in_dim.46
  179.0 5.7 %all-to-all-start.4 = ((bf16[8,16,4096]{2,1,0:T(8,128)(2,1)}), bf16[8,16,4096]{2,1,0:T(8,128)(2,1)}, u32[]{:S(2)}, u32[]{:S(2)}) async-start(bf16[8,16,4096]{2,1,0:T(8,128)(2,1)} %broadcast_in_dim.46), calls=%async_computation.4 | async-start | bytes 2097152 | tf_op jit(solution)/shard_map/all_to_all | solution.py:53
  184.7 4.0 %convolution_add_fusion.5 = f32[2048,256]{1,0:T(8,128)} fusion(f32[2048,256]{1,0:T(8,128)} %fusion.66, bf16[256,2048]{1,0:T(8,128)(2,1)} %all-gather.3.cloned.1.call-done, bf16[256,512]{1,0:T(8,128)(2,1)} %bitcast.264), kind=kOutput, calls=%fused_computation.14 | convolution fusion | flops 268959744 | bytes 5373952 | tf_op jit(solution)/shard_map/dot_general | solution.py:78
  189.5 2.3 collective-permute-start.10
  191.9 2.4 convolution_add_fusion.8
  194.9 6.7 %collective-permute-done.10 = bf16[32,2048]{1,0:T(8,128)(2,1)S(1)} collective-permute-done((bf16[32,2048]{1,0:T(8,128)(2,1)S(1)}, bf16[32,2048]{1,0:T(8,128)(2,1)S(1)}, u32[]{:S(2)}, u32[]{:S(2)}) %collective-permute-start.10) | collective-permute-done | bytes 131104 | tf_op jit(solution)/shard_map/ppermute | solution.py:37
  202.3 33.3 %all_gather.15 = bf16[128,2048]{1,0:T(8,128)(2,1)} all-gather(bf16[16,2048]{1,0:T(8,128)(2,1)S(1)} %get-tuple-element.24), channel_id=1, replica_groups={{0,2,4,6,8,10,12,14},{1,3,5,7,9,11,13,15},{16,18,20,22,24,26,28,30},{17..., dimensions={0}, use_global_device_ids=true | all-gather | bytes 589824 | tf_op jit(solution)/shard_map/all_gather | solution.py:66
  235.6 4.0 %fusion.31 = bf16[128,512]{1,0:T(8,128)(2,1)} fusion(bf16[128,4096]{1,0:T(8,128)(2,1)} %bitcast.40, bf16[4096,256]{1,0:T(8,128)(2,1)} %collective-permute-done.1, bf16[4096,256]{1,0:T(8,128)(2,1)} %bitcast.293), kind=kOutput, calls=%fused_computation.46 | convolution fusion | flops 545325056 | bytes 5373952 | tf_op jit(solution)/shard_map/dot_general | solution.py:70
  245.9 1.7 fusion.13
  247.7 4.1 %fusion.4 = bf16[128,4096]{1,0:T(8,128)(2,1)} fusion(f32[128,4096]{1,0:T(8,128)S(1)} %fusion.13, bf16[128,512]{0,1:T(8,128)(2,1)S(1)} %bitcast.288, bf16[4096,256]{1,0:T(8,128)(2,1)} %collective-permute-done.2, bf16[4096,256]{1,0:T(8,128)(2,1)S(1)} %bitcast.296), kind=kOutput, calls=%fused_computation.6 | convolution fusion | flops 546308096 | bytes 7471104 | tf_op jit(solution)/shard_map/dot_general | solution.py:74
  251.8 5.7 %all-to-all-start.5 = ((bf16[8,16,4096]{2,1,0:T(8,128)(2,1)}), bf16[8,16,4096]{2,1,0:T(8,128)(2,1)}, u32[]{:S(2)}, u32[]{:S(2)}) async-start(bf16[8,16,4096]{2,1,0:T(8,128)(2,1)} %bitcast.259), calls=%async_computation.5 | async-start | bytes 2097152 | tf_op jit(solution)/shard_map/all_to_all | solution.py:53
  258.7 2.1 pad_maximum_fusion.11
  260.8 4.7 %collective-permute-done.11 = bf16[128,256]{0,1:T(8,128)(2,1)S(1)} collective-permute-done((bf16[128,256]{0,1:T(8,128)(2,1)S(1)}, bf16[128,256]{0,1:T(8,128)(2,1)S(1)}, u32[]{:S(2)}, u32[]{:S(2)}) %collective-permute-start.11) | collective-permute-done | bytes 65568 | tf_op jit(solution)/shard_map/ppermute | solution.py:33
  266.3 3.1 collective-permute-start.14
  269.4 3.2 collective-permute-start.12
  272.6 2.7 fusion.76
  275.4 3.9 %collective-permute-done.12 = bf16[128,512]{0,1:T(8,128)(2,1)} collective-permute-done((bf16[128,512]{0,1:T(8,128)(2,1)S(1)}, bf16[128,512]{0,1:T(8,128)(2,1)}, u32[]{:S(2)}, u32[]{:S(2)}) %collective-permute-start.12) | collective-permute-done | bytes 131104 | tf_op jit(solution)/shard_map/ppermute | solution.py:37
  281.0 6.8 %collective-permute-start.17 = (bf16[128,256]{0,1:T(8,128)(2,1)}, bf16[128,256]{0,1:T(8,128)(2,1)}, u32[]{:S(2)}, u32[]{:S(2)}) collective-permute-start(bf16[128,256]{0,1:T(8,128)(2,1)} %get-tuple-element.18), channel_id=1, source_target_pairs={{0,240},{16,224},{32,208},{48,192},{64,176},{80,160},{96,144},{112... | collective-permute-start | bytes 196616 | tf_op jit(solution)/shard_map/ppermute | solution.py:37
  290.9 3.9 %convolution_add_fusion.4 = f32[2048,256]{1,0:T(8,128)} fusion(f32[2048,256]{1,0:T(8,128)} %convolution_add_fusion.5, bf16[256,2048]{1,0:T(8,128)(2,1)} %all-gather.5.cloned.1.call-done, bf16[256,512]{1,0:T(8,128)(2,1)S(1)} %bitcast.265), kind=kOutput, calls=%fused_computation.13 | convolution fusion | flops 268959744 | bytes 5373952 | tf_op jit(solution)/shard_map/dot_general | solution.py:78
  295.8 1.9 fusion.80
  298.4 2.4 fusion.11
  307.5 9.7 %all-to-all-start.6 = ((bf16[16,16,256]{2,1,0:T(8,128)(2,1)}), bf16[16,16,256]{2,1,0:T(8,128)(2,1)S(1)}, u32[]{:S(2)}, u32[]{:S(2)}) async-start(bf16[16,16,256]{2,1,0:T(8,128)(2,1)} %bitcast.242), calls=%async_computation.6 | async-start | bytes 262144 | tf_op jit(solution)/shard_map/all_to_all | solution.py:57
  317.2 3.4 %fusion.12 = bf16[1,2048,256]{2,1,0:T(8,128)(2,1)} fusion(f32[2048,256]{1,0:T(8,128)} %convolution_add_fusion.4, bf16[256,2048]{1,0:T(8,128)(2,1)} %collective-permute-done.13, bf16[256,512]{1,0:T(8,128)(2,1)S(1)} %bitcast.258), kind=kOutput, calls=%fused_computation.20 | convolution fusion | flops 269484032 | bytes 4325376 | tf_op jit(solution)/shard_map/dot_general | solution.py:78
  320.6 1.7 select_bitcast_fusion
  (203 shorter events, 62.1 us)
Async XLA Ops:
  7.2 91.5 %copy-start = (bf16[1,4096,256]{2,1,0:T(8,128)(2,1)S(1)}, bf16[1,4096,256]{2,1,0:T(8,128)(2,1)}, u32[]{:S(2)}) copy-start(bf16[1,4096,256]{2,1,0:T(8,128)(2,1)} %param.8) | copy-start | bytes 6291460
  7.2 8.1 %copy-start.24 = (bf16[2,2,1,128,256]{4,3,2,1,0:T(8,128)(2,1)S(1)}, bf16[2,2,1,128,256]{4,3,2,1,0:T(8,128)(2,1)}, u32[]{:S(2)}) copy-start(bf16[2,2,1,128,256]{4,3,2,1,0:T(8,128)(2,1)} %param.11) | copy-start | bytes 786436
  7.2 9.2 %copy-start.31 = (bf16[2,2,1,128,256]{4,3,2,1,0:T(8,128)(2,1)S(1)}, bf16[2,2,1,128,256]{4,3,2,1,0:T(8,128)(2,1)}, u32[]{:S(2)}) copy-start(bf16[2,2,1,128,256]{4,3,2,1,0:T(8,128)(2,1)} %param.12) | copy-start | bytes 786436
  9.2 21.6 %all-to-all-start = ((bf16[16,48,256]{2,1,0:T(8,128)(2,1)}), bf16[16,48,256]{2,1,0:T(8,128)(2,1)S(1)}, u32[]{:S(2)}, u32[]{:S(2)}) async-start(bf16[16,48,256]{2,1,0:T(8,128)(2,1)} %bitcast.4), calls=%async_computation | async-start | bytes 786432 | tf_op jit(solution)/shard_map/all_to_all | solution.py:57
  15.1 70.7 %collective-permute-start.1 = (bf16[4096,256]{1,0:T(8,128)(2,1)}, bf16[4096,256]{1,0:T(8,128)(2,1)}, u32[]{:S(2)}, u32[]{:S(2)}) collective-permute-start(bf16[4096,256]{1,0:T(8,128)(2,1)} %bitcast.291), channel_id=1, source_target_pairs={{0,1},{1,0},{2,3},{3,2},{4,5},{5,4},{6,7},{7,6},{8,9},{9,8},{10,11... | collective-permute-start | bytes 6291464 | tf_op jit(solution)/shard_map/ppermute | solution.py:29
  15.4 4.2 %collective-permute-start = (bf16[2,128,256]{1,2,0:T(8,128)(2,1)S(1)}, bf16[2,128,256]{1,2,0:T(8,128)(2,1)S(1)}, u32[]{:S(2)}, u32[]{:S(2)}) collective-permute-start(bf16[2,128,256]{1,2,0:T(8,128)(2,1)S(1)} %bitcast.284), channel_id=1, source_target_pairs={{0,1},{1,0},{2,3},{3,2},{4,5},{5,4},{6,7},{7,6},{8,9},{9,8},{10,11... | collective-permute-start | bytes 393224 | tf_op jit(solution)/shard_map/ppermute | solution.py:29
  15.9 84.6 %collective-permute-start.2 = (bf16[4096,256]{1,0:T(8,128)(2,1)}, bf16[4096,256]{1,0:T(8,128)(2,1)}, u32[]{:S(2)}, u32[]{:S(2)}) collective-permute-start(bf16[4096,256]{1,0:T(8,128)(2,1)} %bitcast.294), channel_id=1, source_target_pairs={{0,1},{1,0},{2,3},{3,2},{4,5},{5,4},{6,7},{7,6},{8,9},{9,8},{10,11... | collective-permute-start | bytes 6291464 | tf_op jit(solution)/shard_map/ppermute | solution.py:29
  20.1 8.3 %copy-start.20 = (bf16[2,128,2,128]{3,1,2,0:T(8,128)(2,1)S(1)}, bf16[2,128,2,128]{3,1,2,0:T(8,128)(2,1)}, u32[]{:S(2)}) copy-start(bf16[2,128,2,128]{3,1,2,0:T(8,128)(2,1)} %copy-done.19) | copy-start | bytes 393220
  21.0 11.0 %copy-start.8 = (bf16[2,4,128,128]{2,3,1,0:T(8,128)(2,1)}, bf16[2,4,128,128]{2,3,1,0:T(8,128)(2,1)S(1)}, u32[]{:S(2)}) copy-start(bf16[2,4,128,128]{2,3,1,0:T(8,128)(2,1)S(1)} %get-tuple-element.10) | copy-start | bytes 786436
  22.9 129.0 %collective-permute-start.20 = (bf16[128,256]{0,1:T(8,128)(2,1)}, bf16[128,256]{0,1:T(8,128)(2,1)}, u32[]{:S(2)}, u32[]{:S(2)}) collective-permute-start(bf16[128,256]{0,1:T(8,128)(2,1)} %get-tuple-element.19), channel_id=1, source_target_pairs={{0,241},{1,240},{2,243},{3,242},{4,245},{5,244},{6,247},{7,246},{8... | collective-permute-start | bytes 196616 | tf_op jit(solution)/shard_map/ppermute | solution.py:25
  31.0 6.8 %copy-start.11 = (bf16[16,2,8,256]{3,2,0,1:T(8,128)(2,1)}, bf16[16,2,8,256]{3,2,0,1:T(8,128)(2,1)S(1)}, u32[]{:S(2)}) copy-start(bf16[16,2,8,256]{3,2,0,1:T(8,128)(2,1)S(1)} %copy.131) | copy-start | bytes 393220
  32.1 53.7 %all-to-all-start.1 = ((bf16[8,16,4096]{2,1,0:T(8,128)(2,1)}), bf16[8,16,4096]{2,1,0:T(8,128)(2,1)}, u32[]{:S(2)}, u32[]{:S(2)}) async-start(bf16[8,16,4096]{2,1,0:T(8,128)(2,1)} %broadcast_in_dim.45), calls=%async_computation.1 | async-start | bytes 2097152 | tf_op jit(solution)/shard_map/all_to_all | solution.py:53
  37.8 109.9 %all-gather.3.cloned.1.call-start = ((), (), s32[]{:S(2)}) async-start(), calls=%async_computation.7 | async-start | bytes 1179648 | tf_op jit(solution)/shard_map/all_gather | solution.py:66
  39.3 14.3 %collective-permute-start.4 = (bf16[32,2048]{1,0:T(8,128)(2,1)S(1)}, bf16[32,2048]{1,0:T(8,128)(2,1)S(1)}, u32[]{:S(2)}, u32[]{:S(2)}) collective-permute-start(bf16[32,2048]{1,0:T(8,128)(2,1)S(1)} %pad_maximum_fusion.20), channel_id=1, source_target_pairs={{0,240},{16,224},{32,208},{48,192},{64,176},{80,160},{96,144},{112... | collective-permute-start | bytes 393224 | tf_op jit(solution)/shard_map/ppermute | solution.py:37
  104.5 50.4 %all-to-all-start.2 = ((bf16[8,16,4096]{2,1,0:T(8,128)(2,1)}), bf16[8,16,4096]{2,1,0:T(8,128)(2,1)}, u32[]{:S(2)}, u32[]{:S(2)}) async-start(bf16[8,16,4096]{2,1,0:T(8,128)(2,1)} %bitcast.260), calls=%async_computation.2 | async-start | bytes 2097152 | tf_op jit(solution)/shard_map/all_to_all | solution.py:53
  110.0 9.0 %copy-start.16 = (bf16[128,128]{0,1:T(8,128)(2,1)S(1)}, bf16[128,128]{0,1:T(8,128)(2,1)}, u32[]{:S(2)}) copy-start(bf16[128,128]{0,1:T(8,128)(2,1)} %copy-done.15) | copy-start | bytes 98308
  110.0 9.0 %copy-start.23 = (bf16[128,128]{0,1:T(8,128)(2,1)S(1)}, bf16[128,128]{0,1:T(8,128)(2,1)}, u32[]{:S(2)}) copy-start(bf16[128,128]{0,1:T(8,128)(2,1)} %fusion.32) | copy-start | bytes 98308
  110.9 8.2 %collective-permute-start.5 = (bf16[128,256]{0,1:T(8,128)(2,1)S(1)}, bf16[128,256]{0,1:T(8,128)(2,1)S(1)}, u32[]{:S(2)}, u32[]{:S(2)}) collective-permute-start(bf16[128,256]{0,1:T(8,128)(2,1)S(1)} %pad_maximum_fusion.24), channel_id=1, source_target_pairs={{0,2},{1,3},{2,0},{3,1},{4,6},{5,7},{6,4},{7,5},{8,10},{9,11},{10,... | collective-permute-start | bytes 196616 | tf_op jit(solution)/shard_map/ppermute | solution.py:33
  113.9 38.0 %collective-permute-start.18 = (bf16[256,2048]{1,0:T(8,128)(2,1)}, bf16[256,2048]{1,0:T(8,128)(2,1)}, u32[]{:S(2)}, u32[]{:S(2)}) collective-permute-start(bf16[256,2048]{1,0:T(8,128)(2,1)} %pad_maximum_fusion.10), channel_id=1, source_target_pairs={{0,1},{1,0},{2,3},{3,2},{4,5},{5,4},{6,7},{7,6},{8,9},{9,8},{10,11... | collective-permute-start | bytes 3145736 | tf_op jit(solution)/shard_map/ppermute | solution.py:29
  119.8 18.3 %collective-permute-start.9 = (bf16[128,512]{0,1:T(8,128)(2,1)}, bf16[128,512]{0,1:T(8,128)(2,1)}, u32[]{:S(2)}, u32[]{:S(2)}) collective-permute-start(bf16[128,512]{0,1:T(8,128)(2,1)} %get-tuple-element.37), channel_id=1, source_target_pairs={{0,241},{1,240},{2,243},{3,242},{4,245},{5,244},{6,247},{7,246},{8... | collective-permute-start | bytes 393224 | tf_op jit(solution)/shard_map/ppermute | solution.py:25
  120.5 25.1 %collective-permute-start.8 = (bf16[128,512]{0,1:T(8,128)(2,1)}, bf16[128,512]{0,1:T(8,128)(2,1)}, u32[]{:S(2)}, u32[]{:S(2)}) collective-permute-start(bf16[128,512]{0,1:T(8,128)(2,1)} %get-tuple-element.37), channel_id=1, source_target_pairs={{0,1},{1,0},{2,3},{3,2},{4,5},{5,4},{6,7},{7,6},{8,9},{9,8},{10,11... | collective-permute-start | bytes 393224 | tf_op jit(solution)/shard_map/ppermute | solution.py:29
  124.6 10.0 %collective-permute-start.6 = (bf16[128,512]{0,1:T(8,128)(2,1)}, bf16[128,512]{0,1:T(8,128)(2,1)}, u32[]{:S(2)}, u32[]{:S(2)}) collective-permute-start(bf16[128,512]{0,1:T(8,128)(2,1)} %get-tuple-element.36), channel_id=1, source_target_pairs={{0,240},{16,224},{32,208},{48,192},{64,176},{80,160},{96,144},{112... | collective-permute-start | bytes 393224 | tf_op jit(solution)/shard_map/ppermute | solution.py:37
  134.6 17.2 %collective-permute-start.19 = (bf16[128,256]{0,1:T(8,128)(2,1)}, bf16[128,256]{0,1:T(8,128)(2,1)}, u32[]{:S(2)}, u32[]{:S(2)}) collective-permute-start(bf16[128,256]{0,1:T(8,128)(2,1)} %get-tuple-element.19), channel_id=1, source_target_pairs={{0,1},{1,0},{2,3},{3,2},{4,5},{5,4},{6,7},{7,6},{8,9},{9,8},{10,11... | collective-permute-start | bytes 196616 | tf_op jit(solution)/shard_map/ppermute | solution.py:29
  138.0 157.7 %collective-permute-start.24 = (bf16[128,256]{0,1:T(8,128)(2,1)}, bf16[128,256]{0,1:T(8,128)(2,1)}, u32[]{:S(2)}, u32[]{:S(2)}) collective-permute-start(bf16[128,256]{0,1:T(8,128)(2,1)} %get-tuple-element.23), channel_id=1, source_target_pairs={{0,241},{1,240},{2,243},{3,242},{4,245},{5,244},{6,247},{7,246},{8... | collective-permute-start | bytes 196616 | tf_op jit(solution)/shard_map/ppermute | solution.py:25
  145.6 123.8 %collective-permute-start.21 = (bf16[128,256]{0,1:T(8,128)(2,1)}, bf16[128,256]{0,1:T(8,128)(2,1)}, u32[]{:S(2)}, u32[]{:S(2)}) collective-permute-start(bf16[128,256]{0,1:T(8,128)(2,1)} %get-tuple-element.22), channel_id=1, source_target_pairs={{0,240},{16,224},{32,208},{48,192},{64,176},{80,160},{96,144},{112... | collective-permute-start | bytes 196616 | tf_op jit(solution)/shard_map/ppermute | solution.py:37
  151.8 19.9 %collective-permute-start.7 = (bf16[256,2048]{1,0:T(8,128)(2,1)}, bf16[256,2048]{1,0:T(8,128)(2,1)}, u32[]{:S(2)}, u32[]{:S(2)}) collective-permute-start(bf16[256,2048]{1,0:T(8,128)(2,1)} %all-gather.3.cloned.1.call-done), channel_id=1, source_target_pairs={{0,1},{1,0},{2,3},{3,2},{4,5},{5,4},{6,7},{7,6},{8,9},{9,8},{10,11... | collective-permute-start | bytes 3145736 | tf_op jit(solution)/shard_map/ppermute | solution.py:29
  155.0 10.2 %copy-start.13 = (f32[2,8,16,256]{3,2,1,0:T(8,128)S(1)}, f32[2,8,16,256]{3,2,1,0:T(8,128)}, u32[]{:S(2)}) copy-start(f32[2,8,16,256]{3,2,1,0:T(8,128)} %copy.132) | copy-start | bytes 786436
  158.3 16.6 %collective-permute-start.3 = (bf16[16,4096]{1,0:T(8,128)(2,1)}, bf16[16,4096]{1,0:T(8,128)(2,1)}, u32[]{:S(2)}, u32[]{:S(2)}) collective-permute-start(bf16[16,4096]{1,0:T(8,128)(2,1)} %fusion.57), channel_id=1, source_target_pairs={{1,17},{3,19},{5,21},{7,23},{9,25},{11,27},{13,29},{15,31},{16,0},... | collective-permute-start | bytes 393224 | tf_op jit(solution)/shard_map/ppermute | solution.py:25
  166.0 11.0 %all-to-all-start.3 = ((bf16[16,16,256]{2,1,0:T(8,128)(2,1)}), bf16[16,16,256]{2,1,0:T(8,128)(2,1)S(1)}, u32[]{:S(2)}, u32[]{:S(2)}) async-start(bf16[16,16,256]{2,1,0:T(8,128)(2,1)} %fusion.59), calls=%async_computation.3 | async-start | bytes 262144 | tf_op jit(solution)/shard_map/all_to_all | solution.py:57
  179.0 56.6 %all-to-all-start.4 = ((bf16[8,16,4096]{2,1,0:T(8,128)(2,1)}), bf16[8,16,4096]{2,1,0:T(8,128)(2,1)}, u32[]{:S(2)}, u32[]{:S(2)}) async-start(bf16[8,16,4096]{2,1,0:T(8,128)(2,1)} %broadcast_in_dim.46), calls=%async_computation.4 | async-start | bytes 2097152 | tf_op jit(solution)/shard_map/all_to_all | solution.py:53
  184.7 7.2 %copy-start.12 = (bf16[8,2,16,512]{3,2,1,0:T(8,128)(2,1)S(1)}, bf16[8,2,16,512]{3,2,1,0:T(8,128)(2,1)}, u32[]{:S(2)}) copy-start(bf16[8,2,16,512]{3,2,1,0:T(8,128)(2,1)} %copy.97) | copy-start | bytes 786436
  184.7 104.2 %all-gather.5.cloned.1.call-start = ((), (), s32[]{:S(2)}) async-start(), calls=%async_computation.8 | async-start | bytes 1179648 | tf_op jit(solution)/shard_map/all_gather | solution.py:66
  184.7 7.2 %copy-start.6 = (f32[1024,256]{1,0:T(8,128)S(1)}, f32[1024,256]{1,0:T(8,128)}, u32[]{:S(2)}) copy-start(f32[1024,256]{1,0:T(8,128)} %fusion.39) | copy-start | bytes 3145732
  188.6 12.9 %copy-start.26 = (bf16[16,2048]{1,0:T(8,128)(2,1)S(1)}, bf16[16,2048]{1,0:T(8,128)(2,1)}, u32[]{:S(2)}) copy-start(bf16[16,2048]{1,0:T(8,128)(2,1)} %get-tuple-element.28) | copy-start | bytes 196612
  189.5 12.0 %collective-permute-start.10 = (bf16[32,2048]{1,0:T(8,128)(2,1)S(1)}, bf16[32,2048]{1,0:T(8,128)(2,1)S(1)}, u32[]{:S(2)}, u32[]{:S(2)}) collective-permute-start(bf16[32,2048]{1,0:T(8,128)(2,1)S(1)} %pad_maximum_fusion.22), channel_id=1, source_target_pairs={{0,240},{16,224},{32,208},{48,192},{64,176},{80,160},{96,144},{112... | collective-permute-start | bytes 393224 | tf_op jit(solution)/shard_map/ppermute | solution.py:37
  251.8 52.4 %all-to-all-start.5 = ((bf16[8,16,4096]{2,1,0:T(8,128)(2,1)}), bf16[8,16,4096]{2,1,0:T(8,128)(2,1)}, u32[]{:S(2)}, u32[]{:S(2)}) async-start(bf16[8,16,4096]{2,1,0:T(8,128)(2,1)} %bitcast.259), calls=%async_computation.5 | async-start | bytes 2097152 | tf_op jit(solution)/shard_map/all_to_all | solution.py:53
  257.5 15.2 %copy-start.3 = (bf16[128,2048]{1,0:T(8,128)(2,1)S(1)}, bf16[128,2048]{1,0:T(8,128)(2,1)}, u32[]{:S(2)}) copy-start(bf16[128,2048]{1,0:T(8,128)(2,1)} %all_gather.15) | copy-start | bytes 1572868
  257.5 15.2 %copy-start.25 = (bf16[128,256]{0,1:T(8,128)(2,1)S(1)}, bf16[128,256]{0,1:T(8,128)(2,1)}, u32[]{:S(2)}) copy-start(bf16[128,256]{0,1:T(8,128)(2,1)} %get-tuple-element.22) | copy-start | bytes 196612
  257.5 8.1 %collective-permute-start.11 = (bf16[128,256]{0,1:T(8,128)(2,1)S(1)}, bf16[128,256]{0,1:T(8,128)(2,1)S(1)}, u32[]{:S(2)}, u32[]{:S(2)}) collective-permute-start(bf16[128,256]{0,1:T(8,128)(2,1)S(1)} %pad_maximum_fusion.25), channel_id=1, source_target_pairs={{0,2},{1,3},{2,0},{3,1},{4,6},{5,7},{6,4},{7,5},{8,10},{9,11},{10,... | collective-permute-start | bytes 196616 | tf_op jit(solution)/shard_map/ppermute | solution.py:33
  260.8 35.0 %collective-permute-start.22 = (bf16[256,2048]{1,0:T(8,128)(2,1)}, bf16[256,2048]{1,0:T(8,128)(2,1)}, u32[]{:S(2)}, u32[]{:S(2)}) collective-permute-start(bf16[256,2048]{1,0:T(8,128)(2,1)} %pad_maximum_fusion.11), channel_id=1, source_target_pairs={{0,1},{1,0},{2,3},{3,2},{4,5},{5,4},{6,7},{7,6},{8,9},{9,8},{10,11... | collective-permute-start | bytes 3145736 | tf_op jit(solution)/shard_map/ppermute | solution.py:29
  266.3 14.1 %collective-permute-start.15 = (bf16[128,512]{0,1:T(8,128)(2,1)}, bf16[128,512]{0,1:T(8,128)(2,1)S(1)}, u32[]{:S(2)}, u32[]{:S(2)}) collective-permute-start(bf16[128,512]{0,1:T(8,128)(2,1)} %get-tuple-element.34), channel_id=1, source_target_pairs={{0,241},{1,240},{2,243},{3,242},{4,245},{5,244},{6,247},{7,246},{8... | collective-permute-start | bytes 393224 | tf_op jit(solution)/shard_map/ppermute | solution.py:25
  266.3 22.6 %collective-permute-start.14 = (bf16[128,512]{0,1:T(8,128)(2,1)}, bf16[128,512]{0,1:T(8,128)(2,1)}, u32[]{:S(2)}, u32[]{:S(2)}) collective-permute-start(bf16[128,512]{0,1:T(8,128)(2,1)} %get-tuple-element.34), channel_id=1, source_target_pairs={{0,1},{1,0},{2,3},{3,2},{4,5},{5,4},{6,7},{7,6},{8,9},{9,8},{10,11... | collective-permute-start | bytes 393224 | tf_op jit(solution)/shard_map/ppermute | solution.py:29
  269.4 9.9 %collective-permute-start.12 = (bf16[128,512]{0,1:T(8,128)(2,1)S(1)}, bf16[128,512]{0,1:T(8,128)(2,1)}, u32[]{:S(2)}, u32[]{:S(2)}) collective-permute-start(bf16[128,512]{0,1:T(8,128)(2,1)S(1)} %get-tuple-element.35), channel_id=1, source_target_pairs={{0,240},{16,224},{32,208},{48,192},{64,176},{80,160},{96,144},{112... | collective-permute-start | bytes 393224 | tf_op jit(solution)/shard_map/ppermute | solution.py:37
  279.3 16.5 %collective-permute-start.23 = (bf16[128,256]{0,1:T(8,128)(2,1)}, bf16[128,256]{0,1:T(8,128)(2,1)}, u32[]{:S(2)}, u32[]{:S(2)}) collective-permute-start(bf16[128,256]{0,1:T(8,128)(2,1)} %get-tuple-element.23), channel_id=1, source_target_pairs={{0,1},{1,0},{2,3},{3,2},{4,5},{5,4},{6,7},{7,6},{8,9},{9,8},{10,11... | collective-permute-start | bytes 196616 | tf_op jit(solution)/shard_map/ppermute | solution.py:29
  281.0 16.7 %collective-permute-start.17 = (bf16[128,256]{0,1:T(8,128)(2,1)}, bf16[128,256]{0,1:T(8,128)(2,1)}, u32[]{:S(2)}, u32[]{:S(2)}) collective-permute-start(bf16[128,256]{0,1:T(8,128)(2,1)} %get-tuple-element.18), channel_id=1, source_target_pairs={{0,240},{16,224},{32,208},{48,192},{64,176},{80,160},{96,144},{112... | collective-permute-start | bytes 196616 | tf_op jit(solution)/shard_map/ppermute | solution.py:37
  288.9 11.9 %collective-permute-start.13 = (bf16[256,2048]{1,0:T(8,128)(2,1)}, bf16[256,2048]{1,0:T(8,128)(2,1)}, u32[]{:S(2)}, u32[]{:S(2)}) collective-permute-start(bf16[256,2048]{1,0:T(8,128)(2,1)} %all-gather.5.cloned.1.call-done), channel_id=1, source_target_pairs={{0,1},{1,0},{2,3},{3,2},{4,5},{5,4},{6,7},{7,6},{8,9},{9,8},{10,11... | collective-permute-start | bytes 3145736 | tf_op jit(solution)/shard_map/ppermute | solution.py:29
  302.9 17.7 %collective-permute-start.16 = (bf16[512,256]{1,0:T(8,128)(2,1)}, bf16[512,256]{1,0:T(8,128)(2,1)}, u32[]{:S(2)}, u32[]{:S(2)}) collective-permute-start(bf16[512,256]{1,0:T(8,128)(2,1)} %constant_dynamic-slice_fusion.2), channel_id=1, source_target_pairs={{0,240},{1,241},{4,244},{5,245},{8,248},{9,249},{12,252},{13,253},... | collective-permute-start | bytes 786440 | tf_op jit(solution)/shard_map/ppermute | solution.py:25
  307.5 14.9 %all-to-all-start.6 = ((bf16[16,16,256]{2,1,0:T(8,128)(2,1)}), bf16[16,16,256]{2,1,0:T(8,128)(2,1)S(1)}, u32[]{:S(2)}, u32[]{:S(2)}) async-start(bf16[16,16,256]{2,1,0:T(8,128)(2,1)} %bitcast.242), calls=%async_computation.6 | async-start | bytes 262144 | tf_op jit(solution)/shard_map/all_to_all | solution.py:57
  (20 other events, 58.3 us)
Sparse Core Ops, SparseCore 0:
  55.1 43.2 all-gather.2
  202.4 42.5 all-gather.4

commit v2 on v1

v2 whole, which is shorter than its diff:
```python
import functools

import jax
import jax.numpy as jnp
from jax import lax
from jax.experimental import pallas as pl
from jax.experimental.pallas import tpu as pltpu
from jax.sharding import PartitionSpec as P

HD = 128
TICKS = 2
TOK = 128
WIDTH = 4096
HALF = WIDTH // 2
SCALE = HD ** (-0.5)
BF = jnp.bfloat16
F32 = jnp.float32

SAME_CORE = [[core + 2 * chip for chip in range(8)] for core in range(2)]
VMEM = pl.BlockSpec(memory_space=pltpu.VMEM)
HBM = pl.BlockSpec(memory_space=pl.ANY)


def send(x, route):
    pairs = []
    for section in range(16):
        for tensor in range(16):
            target = route(section, tensor)
            if target is not None:
                pairs.append((section * 16 + tensor, target[0] * 16 + target[1]))
    return lax.ppermute(x, ("section", "tensor"), pairs)


def swap_core(x):
    return lax.ppermute(x, "tensor", [(i, i ^ 1) for i in range(16)])


def swap_z(x):
    return lax.ppermute(x, "tensor", [(i, i ^ 2) for i in range(16)])


def swap_y(x, k):
    return lax.ppermute(x, "tensor", [(i, i ^ 4 * k) for i in range(16)])


def mirror(x):
    return lax.ppermute(x, "section", [(i, 15 - i) for i in range(16)])


def next_section(x):
    def route(s, c):
        target = s - 1 if c % 2 == 0 else s + 1
        return (target, c) if 0 <= target < 16 else None

    return send(x, route)


def next_mirror(x):
    def route(s, c):
        target = s - 1 if c % 2 == 0 else s + 1
        return (15 - target, c) if 0 <= target < 16 else None

    return send(x, route)


def exchange8(x):
    return lax.all_to_all(x, "tensor", 0, 0, axis_index_groups=SAME_CORE, tiled=True)


def exchange16(x):
    return lax.all_to_all(x, "tensor", 0, 0, tiled=True)


def gather16(x):
    return lax.all_gather(x, "tensor", axis=0, tiled=True)


def dot(a, b):
    return jnp.dot(a, b, preferred_element_type=F32)


def dot_nt(a, b):
    return lax.dot_general(a, b, (((1,), (1,)), ((), ())), preferred_element_type=F32)


def dot_tn(a, b):
    return lax.dot_general(a, b, (((0,), (0,)), ((), ())), preferred_element_type=F32)


def together(*values):
    return lax.optimization_barrier(values)


def params(mib):
    return pltpu.CompilerParams(vmem_limit_bytes=mib * 2**20)


def attend_kernel(q_ref, kv_ref, attention_ref, attended_ref):
    rows = lax.broadcasted_iota(jnp.int32, (TOK, TOK), 0)
    columns = lax.broadcasted_iota(jnp.int32, (TOK, TOK), 1)
    causal = rows >= columns
    for t in range(TICKS):
        keys = kv_ref[t, :, :HD]
        values = kv_ref[t, :, HD:]
        for a in range(4):
            head = slice(a * HD, (a + 1) * HD)
            scores = jnp.where(causal, dot_nt(q_ref[t, :, head], keys) * SCALE, -1e30)
            weights = jnp.exp(scores - jnp.max(scores, axis=-1, keepdims=True))
            weights = weights / jnp.sum(weights, axis=-1, keepdims=True)
            attention_ref[t, a] = weights
            attended_ref[t, :, head] = dot(weights.astype(BF), values).astype(BF)


def attend(queries, pairs):
    return pl.pallas_call(
        attend_kernel,
        out_shape=(
            jax.ShapeDtypeStruct((TICKS, 4, TOK, TOK), F32),
            jax.ShapeDtypeStruct((TICKS, TOK, 4 * HD), BF),
        ),
        in_specs=[VMEM] * 2,
        out_specs=(VMEM, VMEM),
        compiler_params=params(16),
    )(queries, pairs)


CHUNKS = 4
DEEP = WIDTH // CHUNKS


def back_kernel(
    tick,
    g_hbm, wo_own_ref, wo_far_ref, wq_own_ref, wq_far_ref, wkv_ref, q_ref, kv_ref, attention_ref,
    terms_ref, parts_ref,
    g_ref, grad_heads, heads, g_sems,
):
    own_ref, far_ref, pairs_ref = (parts_ref.at[pl.ds(n * TOK, TOK)] for n in range(3))
    copies = []
    for c in range(CHUNKS):
        if tick == 0:
            part = pl.ds(c * 16 // CHUNKS, 16 // CHUNKS)
            copies.append(pltpu.make_async_copy(g_hbm.at[part, :TOK], g_ref.at[part], g_sems.at[c]))
        else:
            deep = pl.ds(c * DEEP, DEEP)
            copies.append(pltpu.make_async_copy(g_hbm.at[:, :, deep], g_ref.at[:, :, deep], g_sems.at[c]))
    for copy in copies:
        copy.start()
    for a in range(4):
        heads[a * TOK:(a + 1) * TOK] = q_ref[tick, :, a * HD:(a + 1) * HD]
    own = jnp.zeros((TOK, 256), F32)
    far = jnp.zeros((TOK, 256), F32)
    for c in range(CHUNKS):
        copies[c].wait()
        if tick == 0:
            for block in range(c * 16 // CHUNKS, (c + 1) * 16 // CHUNKS):
                deep = pl.ds(block * 256, 256)
                own += dot(g_ref[block], wo_own_ref[deep])
                far += dot(g_ref[block], wo_far_ref[deep])
        else:
            deep = pl.ds(c * DEEP, DEEP)
            part = g_ref[:, :, deep].reshape(TOK, DEEP)
            own += dot(part, wo_own_ref[deep])
            far += dot(part, wo_far_ref[deep])
    keys = kv_ref[tick, :, :HD]
    values = kv_ref[tick, :, HD:]
    for a in range(4):
        side = own if a < 2 else far
        grad_heads[a * TOK:(a + 1) * TOK] = side[:, a % 2 * HD:(a % 2 + 1) * HD].astype(BF)
    grad_probs = dot_nt(grad_heads[...], values)
    attention = attention_ref[tick].reshape(4 * TOK, TOK)
    row_delta = jnp.sum(attention * grad_probs, axis=-1, keepdims=True)
    grad_scores = (attention * (grad_probs - row_delta) * SCALE).astype(BF)
    query_grad = dot(grad_scores, keys).astype(BF)
    for a in range(4):
        target = own_ref if a < 2 else far_ref
        target[:, a % 2 * HD:(a % 2 + 1) * HD] = query_grad[a * TOK:(a + 1) * TOK]
    pairs_ref[:, :HD] = dot_tn(grad_scores, heads[...]).astype(BF)
    pairs_ref[:, HD:] = dot_tn(attention.astype(BF), grad_heads[...]).astype(BF)
    for n in range(8):
        wide = pl.ds(n * 512, 512)
        out = dot_nt(own_ref[...], wq_own_ref[wide]) + dot_nt(far_ref[...], wq_far_ref[wide])
        out = out + dot_nt(pairs_ref[...], wkv_ref[wide])
        terms_ref[:, wide] = out.astype(BF)


def back(tick, grads, wo_own, wo_far, wq_own, wq_far, w_kv, queries, pairs, attention):
    return pl.pallas_call(
        functools.partial(back_kernel, tick),
        out_shape=(
            jax.ShapeDtypeStruct((TOK, WIDTH), BF),
            jax.ShapeDtypeStruct((3 * TOK, 256), BF),
        ),
        in_specs=[HBM] + [VMEM] * 8,
        out_specs=(VMEM, VMEM),
        scratch_shapes=[
            pltpu.VMEM((16, TOK, 256) if tick == 0 else (8, 16, WIDTH), BF),
            pltpu.VMEM((4 * TOK, HD), BF),
            pltpu.VMEM((4 * TOK, HD), BF),
            pltpu.SemaphoreType.DMA((CHUNKS,)),
        ],
        compiler_params=params(24),
    )(grads, wo_own, wo_far, wq_own, wq_far, w_kv, queries, pairs, attention)


def finish_kernel(first, tick, chip_ref, terms_ref, rows_ref, grad_ref, out_ref, blocks_ref, kept):
    x_at = TOK + 16 * tick
    here = pl.ds(pl.multiple_of(chip_ref[0] * 16, 16), 16)
    squares = jnp.zeros((16, 256), F32)
    products = jnp.zeros((16, 256), F32)
    for j in range(16):
        wide = pl.ds(j * 256, 256)
        x = rows_ref[j, x_at:x_at + 16].astype(F32)
        total = terms_ref[0, :, wide].astype(F32)
        for m in range(1, 8):
            total += terms_ref[m, :, wide].astype(F32)
        kept[:, wide] = total
        squares += x * x
        products += total * x
    inverse = lax.rsqrt(jnp.sum(squares, axis=-1, keepdims=True) / WIDTH + 1e-06)
    shift = jnp.sum(products, axis=-1, keepdims=True) * inverse * inverse / WIDTH
    for j in range(16):
        wide = pl.ds(j * 256, 256)
        x = rows_ref[j, x_at:x_at + 16].astype(F32)
        before = rows_ref[j, here] if first else grad_ref[:, wide]
        out = before.astype(F32) + inverse * (kept[:, wide] - x * shift)
        out = out.astype(BF)
        out_ref[:, wide] = out
        blocks_ref[j] = out


def finish(tick, chip, terms, rows, grad_rows):
    first = tick == 0
    operands = (chip.reshape(1), terms, rows) + (() if first else (grad_rows,))

    def kernel(*refs):
        if first:
            finish_kernel(first, tick, *refs[:3], None, *refs[3:])
        else:
            finish_kernel(first, tick, *refs)

    return pl.pallas_call(
        kernel,
        out_shape=(
            jax.ShapeDtypeStruct((16, WIDTH), BF),
            jax.ShapeDtypeStruct((16, 16, 256), BF),
        ),
        in_specs=[pl.BlockSpec(memory_space=pltpu.SMEM)] + [VMEM] * (len(operands) - 1),
        out_specs=(VMEM, VMEM),
        scratch_shapes=[pltpu.VMEM((16, WIDTH), F32)],
        compiler_params=params(16),
    )(*operands)


def rows_kernel(half_ref, chip_ref, rows_ref, sent_ref, held_ref):
    rows = 32
    squares = jnp.zeros((rows, 256), F32)
    for j in range(16):
        x = rows_ref[j, TOK:].astype(F32)
        squares += x * x
    inverse = lax.rsqrt(jnp.sum(squares, axis=-1, keepdims=True) / WIDTH + 1e-06)
    half = half_ref[0]
    here = pl.ds(pl.multiple_of(chip_ref[0] * 16, 16), 16)
    for j in range(8):
        wide = pl.ds(j * 256, 256)
        near, far = half * 8 + j, (1 - half) * 8 + j
        held_ref[:rows, wide] = (rows_ref[near, TOK:].astype(F32) * inverse).astype(BF)
        sent_ref[:rows, wide] = (rows_ref[far, TOK:].astype(F32) * inverse).astype(BF)
        sent_ref[rows:, wide] = rows_ref[far, here]
        held_ref[rows:, wide] = rows_ref[near, here]


def split_rows(half, chip, rows):
    return pl.pallas_call(
        rows_kernel,
        out_shape=(
            jax.ShapeDtypeStruct((48, HALF), BF),
            jax.ShapeDtypeStruct((48, HALF), BF),
        ),
        in_specs=[pl.BlockSpec(memory_space=pltpu.SMEM)] * 2 + [VMEM],
        out_specs=(VMEM, VMEM),
        compiler_params=params(16),
    )(half.reshape(1), chip.reshape(1), rows)


def fill_right(core_ref, right_ref, near, far):
    core = core_ref[0]
    for side, sources in enumerate((near, far)):
        direction = core if side == 0 else 1 - core
        for m in range(8):
            for group, source in enumerate(sources):
                at = (2 * m + direction) * 16 * len(sources) + group * 16
                value = source(m * 16)
                right_ref[pl.ds(pl.multiple_of(at, 16), 16)] = value


def columns_kernel(
    core_ref, x_hbm, after_hbm,
    near_0, near_1, near_m0, near_m1, far_0, far_1, far_m0, far_m1,
    query_ref, pairs_ref, x_ref, right_ref, sems,
):
    copies = [
        pltpu.make_async_copy(x_hbm.at[:, :32], x_ref.at[:, :32], sems.at[0]),
        pltpu.make_async_copy(x_hbm.at[:, 48:80], x_ref.at[:, 32:], sems.at[1]),
    ]
    for copy in copies:
        copy.start()

    def both_columns(ref):
        return lambda at: jnp.concatenate([ref[at:at + 16], ref[TOK + at:TOK + at + 16]], -1)

    near = [both_columns(ref) for ref in (near_0, near_1, near_m0, near_m1)]
    far = [both_columns(ref) for ref in (far_0, far_1, far_m0, far_m1)]
    fill_right(core_ref, right_ref, near, far)
    for copy in copies:
        copy.wait()
    core = core_ref[0]
    for n in range(4):
        wide = pl.ds(pl.multiple_of(core * 1024 + n * 256, 256), 256)
        both = dot_tn(x_ref[:, :, wide].reshape(1024, 256), right_ref[...])
        query_ref[wide] = both[:, :256].astype(BF)
        pairs_ref[n * 256:(n + 1) * 256] = both[:, 256:].astype(BF)
    for n in range(4):
        wide = pl.ds(pl.multiple_of((1 - core) * 1024 + n * 256, 256), 256)
        query_ref[wide] = dot_tn(x_ref[:, :, wide].reshape(1024, 256), right_ref[:, :256]).astype(BF)


def columns(core, x, after, rights):
    return pl.pallas_call(
        columns_kernel,
        out_shape=(
            jax.ShapeDtypeStruct((HALF, 256), BF),
            jax.ShapeDtypeStruct((1024, 256), BF),
        ),
        in_specs=[pl.BlockSpec(memory_space=pltpu.SMEM)] + [HBM] * 2 + [VMEM] * 8,
        out_specs=(VMEM, VMEM),
        scratch_shapes=[
            pltpu.VMEM((16, 64, HALF), BF),
            pltpu.VMEM((1024, 512), BF),
            pltpu.SemaphoreType.DMA((2,)),
        ],
        cost_estimate=pl.CostEstimate(flops=1000, bytes_accessed=1000, transcendentals=0),
        compiler_params=params(58),
    )(core.reshape(1), x, after, *rights)


def output_kernel(
    core_ref, x_hbm, near_hbm, far_hbm,
    near_0, near_m0, near_1, near_m1, far_0, far_m0, far_1, far_m1,
    out_ref, g_ref, right_ref, second_ref, second_right, sems,
):
    copies = [
        pltpu.make_async_copy(x_hbm.at[:, 32:48], g_ref.at[:, :16], sems.at[0]),
        pltpu.make_async_copy(x_hbm.at[:, 80:], g_ref.at[:, 16:], sems.at[1]),
        pltpu.make_async_copy(near_hbm, second_ref.at[:2 * TOK], sems.at[2]),
        pltpu.make_async_copy(far_hbm, second_ref.at[2 * TOK:], sems.at[3]),
    ]
    for copy in copies:
        copy.start()

    def rows(ref):
        return lambda at: ref[at:at + 16]

    fill_right(core_ref, right_ref, [rows(near_0), rows(near_m0)], [rows(far_0), rows(far_m0)])
    for n, ref in enumerate((near_1, near_m1, far_1, far_m1)):
        second_right[n * TOK:(n + 1) * TOK] = ref[...]
    for copy in copies:
        copy.wait()
    for j in range(8):
        wide = pl.ds(j * 256, 256)
        out = dot_tn(g_ref[:, :, wide].reshape(512, 256), right_ref[...])
        out += dot_tn(second_ref[:, wide], second_right[...])
        out_ref[wide] = out.astype(BF)


def output_columns(core, x, near, far, attended):
    return pl.pallas_call(
        output_kernel,
        out_shape=jax.ShapeDtypeStruct((HALF, 256), BF),
        in_specs=[pl.BlockSpec(memory_space=pltpu.SMEM)] + [HBM] * 3 + [VMEM] * 8,
        out_specs=VMEM,
        scratch_shapes=[
            pltpu.VMEM((16, 32, HALF), BF),
            pltpu.VMEM((512, 256), BF),
            pltpu.VMEM((512, HALF), BF),
            pltpu.VMEM((512, 256), BF),
            pltpu.SemaphoreType.DMA((4,)),
        ],
        cost_estimate=pl.CostEstimate(flops=1000, bytes_accessed=1000, transcendentals=0),
        compiler_params=params(58),
    )(core.reshape(1), x, near, far, *attended)


def on_device(weight_q, weight_kv, weight_o, section_inputs, saved_q, saved_kv, out_grads):
    position = lax.axis_index("section")
    column = lax.axis_index("tensor")
    core = column % 2
    z_low = column // 2 % 2
    half = (position >= 8).astype(jnp.int32)
    next_half = (position + 2 * core - 1 >= 8).astype(jnp.int32)
    w_q, w_kv, w_o = weight_q[0], weight_kv[0], weight_o[0]
    inputs = section_inputs[:, :, 0]
    grads = out_grads[:, 0]

    def pick(x, index):
        return lax.dynamic_index_in_dim(x, index, 0, keepdims=False)

    def features_of(x, which):
        return lax.dynamic_slice_in_dim(x, which * HALF, HALF, x.ndim - 1)

    by_chip = (8, 2, TOK, 256)
    tokens = inputs.reshape(2, TICKS, 8, 16, 256).transpose(2, 0, 1, 3, 4).reshape(8, 2, 32, 256)
    mixed = jnp.concatenate([jnp.broadcast_to(grads[None], by_chip), tokens], 2)
    rows = exchange16(mixed.reshape(16, TOK + 32, 256))

    wo_far = swap_core(w_o)
    queries = saved_q[:, :, 0]
    queries = jnp.concatenate([pick(queries, core), swap_core(pick(queries, 1 - core))], -1)
    wq_far = swap_core(w_q)
    pairs = pick(saved_kv[:, :, 0], core)
    attention, attended = attend(queries, pairs)
    chip = (column // 2).astype(jnp.int32)
    sent, held = split_rows(half, chip, rows)
    att_m = mirror(attended)
    near_o, near_q, near_kv = swap_core(wo_far), swap_core(wq_far), swap_core(w_kv)
    rows, sent, held, wo_far, wq_far, near_o, near_q, near_kv, attention = together(
        rows, sent, held, wo_far, wq_far, near_o, near_q, near_kv, attention
    )

    def both_chips(p):
        return (p.astype(F32) + swap_z(p).astype(F32)).astype(BF)

    def block(x, at):
        return x[at * TOK:(at + 1) * TOK]

    def held_near(x):
        return pltpu.with_memory_space_constraint(x, pltpu.VMEM)

    w_o, wo_far, w_q, wq_far, w_kv = map(held_near, (near_o, wo_far, near_q, wq_far, near_kv))

    terms, parts_0 = back(
        0, rows, w_o, wo_far, w_q, wq_far, w_kv, queries, pairs, attention
    )
    parts_0, sent = together(parts_0, sent)
    terms, att_m = together(terms, att_m)
    terms_0 = exchange8(terms.reshape(8, 16, WIDTH))
    got = mirror(sent)
    x_rows = jnp.concatenate([held, got], 0)
    terms_0, x_rows = together(terms_0, x_rows)

    grad_in_0, blocks_0 = finish(0, chip, terms_0, rows, None)
    grad_rows = next_section(grad_in_0)
    sum_0 = both_chips(block(parts_0, 2))
    grad_half = next_mirror(
        lax.dynamic_slice_in_dim(grad_in_0, (1 - next_half) * HALF, HALF, 1)
    )

    spread_1 = jnp.concatenate([grad_rows, grad_half], 1)
    spread_1 = jnp.broadcast_to(spread_1[None], (8,) + spread_1.shape)
    spread_1, parts_0, sum_0, x_rows = together(spread_1, parts_0, sum_0, x_rows)
    full_1 = exchange8(spread_1)
    x_all = gather16(x_rows)
    terms, parts_1 = back(
        1, full_1, w_o, wo_far, w_q, wq_far, w_kv, queries, pairs, attention
    )
    sum_1 = both_chips(block(parts_1, 2))
    terms, sum_1 = together(terms, sum_1)
    terms_1 = exchange8(terms.reshape(8, 16, WIDTH))
    here = jnp.stack(
        [jnp.concatenate([parts_0[:2 * TOK], sum_0], 0), jnp.concatenate([parts_1[:2 * TOK], sum_1], 0)]
    )
    late_m = mirror(here)

    att_far = swap_core(jnp.stack([attended[..., 256:], att_m[..., 256:]]))
    g_near = jnp.concatenate(
        [lax.dynamic_slice_in_dim(full_1, half * HALF, HALF, 2), full_1[:, :, WIDTH:]], 0
    ).reshape(256, HALF)
    g_far = swap_core(g_near)
    terms_1, x_all, g_far = together(terms_1, x_all, g_far)

    after, blocks_1 = finish(1, chip, terms_1, rows, grad_rows)
    out = exchange16(jnp.concatenate([blocks_0, blocks_1], 1))
    after, x_all, late_m = together(after, x_all, late_m)
    both = jnp.stack([here, late_m])
    near = jnp.concatenate([both[:, :, :TOK], both[:, :, 2 * TOK:]], 2)
    far = swap_core(both[:, :, TOK:])
    x_all = x_all.reshape(16, 96, HALF)
    grad_query, acc_kv = columns(
        core, x_all, after,
        [near[0, 0], near[0, 1], near[1, 0], near[1, 1], far[0, 0], far[0, 1], far[1, 0], far[1, 1]],
    )
    att, att_got = attended[..., :256], att_m[..., :256]
    grad_output = output_columns(
        core, x_all, g_near, g_far,
        [att[0], att_got[0], att[1], att_got[1],
         att_far[0, 0], att_far[1, 0], att_far[0, 1], att_far[1, 1]],
    )
    kept = lax.dynamic_slice_in_dim(acc_kv, half * 512, 512, 0)
    given = lax.dynamic_slice_in_dim(acc_kv, (1 - half) * 512, 512, 0)
    taken = send(given, lambda s, c: (15 - s, c) if c // 2 % 2 == s // 8 else None)
    grad_kv = jnp.where(z_low == half, kept, taken)

    input_grads = out.reshape(8, 2, TICKS, 16, 256).transpose(1, 2, 0, 3, 4)
    input_grads = input_grads.reshape(2, TICKS, 1, TOK, 256)
    return (input_grads, grad_query[None], grad_kv[None], grad_output[None])


def solution(mesh):
    placed = (
        P("section", None, "tensor"),
        P("section", None, "tensor"),
        P("section", None, "tensor"),
        P(None, None, "section", None, "tensor"),
        P(None, None, "section", None, "tensor"),
        P(None, None, "section", None, "tensor"),
        P(None, "section", None, "tensor"),
    )
    return jax.shard_map(
        on_device,
        mesh=mesh,
        in_specs=placed,
        out_specs=(
            P(None, None, "section", None, "tensor"),
            P("section", None, "tensor"),
            P("section", None, "tensor"),
            P("section", None, "tensor"),
        ),
        check_vma=False,
    )
```

time: 335 us -> 213 us (0.64); the launches traced: 330 us -> 212 us
  matrix products: 64.7 us -> 0 us
  starting transfers between devices: 87.7 us -> 52.6 us
  blocking collectives: 64.1 us -> 29.6 us
  Pallas kernels: 0 us -> 31.5 us
  local copies, waits for them, and re-layouts: 32.5 us -> 13.4 us
  waiting for transfers between devices: 44.9 us -> 60.4 us
  other arithmetic: 21.4 us -> 9.61 us
    dot_general x27 -> x0, matrix products: 64.3 us -> none  [the longest x12 31 us: dot_tn(): lax.dot_general(a, b, (((0,), (0,)), ((), ())), preferred_element_type=F32)]
    all_gather x2 -> x0, blocking collectives: 64.1 us -> none  [gather8(): lax.all_gather(x, 'tensor', axis_index_groups=SAME_CORE, axis=0, tiled=True)]
    pallas_call x0 -> x8, Pallas kernels: none -> 31.5 us  [the longest x2 14.7 us: back(): pl.pallas_call(functools.partial(back_kernel, tick), out_shape=(jax.Shape...]
    all_to_all x0 -> x1, blocking collectives: none -> 29.6 us  [exchange8(): lax.all_to_all(x, 'tensor', 0, 0, axis_index_groups=SAME_CORE, tiled=True)]
    ppermute x6 -> x3, starting transfers between devices: 20.4 us -> 7.02 us  [send(): return lax.ppermute(x, ('section', 'tensor'), pairs)]
    ppermute x6 -> x3, waiting for transfers between devices: 0.02 us -> 13.1 us  [send(): return lax.ppermute(x, ('section', 'tensor'), pairs)]
    all_to_all x4 -> x2, waiting for transfers between devices: 0.01 us -> 12.3 us  [exchange8(): lax.all_to_all(x, 'tensor', 0, 0, axis_index_groups=SAME_CORE, tiled=True)]
    ppermute x6 -> x3, waiting for transfers between devices: 29.6 us -> 19.4 us  [mirror(): return lax.ppermute(x, 'section', [(i, 15 - i) for i in range(16)])]
  transfers between devices with their start and end apart: 34 -> 22, of which waited for: 9 -> 9; matrix products, arithmetic and copies ran while one was open for 34% -> 7% of each run, Pallas kernels for 0% -> 15%
where the time goes in v2:
time: 213 us; the launch traced here: 212 us
  waiting for transfers between devices  60.4 us (28%)
  starting transfers between devices  52.6 us (25%)
  Pallas kernels  31.5 us (15%)
  blocking collectives  29.6 us (14%)
  between operations  14.5 us (7%)
  local copies, waits for them, and re-layouts  13.4 us (6%)
  other arithmetic  9.61 us (5%)
    all_to_all x1, blocking collectives, exchange8(): lax.all_to_all(x, 'tensor', 0, 0, axis_index_groups=SAME_CORE, tiled=True)  29.6 us
    ppermute x3, waiting for transfers between devices, mirror(): return lax.ppermute(x, 'section', [(i, 15 - i) for i in range(16)])  19.4 us
    all_to_all x2, starting transfers between devices, exchange16(): return lax.all_to_all(x, 'tensor', 0, 0, tiled=True)  15.9 us
    pallas_call x2, Pallas kernels, back(): pl.pallas_call(functools.partial(back_kernel, tick), out_shape=(jax.Shape...  14.7 us
    all_to_all x2, starting transfers between devices, exchange8(): lax.all_to_all(x, 'tensor', 0, 0, axis_index_groups=SAME_CORE, tiled=True)  13.9 us
    ppermute x3, waiting for transfers between devices, send(): return lax.ppermute(x, ('section', 'tensor'), pairs)  13.1 us
    all_to_all x2, waiting for transfers between devices, exchange8(): lax.all_to_all(x, 'tensor', 0, 0, axis_index_groups=SAME_CORE, tiled=True)  12.3 us
    ppermute x3, starting transfers between devices, mirror(): return lax.ppermute(x, 'section', [(i, 15 - i) for i in range(16)])  8.97 us
  transfers between devices with their start and end apart: 22, of which 9 were waited for; matrix products, arithmetic and copies ran while one was open for 7% of the time, Pallas kernels for 15%

profile of v2, /device:TPU:96, one launch (start us, length us, event | category | flops | bytes accessed | tf_op | source)
XLA Modules:
  0.0 211.6 jit_solution(14642185601564652176)
XLA Ops:
  7.8 1.0 copy.11
  8.8 1.0 broadcast_in_dim.23
  9.8 1.2 pad_maximum_fusion
  11.0 5.9 %all-to-all-start = ((bf16[16,160,256]{2,1,0:T(8,128)(2,1)}), bf16[16,160,256]{2,1,0:T(8,128)(2,1)S(1)}, u32[]{:S(2)}, u32[]{:S(2)}) async-start(bf16[16,160,256]{2,1,0:T(8,128)(2,1)} %pad_maximum_fusion), calls=%async_computation | async-start | bytes 2621440 | tf_op jit(solution)/shard_map/all_to_all | solution.py:71
  18.1 3.4 %collective-permute-done.5 = bf16[2,128,256]{2,1,0:T(8,128)(2,1)S(1)} collective-permute-done((bf16[2,128,256]{2,1,0:T(8,128)(2,1)S(1)}, bf16[2,128,256]{2,1,0:T(8,128)(2,1)S(1)}, u32[]{:S(2)}, u32[]{:S(2)}) %collective-permute-start.5) | collective-permute-done | bytes 131104 | tf_op jit(solution)/shard_map/ppermute | solution.py:35
  21.5 2.7 %shard_map.103 = (f32[2,4,128,128]{3,2,1,0:T(8,128)S(1)}, bf16[2,128,512]{2,1,0:T(8,128)(2,1)S(1)}) custom-call(bf16[2,128,512]{2,1,0:T(8,128)(2,1)S(1)} %pad_maximum_fusion.5.q_ref, bf16[2,128,256]{2,1,0:T(8,128)(2,1)S(1)} %dynamic-slice_bitcast_fusion.kv_ref), custom_call_target="tpu_custom_call" | custom-call | tf_op jit(solution)/shard_map/pallas_call | solution.py:115
  24.2 5.9 %collective-permute-start.6 = (bf16[2,128,512]{2,1,0:T(8,128)(2,1)S(1)}, bf16[2,128,512]{2,1,0:T(8,128)(2,1)S(1)}, u32[]{:S(2)}, u32[]{:S(2)}) collective-permute-start(bf16[2,128,512]{2,1,0:T(8,128)(2,1)S(1)} %get-tuple-element.56), channel_id=1, source_target_pairs={{0,240},{16,224},{32,208},{48,192},{64,176},{80,160},{96,144},{112... | collective-permute-start | bytes 786440 | tf_op jit(solution)/shard_map/ppermute | solution.py:47
  30.0 8.0 %all-to-all-done.rows_ref.g_hbm.refs_2_ = bf16[16,160,256]{2,1,0:T(8,128)(2,1)S(1)} async-done(((bf16[16,160,256]{2,1,0:T(8,128)(2,1)}), bf16[16,160,256]{2,1,0:T(8,128)(2,1)S(1)}, u32[]{:S(2)}, u32[]{:S(2)}) %all-to-all-start) | async-done | bytes 1310752 | tf_op jit(solution)/shard_map/all_to_all | solution.py:71
  38.2 0.6 copy-done.16
  38.9 7.2 %shard_map.104 = (bf16[128,4096]{1,0:T(8,128)(2,1)S(1)}, bf16[384,256]{1,0:T(8,128)(2,1)S(1)}) custom-call(bf16[16,160,256]{2,1,0:T(8,128)(2,1)S(1)} %all-to-all-done.rows_ref.g_hbm.refs_2_, bf16[4096,256]{1,0:T(8,128)(2,1)} %collective-permute-done.2.wo_own_ref, bf16[4096,256]{1,0:T(8,128)(2,1)} %collective-permute-done.wo_far_ref, ...), custom_call_target="tpu_custom_call" | custom-call | tf_op jit(solution)/shard_map/pallas_call | solution.py:187
  46.2 1.0 copy-done.4
  47.1 0.7 copy-done.21
  47.9 7.4 %all-to-all-start.1 = ((bf16[8,16,4096]{2,1,0:T(8,128)(2,1)}), bf16[8,16,4096]{2,1,0:T(8,128)(2,1)S(1)}, u32[]{:S(2)}, u32[]{:S(2)}) async-start(bf16[8,16,4096]{2,1,0:T(8,128)(2,1)} %bitcast.74), calls=%async_computation.1 | async-start | bytes 2097152 | tf_op jit(solution)/shard_map/all_to_all | solution.py:67
  55.3 3.1 %collective-permute-start.7 = (bf16[48,2048]{1,0:T(8,128)(2,1)}, bf16[48,2048]{1,0:T(8,128)(2,1)}, u32[]{:S(2)}, u32[]{:S(2)}) collective-permute-start(bf16[48,2048]{1,0:T(8,128)(2,1)} %copy-done.16), channel_id=1, source_target_pairs={{0,240},{16,224},{32,208},{48,192},{64,176},{80,160},{96,144},{112... | collective-permute-start | bytes 589832 | tf_op jit(solution)/shard_map/ppermute | solution.py:47
  58.6 16.2 %collective-permute-done.7 = bf16[48,2048]{1,0:T(8,128)(2,1)} collective-permute-done((bf16[48,2048]{1,0:T(8,128)(2,1)}, bf16[48,2048]{1,0:T(8,128)(2,1)}, u32[]{:S(2)}, u32[]{:S(2)}) %collective-permute-start.7) | collective-permute-done | bytes 196640 | tf_op jit(solution)/shard_map/ppermute | solution.py:47
  74.8 1.7 pad_maximum_fusion.3
  76.8 1.9 collective-permute-start.8
  78.8 3.8 %collective-permute-start.9 = (bf16[16,2048]{1,0:T(8,128)(2,1)S(1)}, bf16[16,2048]{1,0:T(8,128)(2,1)S(1)}, u32[]{:S(2)}, u32[]{:S(2)}) collective-permute-start(bf16[16,2048]{1,0:T(8,128)(2,1)S(1)} %constant_dynamic-slice_fusion.2), channel_id=1, source_target_pairs={{1,225},{3,227},{5,229},{7,231},{9,233},{11,235},{13,237},{15,239}... | collective-permute-start | bytes 196616 | tf_op jit(solution)/shard_map/ppermute | solution.py:31
  83.3 7.7 %collective-permute-done.9 = bf16[16,2048]{1,0:T(8,128)(2,1)S(1)} collective-permute-done((bf16[16,2048]{1,0:T(8,128)(2,1)S(1)}, bf16[16,2048]{1,0:T(8,128)(2,1)S(1)}, u32[]{:S(2)}, u32[]{:S(2)}) %collective-permute-start.9) | collective-permute-done | bytes 65568 | tf_op jit(solution)/shard_map/ppermute | solution.py:31
  91.0 0.6 copy-done.5
  91.6 1.3 broadcast_in_dim.24
  93.0 29.6 %all_to_all.25.g_hbm = bf16[8,16,6144]{2,1,0:T(8,128)(2,1)S(1)} all-to-all(bf16[8,16,6144]{2,1,0:T(8,128)(2,1)} %broadcast_in_dim.24), channel_id=1, replica_groups={{0,2,4,6,8,10,12,14},{1,3,5,7,9,11,13,15},{16,18,20,22,24,26,28,30},{17..., dimensions={0} | all-to-all | bytes 3145728 | tf_op jit(solution)/shard_map/all_to_all | solution.py:67
  122.6 7.5 %shard_map.106 = (bf16[128,4096]{1,0:T(8,128)(2,1)S(1)}, bf16[384,256]{1,0:T(8,128)(2,1)S(1)}) custom-call(bf16[8,16,6144]{2,1,0:T(8,128)(2,1)S(1)} %all_to_all.25.g_hbm, bf16[4096,256]{1,0:T(8,128)(2,1)} %collective-permute-done.2.wo_own_ref, bf16[4096,256]{1,0:T(8,128)(2,1)} %collective-permute-done.wo_far_ref, ...), custom_call_target="tpu_custom_call" | custom-call | tf_op jit(solution)/shard_map/pallas_call | solution.py:187
  130.1 1.0 copy-done.3
  131.0 4.2 %collective-permute-start.11 = (bf16[128,256]{1,0:T(8,128)(2,1)S(1)}, bf16[128,256]{1,0:T(8,128)(2,1)S(1)}, u32[]{:S(2)}, u32[]{:S(2)}) collective-permute-start(bf16[128,256]{1,0:T(8,128)(2,1)S(1)} %slice.85), channel_id=1, source_target_pairs={{0,2},{1,3},{2,0},{3,1},{4,6},{5,7},{6,4},{7,5},{8,10},{9,11},{10,... | collective-permute-start | bytes 196616 | tf_op jit(solution)/shard_map/ppermute | solution.py:39
  135.3 3.9 %collective-permute-done.11 = bf16[128,256]{1,0:T(8,128)(2,1)S(1)} collective-permute-done((bf16[128,256]{1,0:T(8,128)(2,1)S(1)}, bf16[128,256]{1,0:T(8,128)(2,1)S(1)}, u32[]{:S(2)}, u32[]{:S(2)}) %collective-permute-start.11) | collective-permute-done | bytes 65568 | tf_op jit(solution)/shard_map/ppermute | solution.py:39
  139.8 6.5 %all-to-all-start.3 = ((bf16[8,16,4096]{2,1,0:T(8,128)(2,1)}), bf16[8,16,4096]{2,1,0:T(8,128)(2,1)}, u32[]{:S(2)}, u32[]{:S(2)}) async-start(bf16[8,16,4096]{2,1,0:T(8,128)(2,1)} %bitcast.73), calls=%async_computation.3 | async-start | bytes 2097152 | tf_op jit(solution)/shard_map/all_to_all | solution.py:67
  147.4 0.9 fusion.9
  148.3 0.7 slice_bitcast_fusion.11
  149.4 12.3 %all-to-all-done.3.refs_1_ = bf16[8,16,4096]{2,1,0:T(8,128)(2,1)} async-done(((bf16[8,16,4096]{2,1,0:T(8,128)(2,1)}), bf16[8,16,4096]{2,1,0:T(8,128)(2,1)}, u32[]{:S(2)}, u32[]{:S(2)}) %all-to-all-start.3) | async-done | bytes 1048608 | tf_op jit(solution)/shard_map/all_to_all | solution.py:67
  161.7 1.6 shard_map.107
  163.3 0.6 copy-done.13
  163.9 3.1 %collective-permute-done.13 = bf16[2,384,256]{2,1,0:T(8,128)(2,1)} collective-permute-done((bf16[2,384,256]{2,1,0:T(8,128)(2,1)}, bf16[2,384,256]{2,1,0:T(8,128)(2,1)}, u32[]{:S(2)}, u32[]{:S(2)}) %collective-permute-start.13) | collective-permute-done | bytes 393248 | tf_op jit(solution)/shard_map/ppermute | solution.py:47
  167.0 1.0 pad_maximum_fusion.2
  168.7 0.7 pad_maximum_fusion.6
  169.5 9.9 %all-to-all-start.4 = ((bf16[16,32,256]{2,1,0:T(8,128)(2,1)}), bf16[16,32,256]{2,1,0:T(8,128)(2,1)S(1)}, u32[]{:S(2)}, u32[]{:S(2)}) async-start(bf16[16,32,256]{2,1,0:T(8,128)(2,1)} %pad_maximum_fusion.6), calls=%async_computation.4 | async-start | bytes 524288 | tf_op jit(solution)/shard_map/all_to_all | solution.py:71
  179.4 1.0 fusion
  180.4 0.8 fusion.8
  181.2 0.8 slice_bitcast_fusion
  182.0 6.5 %shard_map.108 = (bf16[2048,256]{1,0:T(8,128)(2,1)}, bf16[1024,256]{1,0:T(8,128)(2,1)}) custom-call(s32[1]{0:T(128)} %bitcast.19.core_ref, bf16[16,96,2048]{2,1,0:T(8,128)(2,1)} %bitcast.75, bf16[16,4096]{1,0:T(8,128)(2,1)} %copy-done.13, bf16[256,256]{1,0:T(8,128)(2,1)} %get-tuple-element.95.near_0, bf16[256,256]{1,0:T(8,128)(2,1)} %get-tuple-element.96.near_1, ...), custom_call_target="tpu_custom_call" | custom-call | flops 1000 | bytes 1000 | tf_op jit(solution)/shard_map/pallas_call | solution.py:328
  188.5 1.0 constant_dynamic-slice_fusion
  189.5 1.3 collective-permute-start.15
  190.8 0.6 slice_bitcast_fusion.10
  191.5 0.7 slice_bitcast_fusion.6
  192.2 5.6 %shard_map.109 = bf16[2048,256]{1,0:T(8,128)(2,1)} custom-call(s32[1]{0:T(128)} %bitcast.19.core_ref, bf16[16,96,2048]{2,1,0:T(8,128)(2,1)} %bitcast.76, bf16[256,2048]{1,0:T(8,128)(2,1)} %bitcast.78, bf16[256,2048]{1,0:T(8,128)(2,1)} %collective-permute-done.12.far_hbm, bf16[128,256]{1,0:T(8,128)(2,1)} %get-tuple-element.107.near_0, ...), custom_call_target="tpu_custom_call" | custom-call | flops 1000 | bytes 1000 | tf_op jit(solution)/shard_map/pallas_call | solution.py:376
  197.9 0.7 copy.12
  198.6 5.4 %collective-permute-done.15 = bf16[512,256]{1,0:T(8,128)(2,1)S(1)} collective-permute-done((bf16[512,256]{1,0:T(8,128)(2,1)S(1)}, bf16[512,256]{1,0:T(8,128)(2,1)S(1)}, u32[]{:S(2)}, u32[]{:S(2)}) %collective-permute-start.15) | collective-permute-done | bytes 262176 | tf_op jit(solution)/shard_map/ppermute | solution.py:31
  204.0 0.8 select_bitcast_fusion
  (93 shorter events, 5.8 us)
Async XLA Ops:
  7.2 10.9 %copy-start = (bf16[2,2,1,128,256]{4,3,2,1,0:T(8,128)(2,1)S(1)}, bf16[2,2,1,128,256]{4,3,2,1,0:T(8,128)(2,1)}, u32[]{:S(2)}) copy-start(bf16[2,2,1,128,256]{4,3,2,1,0:T(8,128)(2,1)} %param.12) | copy-start | bytes 786436
  7.2 9.9 %collective-permute-start = (bf16[4096,256]{1,0:T(8,128)(2,1)}, bf16[4096,256]{1,0:T(8,128)(2,1)}, u32[]{:S(2)}, u32[]{:S(2)}) collective-permute-start(bf16[4096,256]{1,0:T(8,128)(2,1)} %bitcast.86), channel_id=1, source_target_pairs={{0,1},{1,0},{2,3},{3,2},{4,5},{5,4},{6,7},{7,6},{8,9},{9,8},{10,11... | collective-permute-start | bytes 6291464 | tf_op jit(solution)/shard_map/ppermute | solution.py:35
  7.3 10.1 %collective-permute-start.1 = (bf16[4096,256]{1,0:T(8,128)(2,1)}, bf16[4096,256]{1,0:T(8,128)(2,1)}, u32[]{:S(2)}, u32[]{:S(2)}) collective-permute-start(bf16[4096,256]{1,0:T(8,128)(2,1)} %bitcast.87), channel_id=1, source_target_pairs={{0,1},{1,0},{2,3},{3,2},{4,5},{5,4},{6,7},{7,6},{8,9},{9,8},{10,11... | collective-permute-start | bytes 6291464 | tf_op jit(solution)/shard_map/ppermute | solution.py:35
  9.8 7.8 %copy-start.20 = (bf16[2,2,1,128,256]{4,3,2,1,0:T(8,128)(2,1)S(1)}, bf16[2,2,1,128,256]{4,3,2,1,0:T(8,128)(2,1)}, u32[]{:S(2)}) copy-start(bf16[2,2,1,128,256]{4,3,2,1,0:T(8,128)(2,1)} %param.11) | copy-start | bytes 786436
  11.0 27.1 %all-to-all-start = ((bf16[16,160,256]{2,1,0:T(8,128)(2,1)}), bf16[16,160,256]{2,1,0:T(8,128)(2,1)S(1)}, u32[]{:S(2)}, u32[]{:S(2)}) async-start(bf16[16,160,256]{2,1,0:T(8,128)(2,1)} %pad_maximum_fusion), calls=%async_computation | async-start | bytes 2621440 | tf_op jit(solution)/shard_map/all_to_all | solution.py:71
  16.9 21.3 %collective-permute-start.4 = (bf16[4096,256]{1,0:T(8,128)(2,1)}, bf16[4096,256]{1,0:T(8,128)(2,1)}, u32[]{:S(2)}, u32[]{:S(2)}) collective-permute-start(bf16[4096,256]{1,0:T(8,128)(2,1)} %bitcast.88), channel_id=1, source_target_pairs={{0,1},{1,0},{2,3},{3,2},{4,5},{5,4},{6,7},{7,6},{8,9},{9,8},{10,11... | collective-permute-start | bytes 6291464 | tf_op jit(solution)/shard_map/ppermute | solution.py:35
  17.1 21.2 %collective-permute-start.2 = (bf16[4096,256]{1,0:T(8,128)(2,1)}, bf16[4096,256]{1,0:T(8,128)(2,1)}, u32[]{:S(2)}, u32[]{:S(2)}) collective-permute-start(bf16[4096,256]{1,0:T(8,128)(2,1)} %collective-permute-done.wo_far_ref), channel_id=1, source_target_pairs={{0,1},{1,0},{2,3},{3,2},{4,5},{5,4},{6,7},{7,6},{8,9},{9,8},{10,11... | collective-permute-start | bytes 6291464 | tf_op jit(solution)/shard_map/ppermute | solution.py:35
  17.4 20.8 %collective-permute-start.3 = (bf16[4096,256]{1,0:T(8,128)(2,1)}, bf16[4096,256]{1,0:T(8,128)(2,1)}, u32[]{:S(2)}, u32[]{:S(2)}) collective-permute-start(bf16[4096,256]{1,0:T(8,128)(2,1)} %collective-permute-done.1.wq_far_ref), channel_id=1, source_target_pairs={{0,1},{1,0},{2,3},{3,2},{4,5},{5,4},{6,7},{7,6},{8,9},{9,8},{10,11... | collective-permute-start | bytes 6291464 | tf_op jit(solution)/shard_map/ppermute | solution.py:35
  17.6 3.8 %collective-permute-start.5 = (bf16[2,128,256]{2,1,0:T(8,128)(2,1)S(1)}, bf16[2,128,256]{2,1,0:T(8,128)(2,1)S(1)}, u32[]{:S(2)}, u32[]{:S(2)}) collective-permute-start(bf16[2,128,256]{2,1,0:T(8,128)(2,1)S(1)} %get-tuple-element.109), channel_id=1, source_target_pairs={{0,1},{1,0},{2,3},{3,2},{4,5},{5,4},{6,7},{7,6},{8,9},{9,8},{10,11... | collective-permute-start | bytes 393224 | tf_op jit(solution)/shard_map/ppermute | solution.py:35
  24.1 22.0 %copy-start.1 = (f32[2,4,128,128]{3,2,1,0:T(8,128)}, f32[2,4,128,128]{3,2,1,0:T(8,128)S(1)}, u32[]{:S(2)}) copy-start(f32[2,4,128,128]{3,2,1,0:T(8,128)S(1)} %get-tuple-element.54.attention_ref) | copy-start | bytes 1572868
  24.2 22.0 %copy-start.11 = (bf16[2,128,512]{2,1,0:T(8,128)(2,1)}, bf16[2,128,512]{2,1,0:T(8,128)(2,1)S(1)}, u32[]{:S(2)}) copy-start(bf16[2,128,512]{2,1,0:T(8,128)(2,1)S(1)} %get-tuple-element.56) | copy-start | bytes 786436
  24.2 23.0 %collective-permute-start.6 = (bf16[2,128,512]{2,1,0:T(8,128)(2,1)S(1)}, bf16[2,128,512]{2,1,0:T(8,128)(2,1)S(1)}, u32[]{:S(2)}, u32[]{:S(2)}) collective-permute-start(bf16[2,128,512]{2,1,0:T(8,128)(2,1)S(1)} %get-tuple-element.56), channel_id=1, source_target_pairs={{0,240},{16,224},{32,208},{48,192},{64,176},{80,160},{96,144},{112... | collective-permute-start | bytes 786440 | tf_op jit(solution)/shard_map/ppermute | solution.py:47
  38.2 0.7 copy-start.16
  46.2 1.0 copy-start.4
  47.1 35.5 %copy-start.7 = (bf16[384,256]{1,0:T(8,128)(2,1)}, bf16[384,256]{1,0:T(8,128)(2,1)S(1)}, u32[]{:S(2)}) copy-start(bf16[384,256]{1,0:T(8,128)(2,1)S(1)} %get-tuple-element.76) | copy-start | bytes 589828
  47.1 0.8 copy-start.21
  47.9 28.6 %all-to-all-start.1 = ((bf16[8,16,4096]{2,1,0:T(8,128)(2,1)}), bf16[8,16,4096]{2,1,0:T(8,128)(2,1)S(1)}, u32[]{:S(2)}, u32[]{:S(2)}) async-start(bf16[8,16,4096]{2,1,0:T(8,128)(2,1)} %bitcast.74), calls=%async_computation.1 | async-start | bytes 2097152 | tf_op jit(solution)/shard_map/all_to_all | solution.py:67
  55.3 106.4 %all-gather.2.cloned.1.call-start = ((), (), s32[]{:S(2)}) async-start(), calls=%async_computation.5 | async-start | bytes 6684672 | tf_op jit(solution)/shard_map/all_gather | solution.py:75
  55.3 19.5 %collective-permute-start.7 = (bf16[48,2048]{1,0:T(8,128)(2,1)}, bf16[48,2048]{1,0:T(8,128)(2,1)}, u32[]{:S(2)}, u32[]{:S(2)}) collective-permute-start(bf16[48,2048]{1,0:T(8,128)(2,1)} %copy-done.16), channel_id=1, source_target_pairs={{0,240},{16,224},{32,208},{48,192},{64,176},{80,160},{96,144},{112... | collective-permute-start | bytes 589832 | tf_op jit(solution)/shard_map/ppermute | solution.py:47
  58.4 24.2 %collective-permute-start.10 = (bf16[128,256]{1,0:T(8,128)(2,1)S(1)}, bf16[128,256]{1,0:T(8,128)(2,1)S(1)}, u32[]{:S(2)}, u32[]{:S(2)}) collective-permute-start(bf16[128,256]{1,0:T(8,128)(2,1)S(1)} %slice.84), channel_id=1, source_target_pairs={{0,2},{1,3},{2,0},{3,1},{4,6},{5,7},{6,4},{7,5},{8,10},{9,11},{10,... | collective-permute-start | bytes 196616 | tf_op jit(solution)/shard_map/ppermute | solution.py:39
  76.8 14.1 %copy-start.14 = (bf16[16,16,256]{2,1,0:T(8,128)(2,1)}, bf16[16,16,256]{2,1,0:T(8,128)(2,1)S(1)}, u32[]{:S(2)}) copy-start(bf16[16,16,256]{2,1,0:T(8,128)(2,1)S(1)} %get-tuple-element.63) | copy-start | bytes 393220
  76.8 14.1 %collective-permute-start.8 = (bf16[16,4096]{1,0:T(8,128)(2,1)S(1)}, bf16[16,4096]{1,0:T(8,128)(2,1)S(1)}, u32[]{:S(2)}, u32[]{:S(2)}) collective-permute-start(bf16[16,4096]{1,0:T(8,128)(2,1)S(1)} %get-tuple-element.64), channel_id=1, source_target_pairs={{1,17},{3,19},{5,21},{7,23},{9,25},{11,27},{13,29},{15,31},{16,0},... | collective-permute-start | bytes 393224 | tf_op jit(solution)/shard_map/ppermute | solution.py:31
  78.8 12.2 %collective-permute-start.9 = (bf16[16,2048]{1,0:T(8,128)(2,1)S(1)}, bf16[16,2048]{1,0:T(8,128)(2,1)S(1)}, u32[]{:S(2)}, u32[]{:S(2)}) collective-permute-start(bf16[16,2048]{1,0:T(8,128)(2,1)S(1)} %constant_dynamic-slice_fusion.2), channel_id=1, source_target_pairs={{1,225},{3,227},{5,229},{7,231},{9,233},{11,235},{13,237},{15,239}... | collective-permute-start | bytes 196616 | tf_op jit(solution)/shard_map/ppermute | solution.py:31
  91.0 0.7 copy-start.5
  93.0 29.6 %copy-start.2 = (f32[2,4,128,128]{3,2,1,0:T(8,128)S(1)}, f32[2,4,128,128]{3,2,1,0:T(8,128)}, u32[]{:S(2)}) copy-start(f32[2,4,128,128]{3,2,1,0:T(8,128)} %copy-done.1) | copy-start | bytes 1572868
  130.1 1.0 copy-start.3
  131.0 8.1 %copy-start.9 = (bf16[384,256]{1,0:T(8,128)(2,1)}, bf16[384,256]{1,0:T(8,128)(2,1)S(1)}, u32[]{:S(2)}) copy-start(bf16[384,256]{1,0:T(8,128)(2,1)S(1)} %get-tuple-element.69) | copy-start | bytes 589828
  131.0 8.1 %collective-permute-start.11 = (bf16[128,256]{1,0:T(8,128)(2,1)S(1)}, bf16[128,256]{1,0:T(8,128)(2,1)S(1)}, u32[]{:S(2)}, u32[]{:S(2)}) collective-permute-start(bf16[128,256]{1,0:T(8,128)(2,1)S(1)} %slice.85), channel_id=1, source_target_pairs={{0,2},{1,3},{2,0},{3,1},{4,6},{5,7},{6,4},{7,5},{8,10},{9,11},{10,... | collective-permute-start | bytes 196616 | tf_op jit(solution)/shard_map/ppermute | solution.py:39
  139.8 21.9 %all-to-all-start.3 = ((bf16[8,16,4096]{2,1,0:T(8,128)(2,1)}), bf16[8,16,4096]{2,1,0:T(8,128)(2,1)}, u32[]{:S(2)}, u32[]{:S(2)}) async-start(bf16[8,16,4096]{2,1,0:T(8,128)(2,1)} %bitcast.73), calls=%async_computation.3 | async-start | bytes 2097152 | tf_op jit(solution)/shard_map/all_to_all | solution.py:67
  146.2 0.9 copy-start.8
  146.3 0.9 copy-start.24
  146.3 1.0 copy-start.10
  146.3 1.0 copy-start.25
  146.3 2.0 copy-start.12
  146.4 15.3 %copy-start.6 = (bf16[16,4096]{1,0:T(8,128)(2,1)S(1)}, bf16[16,4096]{1,0:T(8,128)(2,1)}, u32[]{:S(2)}) copy-start(bf16[16,4096]{1,0:T(8,128)(2,1)} %copy-done.5) | copy-start | bytes 393220
  146.5 16.8 %copy-start.17 = (bf16[16,16,2048]{2,1,0:T(8,128)(2,1)}, bf16[16,16,2048]{2,1,0:T(8,128)(2,1)S(1)}, u32[]{:S(2)}) copy-start(bf16[16,16,2048]{2,1,0:T(8,128)(2,1)S(1)} %pad_maximum_fusion.1) | copy-start | bytes 3145732
  146.5 2.9 %collective-permute-start.12 = (bf16[256,2048]{1,0:T(8,128)(2,1)S(1)}, bf16[256,2048]{1,0:T(8,128)(2,1)}, u32[]{:S(2)}, u32[]{:S(2)}) collective-permute-start(bf16[256,2048]{1,0:T(8,128)(2,1)S(1)} %bitcast.77), channel_id=1, source_target_pairs={{0,1},{1,0},{2,3},{3,2},{4,5},{5,4},{6,7},{7,6},{8,9},{9,8},{10,11... | collective-permute-start | bytes 3145736 | tf_op jit(solution)/shard_map/ppermute | solution.py:35
  148.3 18.7 %collective-permute-start.13 = (bf16[2,384,256]{2,1,0:T(8,128)(2,1)}, bf16[2,384,256]{2,1,0:T(8,128)(2,1)}, u32[]{:S(2)}, u32[]{:S(2)}) collective-permute-start(bf16[2,384,256]{2,1,0:T(8,128)(2,1)} %get-tuple-element.99), channel_id=1, source_target_pairs={{0,240},{16,224},{32,208},{48,192},{64,176},{80,160},{96,144},{112... | collective-permute-start | bytes 1179656 | tf_op jit(solution)/shard_map/ppermute | solution.py:47
  149.0 18.0 %copy-start.18 = (bf16[1,2,384,256]{3,2,1,0:T(8,128)(2,1)S(1)}, bf16[1,2,384,256]{3,2,1,0:T(8,128)(2,1)}, u32[]{:S(2)}) copy-start(bf16[1,2,384,256]{3,2,1,0:T(8,128)(2,1)} %get-tuple-element.98) | copy-start | bytes 1179652
  149.0 19.8 %copy-start.15 = (bf16[16,16,256]{2,1,0:T(8,128)(2,1)S(1)}, bf16[16,16,256]{2,1,0:T(8,128)(2,1)}, u32[]{:S(2)}) copy-start(bf16[16,16,256]{2,1,0:T(8,128)(2,1)} %copy-done.14) | copy-start | bytes 393220
  161.7 6.4 %copy-start.22 = (bf16[2,128,512]{2,1,0:T(8,128)(2,1)S(1)}, bf16[2,128,512]{2,1,0:T(8,128)(2,1)}, u32[]{:S(2)}) copy-start(bf16[2,128,512]{2,1,0:T(8,128)(2,1)} %copy-done.21) | copy-start | bytes 786436
  163.3 0.7 copy-start.13
  168.0 13.2 %collective-permute-start.14 = (bf16[2,2,256,256]{3,2,1,0:T(8,128)(2,1)S(1)}, bf16[2,2,256,256]{3,2,1,0:T(8,128)(2,1)S(1)}, u32[]{:S(2)}, u32[]{:S(2)}) collective-permute-start(bf16[2,2,256,256]{3,2,1,0:T(8,128)(2,1)S(1)} %pad_maximum_fusion.2), channel_id=1, source_target_pairs={{0,1},{1,0},{2,3},{3,2},{4,5},{5,4},{6,7},{7,6},{8,9},{9,8},{10,11... | collective-permute-start | bytes 1572872 | tf_op jit(solution)/shard_map/ppermute | solution.py:35
  168.2 23.3 %collective-permute-start.16 = (bf16[2,2,128,256]{3,2,1,0:T(8,128)(2,1)S(1)}, bf16[2,2,128,256]{3,2,1,0:T(8,128)(2,1)S(1)}, u32[]{:S(2)}, u32[]{:S(2)}) collective-permute-start(bf16[2,2,128,256]{3,2,1,0:T(8,128)(2,1)S(1)} %pad_maximum_fusion.7), channel_id=1, source_target_pairs={{0,1},{1,0},{2,3},{3,2},{4,5},{5,4},{6,7},{7,6},{8,9},{9,8},{10,11... | collective-permute-start | bytes 786440 | tf_op jit(solution)/shard_map/ppermute | solution.py:35
  169.5 28.4 %all-to-all-start.4 = ((bf16[16,32,256]{2,1,0:T(8,128)(2,1)}), bf16[16,32,256]{2,1,0:T(8,128)(2,1)S(1)}, u32[]{:S(2)}, u32[]{:S(2)}) async-start(bf16[16,32,256]{2,1,0:T(8,128)(2,1)} %pad_maximum_fusion.6), calls=%async_computation.4 | async-start | bytes 524288 | tf_op jit(solution)/shard_map/all_to_all | solution.py:71
  182.0 8.8 %copy-start.23 = (bf16[2,128,512]{2,1,0:T(8,128)(2,1)S(1)}, bf16[2,128,512]{2,1,0:T(8,128)(2,1)}, u32[]{:S(2)}) copy-start(bf16[2,128,512]{2,1,0:T(8,128)(2,1)} %copy-done.21) | copy-start | bytes 786436
  189.5 14.5 %collective-permute-start.15 = (bf16[512,256]{1,0:T(8,128)(2,1)S(1)}, bf16[512,256]{1,0:T(8,128)(2,1)S(1)}, u32[]{:S(2)}, u32[]{:S(2)}) collective-permute-start(bf16[512,256]{1,0:T(8,128)(2,1)S(1)} %constant_dynamic-slice_fusion), channel_id=1, source_target_pairs={{0,240},{1,241},{4,244},{5,245},{8,248},{9,249},{12,252},{13,253},... | collective-permute-start | bytes 786440 | tf_op jit(solution)/shard_map/ppermute | solution.py:31
  192.2 11.8 %copy-start.19 = (bf16[1024,256]{1,0:T(8,128)(2,1)S(1)}, bf16[1024,256]{1,0:T(8,128)(2,1)}, u32[]{:S(2)}) copy-start(bf16[1024,256]{1,0:T(8,128)(2,1)} %get-tuple-element.83) | copy-start | bytes 1572868
Sparse Core Ops, SparseCore 0:
  93.1 57.3 all-gather.1

commit v3 on v2

--- a/solution.py
+++ b/solution.py
@@ -93,6 +93,25 @@
 
 def params(mib):
     return pltpu.CompilerParams(vmem_limit_bytes=mib * 2**20)
+
+
+def first_kernel(grads_ref, inputs_ref, out_ref):
+    for m in range(8):
+        for r in range(2):
+            out_ref[2 * m + r, :TOK] = grads_ref[r]
+            for t in range(TICKS):
+                at = TOK + 16 * t
+                out_ref[2 * m + r, at:at + 16] = inputs_ref[r, t, m * 16:m * 16 + 16]
+
+
+def first_blocks(grads, inputs):
+    return pl.pallas_call(
+        first_kernel,
+        out_shape=jax.ShapeDtypeStruct((16, TOK + 32, 256), BF),
+        in_specs=[VMEM] * 2,
+        out_specs=VMEM,
+        compiler_params=params(16),
+    )(grads, inputs)
 
 
 def attend_kernel(q_ref, kv_ref, attention_ref, attended_ref):
@@ -202,7 +221,7 @@
     )(grads, wo_own, wo_far, wq_own, wq_far, w_kv, queries, pairs, attention)
 
 
-def finish_kernel(first, tick, chip_ref, terms_ref, rows_ref, grad_ref, out_ref, blocks_ref, kept):
+def finish_kernel(first, tick, chip_ref, terms_ref, rows_ref, grad_ref, before_ref, out_ref, blocks_ref, kept):
     x_at = TOK + 16 * tick
     here = pl.ds(pl.multiple_of(chip_ref[0] * 16, 16), 16)
     squares = jnp.zeros((16, 256), F32)
@@ -225,16 +244,20 @@
         out = before.astype(F32) + inverse * (kept[:, wide] - x * shift)
         out = out.astype(BF)
         out_ref[:, wide] = out
-        blocks_ref[j] = out
-
-
-def finish(tick, chip, terms, rows, grad_rows):
+        if first:
+            blocks_ref[j] = out
+        else:
+            blocks_ref[j, :16] = before_ref[j]
+            blocks_ref[j, 16:] = out
+
+
+def finish(tick, chip, terms, rows, grad_rows=None, blocks=None):
     first = tick == 0
-    operands = (chip.reshape(1), terms, rows) + (() if first else (grad_rows,))
+    operands = (chip.reshape(1), terms, rows) + (() if first else (grad_rows, blocks))
 
     def kernel(*refs):
         if first:
-            finish_kernel(first, tick, *refs[:3], None, *refs[3:])
+            finish_kernel(first, tick, *refs[:3], None, None, *refs[3:])
         else:
             finish_kernel(first, tick, *refs)
 
@@ -242,7 +265,7 @@
         kernel,
         out_shape=(
             jax.ShapeDtypeStruct((16, WIDTH), BF),
-            jax.ShapeDtypeStruct((16, 16, 256), BF),
+            jax.ShapeDtypeStruct((16, 16 if first else 32, 256), BF),
         ),
         in_specs=[pl.BlockSpec(memory_space=pltpu.SMEM)] + [VMEM] * (len(operands) - 1),
         out_specs=(VMEM, VMEM),
@@ -294,8 +317,7 @@
 
 
 def columns_kernel(
-    core_ref, x_hbm, after_hbm,
-    near_0, near_1, near_m0, near_m1, far_0, far_1, far_m0, far_m1,
+    core_ref, x_hbm, after_hbm, here_ref, got_ref, far_ref, far_got_ref,
     query_ref, pairs_ref, x_ref, right_ref, sems,
 ):
     copies = [
@@ -305,11 +327,13 @@
     for copy in copies:
         copy.start()
 
-    def both_columns(ref):
-        return lambda at: jnp.concatenate([ref[at:at + 16], ref[TOK + at:TOK + at + 16]], -1)
-
-    near = [both_columns(ref) for ref in (near_0, near_1, near_m0, near_m1)]
-    far = [both_columns(ref) for ref in (far_0, far_1, far_m0, far_m1)]
+    def both_columns(ref, t, pairs_at):
+        return lambda at: jnp.concatenate(
+            [ref[t, at:at + 16], ref[t, pairs_at + at:pairs_at + at + 16]], -1
+        )
+
+    near = [both_columns(ref, t, 2 * TOK) for ref in (here_ref, got_ref) for t in range(TICKS)]
+    far = [both_columns(ref, t, TOK) for ref in (far_ref, far_got_ref) for t in range(TICKS)]
     fill_right(core_ref, right_ref, near, far)
     for copy in copies:
         copy.wait()
@@ -331,7 +355,7 @@
             jax.ShapeDtypeStruct((HALF, 256), BF),
             jax.ShapeDtypeStruct((1024, 256), BF),
         ),
-        in_specs=[pl.BlockSpec(memory_space=pltpu.SMEM)] + [HBM] * 2 + [VMEM] * 8,
+        in_specs=[pl.BlockSpec(memory_space=pltpu.SMEM)] + [HBM] * 2 + [VMEM] * 4,
         out_specs=(VMEM, VMEM),
         scratch_shapes=[
             pltpu.VMEM((16, 64, HALF), BF),
@@ -344,8 +368,7 @@
 
 
 def output_kernel(
-    core_ref, x_hbm, near_hbm, far_hbm,
-    near_0, near_m0, near_1, near_m1, far_0, far_m0, far_1, far_m1,
+    core_ref, x_hbm, near_hbm, far_hbm, here, got, far,
     out_ref, g_ref, right_ref, second_ref, second_right, sems,
 ):
     copies = [
@@ -357,12 +380,13 @@
     for copy in copies:
         copy.start()
 
-    def rows(ref):
-        return lambda at: ref[at:at + 16]
-
-    fill_right(core_ref, right_ref, [rows(near_0), rows(near_m0)], [rows(far_0), rows(far_m0)])
-    for n, ref in enumerate((near_1, near_m1, far_1, far_m1)):
-        second_right[n * TOK:(n + 1) * TOK] = ref[...]
+    near_rows = [lambda at, ref=ref: ref[0, at:at + 16, :256] for ref in (here, got)]
+    far_rows = [lambda at, s=s: far[s, 0, at:at + 16] for s in range(2)]
+    fill_right(core_ref, right_ref, near_rows, far_rows)
+    for n, ref in enumerate((here, got)):
+        second_right[n * TOK:(n + 1) * TOK] = ref[1, :, :256]
+    for s in range(2):
+        second_right[(2 + s) * TOK:(3 + s) * TOK] = far[s, 1]
     for copy in copies:
         copy.wait()
     for j in range(8):
@@ -376,7 +400,7 @@
     return pl.pallas_call(
         output_kernel,
         out_shape=jax.ShapeDtypeStruct((HALF, 256), BF),
-        in_specs=[pl.BlockSpec(memory_space=pltpu.SMEM)] + [HBM] * 3 + [VMEM] * 8,
+        in_specs=[pl.BlockSpec(memory_space=pltpu.SMEM)] + [HBM] * 3 + [VMEM] * 3,
         out_specs=VMEM,
         scratch_shapes=[
             pltpu.VMEM((16, 32, HALF), BF),
@@ -407,10 +431,7 @@
     def features_of(x, which):
         return lax.dynamic_slice_in_dim(x, which * HALF, HALF, x.ndim - 1)
 
-    by_chip = (8, 2, TOK, 256)
-    tokens = inputs.reshape(2, TICKS, 8, 16, 256).transpose(2, 0, 1, 3, 4).reshape(8, 2, 32, 256)
-    mixed = jnp.concatenate([jnp.broadcast_to(grads[None], by_chip), tokens], 2)
-    rows = exchange16(mixed.reshape(16, TOK + 32, 256))
+    rows = exchange16(first_blocks(grads, inputs))
 
     wo_far = swap_core(w_o)
     queries = saved_q[:, :, 0]
@@ -444,10 +465,9 @@
     terms, att_m = together(terms, att_m)
     terms_0 = exchange8(terms.reshape(8, 16, WIDTH))
     got = mirror(sent)
-    x_rows = jnp.concatenate([held, got], 0)
-    terms_0, x_rows = together(terms_0, x_rows)
-
-    grad_in_0, blocks_0 = finish(0, chip, terms_0, rows, None)
+    terms_0, got = together(terms_0, got)
+
+    grad_in_0, blocks_0 = finish(0, chip, terms_0, rows)
     grad_rows = next_section(grad_in_0)
     sum_0 = both_chips(block(parts_0, 2))
     grad_half = next_mirror(
@@ -456,6 +476,7 @@
 
     spread_1 = jnp.concatenate([grad_rows, grad_half], 1)
     spread_1 = jnp.broadcast_to(spread_1[None], (8,) + spread_1.shape)
+    x_rows = jnp.concatenate([held, got], 0)
     spread_1, parts_0, sum_0, x_rows = together(spread_1, parts_0, sum_0, x_rows)
     full_1 = exchange8(spread_1)
     x_all = gather16(x_rows)
@@ -469,6 +490,7 @@
         [jnp.concatenate([parts_0[:2 * TOK], sum_0], 0), jnp.concatenate([parts_1[:2 * TOK], sum_1], 0)]
     )
     late_m = mirror(here)
+    far_here = swap_core(here[:, TOK:])
 
     att_far = swap_core(jnp.stack([attended[..., 256:], att_m[..., 256:]]))
     g_near = jnp.concatenate(
@@ -477,23 +499,13 @@
     g_far = swap_core(g_near)
     terms_1, x_all, g_far = together(terms_1, x_all, g_far)
 
-    after, blocks_1 = finish(1, chip, terms_1, rows, grad_rows)
-    out = exchange16(jnp.concatenate([blocks_0, blocks_1], 1))
+    after, blocks_1 = finish(1, chip, terms_1, rows, grad_rows, blocks_0)
+    out = exchange16(blocks_1)
     after, x_all, late_m = together(after, x_all, late_m)
-    both = jnp.stack([here, late_m])
-    near = jnp.concatenate([both[:, :, :TOK], both[:, :, 2 * TOK:]], 2)
-    far = swap_core(both[:, :, TOK:])
+    far_late = swap_core(late_m[:, TOK:])
     x_all = x_all.reshape(16, 96, HALF)
-    grad_query, acc_kv = columns(
-        core, x_all, after,
-        [near[0, 0], near[0, 1], near[1, 0], near[1, 1], far[0, 0], far[0, 1], far[1, 0], far[1, 1]],
-    )
-    att, att_got = attended[..., :256], att_m[..., :256]
-    grad_output = output_columns(
-        core, x_all, g_near, g_far,
-        [att[0], att_got[0], att[1], att_got[1],
-         att_far[0, 0], att_far[1, 0], att_far[0, 1], att_far[1, 1]],
-    )
+    grad_query, acc_kv = columns(core, x_all, after, [here, late_m, far_here, far_late])
+    grad_output = output_columns(core, x_all, g_near, g_far, [attended, att_m, att_far])
     kept = lax.dynamic_slice_in_dim(acc_kv, half * 512, 512, 0)
     given = lax.dynamic_slice_in_dim(acc_kv, (1 - half) * 512, 512, 0)
     taken = send(given, lambda s, c: (15 - s, c) if c // 2 % 2 == s // 8 else None)

time: 213 us -> 210 us (0.986)
  other arithmetic: 9.61 us -> 5.47 us
  waiting for transfers between devices: 60.4 us -> 56.6 us
  starting transfers between devices: 52.6 us -> 55.3 us
    ppermute x3, waiting for transfers between devices: 19.4 us -> 5.17 us  [mirror(): return lax.ppermute(x, 'section', [(i, 15 - i) for i in range(16)])]
    ppermute x2, waiting for transfers between devices: 3.85 us -> 17.4 us  [swap_z(): return lax.ppermute(x, 'tensor', [(i, i ^ 2) for i in range(16)])]
    unnamed x52 -> x60, local copies, waits for them, and re-layouts: 5.38 us -> 8.72 us
    another operation x3 -> x0, other arithmetic: 2.94 us -> none  [on_device(): both = jnp.stack([here, late_m])]
    squeeze x4 -> x0, local copies, waits for them, and re-layouts: 2.82 us -> none  [the longest x1 0.8 us: on_device(): far[1, 1]]
  transfers between devices with their start and end apart: 22 -> 23, of which waited for: 9 -> 9; matrix products, arithmetic and copies ran while one was open for 7% -> 4% of each run, Pallas kernels for 15% -> 16%
where the time goes in v3:
time: 210 us; the launch traced here: 208 us
  waiting for transfers between devices  56.6 us (27%)
  starting transfers between devices  55.3 us (26%)
  Pallas kernels  33.3 us (16%)
  blocking collectives  29.7 us (14%)
  between operations  14.5 us (7%)
  local copies, waits for them, and re-layouts  13.5 us (6%)
  other arithmetic  5.47 us (3%)
    all_to_all x1, blocking collectives, exchange8(): lax.all_to_all(x, 'tensor', 0, 0, axis_index_groups=SAME_CORE, tiled=True)  29.7 us
    ppermute x2, waiting for transfers between devices, swap_z(): return lax.ppermute(x, 'tensor', [(i, i ^ 2) for i in range(16)])  17.4 us
    all_to_all x2, starting transfers between devices, exchange16(): return lax.all_to_all(x, 'tensor', 0, 0, tiled=True)  15.9 us
    pallas_call x2, Pallas kernels, back(): pl.pallas_call(functools.partial(back_kernel, tick), out_shape=(jax.Shape...  14.7 us
    all_to_all x2, starting transfers between devices, exchange8(): lax.all_to_all(x, 'tensor', 0, 0, axis_index_groups=SAME_CORE, tiled=True)  13.6 us
    ppermute x3, waiting for transfers between devices, send(): return lax.ppermute(x, ('section', 'tensor'), pairs)  11.6 us
    all_to_all x2, waiting for transfers between devices, exchange8(): lax.all_to_all(x, 'tensor', 0, 0, axis_index_groups=SAME_CORE, tiled=True)  11 us
    ppermute x3, starting transfers between devices, mirror(): return lax.ppermute(x, 'section', [(i, 15 - i) for i in range(16)])  9.95 us
  transfers between devices with their start and end apart: 23, of which 9 were waited for; matrix products, arithmetic and copies ran while one was open for 4% of the time, Pallas kernels for 16%

profile of v3, /device:TPU:96, one launch (start us, length us, event | category | flops | bytes accessed | tf_op | source)
XLA Modules:
  0.0 208.4 jit_solution(8302170981058857057)
XLA Ops:
  7.8 0.9 copy-done.13
  8.7 0.9 copy-done.17
  9.6 1.2 shard_map.102
  10.8 5.9 %all-to-all-start = ((bf16[16,160,256]{2,1,0:T(8,128)(2,1)}), bf16[16,160,256]{2,1,0:T(8,128)(2,1)S(1)}, u32[]{:S(2)}, u32[]{:S(2)}) async-start(bf16[16,160,256]{2,1,0:T(8,128)(2,1)} %shard_map.102), calls=%async_computation | async-start | bytes 2621440 | tf_op jit(solution)/shard_map/all_to_all | solution.py:71
  17.9 3.4 %collective-permute-done.5 = bf16[2,128,256]{2,1,0:T(8,128)(2,1)S(1)} collective-permute-done((bf16[2,128,256]{2,1,0:T(8,128)(2,1)S(1)}, bf16[2,128,256]{2,1,0:T(8,128)(2,1)S(1)}, u32[]{:S(2)}, u32[]{:S(2)}) %collective-permute-start.5) | collective-permute-done | bytes 131104 | tf_op jit(solution)/shard_map/ppermute | solution.py:35
  21.3 2.7 %shard_map.104 = (f32[2,4,128,128]{3,2,1,0:T(8,128)S(1)}, bf16[2,128,512]{2,1,0:T(8,128)(2,1)S(1)}) custom-call(bf16[2,128,512]{2,1,0:T(8,128)(2,1)S(1)} %pad_maximum_fusion.3.q_ref, bf16[2,128,256]{2,1,0:T(8,128)(2,1)S(1)} %dynamic-slice_bitcast_fusion.kv_ref), custom_call_target="tpu_custom_call" | custom-call | tf_op jit(solution)/shard_map/pallas_call | solution.py:134
  24.0 5.9 %collective-permute-start.6 = (bf16[2,128,512]{2,1,0:T(8,128)(2,1)S(1)}, bf16[2,128,512]{2,1,0:T(8,128)(2,1)S(1)}, u32[]{:S(2)}, u32[]{:S(2)}) collective-permute-start(bf16[2,128,512]{2,1,0:T(8,128)(2,1)S(1)} %get-tuple-element.56.here), channel_id=1, source_target_pairs={{0,240},{16,224},{32,208},{48,192},{64,176},{80,160},{96,144},{112... | collective-permute-start | bytes 786440 | tf_op jit(solution)/shard_map/ppermute | solution.py:47
  29.9 8.0 %all-to-all-done.rows_ref.g_hbm.refs_2_ = bf16[16,160,256]{2,1,0:T(8,128)(2,1)S(1)} async-done(((bf16[16,160,256]{2,1,0:T(8,128)(2,1)}), bf16[16,160,256]{2,1,0:T(8,128)(2,1)S(1)}, u32[]{:S(2)}, u32[]{:S(2)}) %all-to-all-start) | async-done | bytes 1310752 | tf_op jit(solution)/shard_map/all_to_all | solution.py:71
  38.1 0.6 copy-done.18
  38.7 7.2 %shard_map.105 = (bf16[128,4096]{1,0:T(8,128)(2,1)S(1)}, bf16[384,256]{1,0:T(8,128)(2,1)S(1)}) custom-call(bf16[16,160,256]{2,1,0:T(8,128)(2,1)S(1)} %all-to-all-done.rows_ref.g_hbm.refs_2_, bf16[4096,256]{1,0:T(8,128)(2,1)} %collective-permute-done.2.wo_own_ref, bf16[4096,256]{1,0:T(8,128)(2,1)} %collective-permute-done.wo_far_ref, ...), custom_call_target="tpu_custom_call" | custom-call | tf_op jit(solution)/shard_map/pallas_call | solution.py:206
  46.0 1.0 copy-done.4
  47.0 0.7 copy-done.20
  47.7 7.4 %all-to-all-start.1 = ((bf16[8,16,4096]{2,1,0:T(8,128)(2,1)}), bf16[8,16,4096]{2,1,0:T(8,128)(2,1)S(1)}, u32[]{:S(2)}, u32[]{:S(2)}) async-start(bf16[8,16,4096]{2,1,0:T(8,128)(2,1)} %bitcast.35), calls=%async_computation.1 | async-start | bytes 2097152 | tf_op jit(solution)/shard_map/all_to_all | solution.py:67
  55.4 3.1 %collective-permute-start.7 = (bf16[48,2048]{1,0:T(8,128)(2,1)}, bf16[48,2048]{1,0:T(8,128)(2,1)}, u32[]{:S(2)}, u32[]{:S(2)}) collective-permute-start(bf16[48,2048]{1,0:T(8,128)(2,1)} %copy-done.18), channel_id=1, source_target_pairs={{0,240},{16,224},{32,208},{48,192},{64,176},{80,160},{96,144},{112... | collective-permute-start | bytes 589832 | tf_op jit(solution)/shard_map/ppermute | solution.py:47
  58.5 13.5 %collective-permute-done.10 = bf16[128,256]{1,0:T(8,128)(2,1)S(1)} collective-permute-done((bf16[128,256]{1,0:T(8,128)(2,1)S(1)}, bf16[128,256]{1,0:T(8,128)(2,1)S(1)}, u32[]{:S(2)}, u32[]{:S(2)}) %collective-permute-start.10) | collective-permute-done | bytes 65568 | tf_op jit(solution)/shard_map/ppermute | solution.py:39
  72.6 2.7 %collective-permute-done.7 = bf16[48,2048]{1,0:T(8,128)(2,1)} collective-permute-done((bf16[48,2048]{1,0:T(8,128)(2,1)}, bf16[48,2048]{1,0:T(8,128)(2,1)}, u32[]{:S(2)}, u32[]{:S(2)}) %collective-permute-start.7) | collective-permute-done | bytes 196640 | tf_op jit(solution)/shard_map/ppermute | solution.py:47
  75.7 0.6 copy-done.15
  76.3 1.9 collective-permute-start.8
  78.2 5.1 %collective-permute-start.9 = (bf16[16,2048]{1,0:T(8,128)(2,1)S(1)}, bf16[16,2048]{1,0:T(8,128)(2,1)S(1)}, u32[]{:S(2)}, u32[]{:S(2)}) collective-permute-start(bf16[16,2048]{1,0:T(8,128)(2,1)S(1)} %constant_dynamic-slice_fusion.2), channel_id=1, source_target_pairs={{1,225},{3,227},{5,229},{7,231},{9,233},{11,235},{13,237},{15,239}... | collective-permute-start | bytes 196616 | tf_op jit(solution)/shard_map/ppermute | solution.py:31
  83.3 1.7 pad_maximum_fusion.2
  85.0 5.4 %collective-permute-done.9 = bf16[16,2048]{1,0:T(8,128)(2,1)S(1)} collective-permute-done((bf16[16,2048]{1,0:T(8,128)(2,1)S(1)}, bf16[16,2048]{1,0:T(8,128)(2,1)S(1)}, u32[]{:S(2)}, u32[]{:S(2)}) %collective-permute-start.9) | collective-permute-done | bytes 65568 | tf_op jit(solution)/shard_map/ppermute | solution.py:31
  90.4 1.3 broadcast_in_dim.15
  91.8 29.7 %all_to_all.25.g_hbm = bf16[8,16,6144]{2,1,0:T(8,128)(2,1)S(1)} all-to-all(bf16[8,16,6144]{2,1,0:T(8,128)(2,1)} %broadcast_in_dim.15), channel_id=1, replica_groups={{0,2,4,6,8,10,12,14},{1,3,5,7,9,11,13,15},{16,18,20,22,24,26,28,30},{17..., dimensions={0} | all-to-all | bytes 3145728 | tf_op jit(solution)/shard_map/all_to_all | solution.py:67
  121.6 7.5 %shard_map.107 = (bf16[128,4096]{1,0:T(8,128)(2,1)S(1)}, bf16[384,256]{1,0:T(8,128)(2,1)S(1)}) custom-call(bf16[8,16,6144]{2,1,0:T(8,128)(2,1)S(1)} %all_to_all.25.g_hbm, bf16[4096,256]{1,0:T(8,128)(2,1)} %collective-permute-done.2.wo_own_ref, bf16[4096,256]{1,0:T(8,128)(2,1)} %collective-permute-done.wo_far_ref, ...), custom_call_target="tpu_custom_call" | custom-call | tf_op jit(solution)/shard_map/pallas_call | solution.py:206
  129.0 1.0 copy-done.3
  130.0 5.1 %collective-permute-start.11 = (bf16[128,256]{1,0:T(8,128)(2,1)S(1)}, bf16[128,256]{1,0:T(8,128)(2,1)S(1)}, u32[]{:S(2)}, u32[]{:S(2)}) collective-permute-start(bf16[128,256]{1,0:T(8,128)(2,1)S(1)} %slice.28), channel_id=1, source_target_pairs={{0,2},{1,3},{2,0},{3,1},{4,6},{5,7},{6,4},{7,5},{8,10},{9,11},{10,... | collective-permute-start | bytes 196616 | tf_op jit(solution)/shard_map/ppermute | solution.py:39
  135.1 3.9 %collective-permute-done.11 = bf16[128,256]{1,0:T(8,128)(2,1)S(1)} collective-permute-done((bf16[128,256]{1,0:T(8,128)(2,1)S(1)}, bf16[128,256]{1,0:T(8,128)(2,1)S(1)}, u32[]{:S(2)}, u32[]{:S(2)}) %collective-permute-start.11) | collective-permute-done | bytes 65568 | tf_op jit(solution)/shard_map/ppermute | solution.py:39
  139.0 0.6 add_convert_fusion
  139.6 6.2 %all-to-all-start.3 = ((bf16[8,16,4096]{2,1,0:T(8,128)(2,1)}), bf16[8,16,4096]{2,1,0:T(8,128)(2,1)}, u32[]{:S(2)}, u32[]{:S(2)}) async-start(bf16[8,16,4096]{2,1,0:T(8,128)(2,1)} %bitcast.34), calls=%async_computation.3 | async-start | bytes 2097152 | tf_op jit(solution)/shard_map/all_to_all | solution.py:67
  146.9 0.8 pad_maximum_fusion.1.here_ref
  147.7 1.0 collective-permute-start.13
  148.8 0.7 slice_bitcast_fusion.1
  149.4 0.7 fusion
  150.2 11.0 %all-to-all-done.3.refs_1_ = bf16[8,16,4096]{2,1,0:T(8,128)(2,1)} async-done(((bf16[8,16,4096]{2,1,0:T(8,128)(2,1)}), bf16[8,16,4096]{2,1,0:T(8,128)(2,1)}, u32[]{:S(2)}, u32[]{:S(2)}) %all-to-all-start.3) | async-done | bytes 1048608 | tf_op jit(solution)/shard_map/all_to_all | solution.py:67
  161.2 2.2 %shard_map.108 = (bf16[16,4096]{1,0:T(8,128)(2,1)S(1)}, bf16[16,32,256]{2,1,0:T(8,128)(2,1)}) custom-call(s32[1]{0:T(128)} %bitcast.chip_ref.refs_0_, bf16[8,16,4096]{2,1,0:T(8,128)(2,1)} %all-to-all-done.3.refs_1_, bf16[16,160,256]{2,1,0:T(8,128)(2,1)S(1)} %all-to-all-done.rows_ref.g_hbm.refs_2_, bf16[16,4096]{1,0:T(8,128)(2,1)S(1)} %copy-done.8, ...), custom_call_target="tpu_custom_call" | custom-call | tf_op jit(solution)/shard_map/pallas_call | solution.py:264
  163.4 0.6 copy-done.14
  164.0 2.4 %collective-permute-done.13.got_ref = bf16[2,384,256]{2,1,0:T(8,128)(2,1)} collective-permute-done((bf16[2,384,256]{2,1,0:T(8,128)(2,1)}, bf16[2,384,256]{2,1,0:T(8,128)(2,1)}, u32[]{:S(2)}, u32[]{:S(2)}) %collective-permute-start.13) | collective-permute-done | bytes 393248 | tf_op jit(solution)/shard_map/ppermute | solution.py:47
  166.5 1.0 slice.33
  167.6 10.0 %all-to-all-start.4 = ((bf16[16,32,256]{2,1,0:T(8,128)(2,1)}), bf16[16,32,256]{2,1,0:T(8,128)(2,1)S(1)}, u32[]{:S(2)}, u32[]{:S(2)}) async-start(bf16[16,32,256]{2,1,0:T(8,128)(2,1)} %get-tuple-element.73), calls=%async_computation.4 | async-start | bytes 524288 | tf_op jit(solution)/shard_map/all_to_all | solution.py:71
  177.9 0.7 copy-done.25
  178.6 6.5 %shard_map.109 = (bf16[2048,256]{1,0:T(8,128)(2,1)}, bf16[1024,256]{1,0:T(8,128)(2,1)}) custom-call(s32[1]{0:T(128)} %bitcast.16.core_ref, bf16[16,96,2048]{2,1,0:T(8,128)(2,1)} %bitcast.38, bf16[16,4096]{1,0:T(8,128)(2,1)} %copy-done.14, bf16[2,384,256]{2,1,0:T(8,128)(2,1)} %pad_maximum_fusion.1.here_ref, ...), custom_call_target="tpu_custom_call" | custom-call | flops 1000 | bytes 1000 | tf_op jit(solution)/shard_map/pallas_call | solution.py:352
  185.1 1.0 constant_dynamic-slice_fusion
  186.1 1.3 collective-permute-start.16
  187.4 0.7 copy-done.24
  188.1 5.6 %shard_map.110 = bf16[2048,256]{1,0:T(8,128)(2,1)} custom-call(s32[1]{0:T(128)} %bitcast.16.core_ref, bf16[16,96,2048]{2,1,0:T(8,128)(2,1)} %bitcast.39, bf16[256,2048]{1,0:T(8,128)(2,1)} %bitcast.41, bf16[256,2048]{1,0:T(8,128)(2,1)} %collective-permute-done.12.far_hbm, bf16[2,128,512]{2,1,0:T(8,128)(2,1)} %copy-done.5, bf16[2,128,512]{2,1,0:T(8,128)(2,1)} %copy-done.20, ...), custom_call_target="tpu_custom_call" | custom-call | flops 1000 | bytes 1000 | tf_op jit(solution)/shard_map/pallas_call | solution.py:400
  193.8 0.7 copy.11
  194.5 6.3 %collective-permute-done.16 = bf16[512,256]{1,0:T(8,128)(2,1)S(1)} collective-permute-done((bf16[512,256]{1,0:T(8,128)(2,1)S(1)}, bf16[512,256]{1,0:T(8,128)(2,1)S(1)}, u32[]{:S(2)}, u32[]{:S(2)}) %collective-permute-start.16) | collective-permute-done | bytes 262176 | tf_op jit(solution)/shard_map/ppermute | solution.py:31
  200.8 0.8 select_bitcast_fusion
  (95 shorter events, 4.7 us)
Async XLA Ops:
  7.2 10.7 %copy-start = (bf16[2,2,1,128,256]{4,3,2,1,0:T(8,128)(2,1)S(1)}, bf16[2,2,1,128,256]{4,3,2,1,0:T(8,128)(2,1)}, u32[]{:S(2)}) copy-start(bf16[2,2,1,128,256]{4,3,2,1,0:T(8,128)(2,1)} %param.12) | copy-start | bytes 786436
  7.2 9.7 %collective-permute-start = (bf16[4096,256]{1,0:T(8,128)(2,1)}, bf16[4096,256]{1,0:T(8,128)(2,1)}, u32[]{:S(2)}, u32[]{:S(2)}) collective-permute-start(bf16[4096,256]{1,0:T(8,128)(2,1)} %bitcast.45), channel_id=1, source_target_pairs={{0,1},{1,0},{2,3},{3,2},{4,5},{5,4},{6,7},{7,6},{8,9},{9,8},{10,11... | collective-permute-start | bytes 6291464 | tf_op jit(solution)/shard_map/ppermute | solution.py:35
  7.3 10.0 %collective-permute-start.1 = (bf16[4096,256]{1,0:T(8,128)(2,1)}, bf16[4096,256]{1,0:T(8,128)(2,1)}, u32[]{:S(2)}, u32[]{:S(2)}) collective-permute-start(bf16[4096,256]{1,0:T(8,128)(2,1)} %bitcast.46), channel_id=1, source_target_pairs={{0,1},{1,0},{2,3},{3,2},{4,5},{5,4},{6,7},{7,6},{8,9},{9,8},{10,11... | collective-permute-start | bytes 6291464 | tf_op jit(solution)/shard_map/ppermute | solution.py:35
  7.8 0.9 copy-start.13
  8.7 0.9 copy-start.17
  9.6 7.8 %copy-start.27 = (bf16[2,2,1,128,256]{4,3,2,1,0:T(8,128)(2,1)S(1)}, bf16[2,2,1,128,256]{4,3,2,1,0:T(8,128)(2,1)}, u32[]{:S(2)}) copy-start(bf16[2,2,1,128,256]{4,3,2,1,0:T(8,128)(2,1)} %param.11) | copy-start | bytes 786436
  10.8 27.1 %all-to-all-start = ((bf16[16,160,256]{2,1,0:T(8,128)(2,1)}), bf16[16,160,256]{2,1,0:T(8,128)(2,1)S(1)}, u32[]{:S(2)}, u32[]{:S(2)}) async-start(bf16[16,160,256]{2,1,0:T(8,128)(2,1)} %shard_map.102), calls=%async_computation | async-start | bytes 2621440 | tf_op jit(solution)/shard_map/all_to_all | solution.py:71
  16.8 21.3 %collective-permute-start.4 = (bf16[4096,256]{1,0:T(8,128)(2,1)}, bf16[4096,256]{1,0:T(8,128)(2,1)}, u32[]{:S(2)}, u32[]{:S(2)}) collective-permute-start(bf16[4096,256]{1,0:T(8,128)(2,1)} %bitcast.47), channel_id=1, source_target_pairs={{0,1},{1,0},{2,3},{3,2},{4,5},{5,4},{6,7},{7,6},{8,9},{9,8},{10,11... | collective-permute-start | bytes 6291464 | tf_op jit(solution)/shard_map/ppermute | solution.py:35
  16.9 21.2 %collective-permute-start.2 = (bf16[4096,256]{1,0:T(8,128)(2,1)}, bf16[4096,256]{1,0:T(8,128)(2,1)}, u32[]{:S(2)}, u32[]{:S(2)}) collective-permute-start(bf16[4096,256]{1,0:T(8,128)(2,1)} %collective-permute-done.wo_far_ref), channel_id=1, source_target_pairs={{0,1},{1,0},{2,3},{3,2},{4,5},{5,4},{6,7},{7,6},{8,9},{9,8},{10,11... | collective-permute-start | bytes 6291464 | tf_op jit(solution)/shard_map/ppermute | solution.py:35
  17.3 20.8 %collective-permute-start.3 = (bf16[4096,256]{1,0:T(8,128)(2,1)}, bf16[4096,256]{1,0:T(8,128)(2,1)}, u32[]{:S(2)}, u32[]{:S(2)}) collective-permute-start(bf16[4096,256]{1,0:T(8,128)(2,1)} %collective-permute-done.1.wq_far_ref), channel_id=1, source_target_pairs={{0,1},{1,0},{2,3},{3,2},{4,5},{5,4},{6,7},{7,6},{8,9},{9,8},{10,11... | collective-permute-start | bytes 6291464 | tf_op jit(solution)/shard_map/ppermute | solution.py:35
  17.4 3.8 %collective-permute-start.5 = (bf16[2,128,256]{2,1,0:T(8,128)(2,1)S(1)}, bf16[2,128,256]{2,1,0:T(8,128)(2,1)S(1)}, u32[]{:S(2)}, u32[]{:S(2)}) collective-permute-start(bf16[2,128,256]{2,1,0:T(8,128)(2,1)S(1)} %get-tuple-element.89), channel_id=1, source_target_pairs={{0,1},{1,0},{2,3},{3,2},{4,5},{5,4},{6,7},{7,6},{8,9},{9,8},{10,11... | collective-permute-start | bytes 393224 | tf_op jit(solution)/shard_map/ppermute | solution.py:35
  24.0 22.0 %copy-start.1 = (f32[2,4,128,128]{3,2,1,0:T(8,128)}, f32[2,4,128,128]{3,2,1,0:T(8,128)S(1)}, u32[]{:S(2)}) copy-start(f32[2,4,128,128]{3,2,1,0:T(8,128)S(1)} %get-tuple-element.54.attention_ref) | copy-start | bytes 1572868
  24.0 22.0 %copy-start.5 = (bf16[2,128,512]{2,1,0:T(8,128)(2,1)}, bf16[2,128,512]{2,1,0:T(8,128)(2,1)S(1)}, u32[]{:S(2)}) copy-start(bf16[2,128,512]{2,1,0:T(8,128)(2,1)S(1)} %get-tuple-element.56.here) | copy-start | bytes 786436
  24.0 23.0 %collective-permute-start.6 = (bf16[2,128,512]{2,1,0:T(8,128)(2,1)S(1)}, bf16[2,128,512]{2,1,0:T(8,128)(2,1)S(1)}, u32[]{:S(2)}, u32[]{:S(2)}) collective-permute-start(bf16[2,128,512]{2,1,0:T(8,128)(2,1)S(1)} %get-tuple-element.56.here), channel_id=1, source_target_pairs={{0,240},{16,224},{32,208},{48,192},{64,176},{80,160},{96,144},{112... | collective-permute-start | bytes 786440 | tf_op jit(solution)/shard_map/ppermute | solution.py:47
  46.0 1.0 copy-start.4
  47.0 28.7 %copy-start.9 = (bf16[384,256]{1,0:T(8,128)(2,1)}, bf16[384,256]{1,0:T(8,128)(2,1)S(1)}, u32[]{:S(2)}) copy-start(bf16[384,256]{1,0:T(8,128)(2,1)S(1)} %get-tuple-element.76) | copy-start | bytes 589828
  47.0 0.7 copy-start.20
  47.7 27.6 %all-to-all-start.1 = ((bf16[8,16,4096]{2,1,0:T(8,128)(2,1)}), bf16[8,16,4096]{2,1,0:T(8,128)(2,1)S(1)}, u32[]{:S(2)}, u32[]{:S(2)}) async-start(bf16[8,16,4096]{2,1,0:T(8,128)(2,1)} %bitcast.35), calls=%async_computation.1 | async-start | bytes 2097152 | tf_op jit(solution)/shard_map/all_to_all | solution.py:67
  55.1 106.0 %all-gather.2.cloned.1.call-start = ((), (), s32[]{:S(2)}) async-start(), calls=%async_computation.5 | async-start | bytes 6684672 | tf_op jit(solution)/shard_map/all_gather | solution.py:75
  55.2 16.8 %collective-permute-start.10 = (bf16[128,256]{1,0:T(8,128)(2,1)S(1)}, bf16[128,256]{1,0:T(8,128)(2,1)S(1)}, u32[]{:S(2)}, u32[]{:S(2)}) collective-permute-start(bf16[128,256]{1,0:T(8,128)(2,1)S(1)} %slice.27), channel_id=1, source_target_pairs={{0,2},{1,3},{2,0},{3,1},{4,6},{5,7},{6,4},{7,5},{8,10},{9,11},{10,... | collective-permute-start | bytes 196616 | tf_op jit(solution)/shard_map/ppermute | solution.py:39
  55.4 19.9 %collective-permute-start.7 = (bf16[48,2048]{1,0:T(8,128)(2,1)}, bf16[48,2048]{1,0:T(8,128)(2,1)}, u32[]{:S(2)}, u32[]{:S(2)}) collective-permute-start(bf16[48,2048]{1,0:T(8,128)(2,1)} %copy-done.18), channel_id=1, source_target_pairs={{0,240},{16,224},{32,208},{48,192},{64,176},{80,160},{96,144},{112... | collective-permute-start | bytes 589832 | tf_op jit(solution)/shard_map/ppermute | solution.py:47
  76.3 14.1 %collective-permute-start.8 = (bf16[16,4096]{1,0:T(8,128)(2,1)S(1)}, bf16[16,4096]{1,0:T(8,128)(2,1)S(1)}, u32[]{:S(2)}, u32[]{:S(2)}) collective-permute-start(bf16[16,4096]{1,0:T(8,128)(2,1)S(1)} %get-tuple-element.62), channel_id=1, source_target_pairs={{1,17},{3,19},{5,21},{7,23},{9,25},{11,27},{13,29},{15,31},{16,0},... | collective-permute-start | bytes 393224 | tf_op jit(solution)/shard_map/ppermute | solution.py:31
  78.2 12.2 %collective-permute-start.9 = (bf16[16,2048]{1,0:T(8,128)(2,1)S(1)}, bf16[16,2048]{1,0:T(8,128)(2,1)S(1)}, u32[]{:S(2)}, u32[]{:S(2)}) collective-permute-start(bf16[16,2048]{1,0:T(8,128)(2,1)S(1)} %constant_dynamic-slice_fusion.2), channel_id=1, source_target_pairs={{1,225},{3,227},{5,229},{7,231},{9,233},{11,235},{13,237},{15,239}... | collective-permute-start | bytes 196616 | tf_op jit(solution)/shard_map/ppermute | solution.py:31
  90.4 1.4 copy-start.7
  91.8 29.8 %copy-start.2 = (f32[2,4,128,128]{3,2,1,0:T(8,128)S(1)}, f32[2,4,128,128]{3,2,1,0:T(8,128)}, u32[]{:S(2)}) copy-start(f32[2,4,128,128]{3,2,1,0:T(8,128)} %copy-done.1) | copy-start | bytes 1572868
  129.0 1.0 copy-start.3
  130.0 9.0 %copy-start.11 = (bf16[384,256]{1,0:T(8,128)(2,1)}, bf16[384,256]{1,0:T(8,128)(2,1)S(1)}, u32[]{:S(2)}) copy-start(bf16[384,256]{1,0:T(8,128)(2,1)S(1)} %get-tuple-element.68) | copy-start | bytes 589828
  130.0 9.0 %collective-permute-start.11 = (bf16[128,256]{1,0:T(8,128)(2,1)S(1)}, bf16[128,256]{1,0:T(8,128)(2,1)S(1)}, u32[]{:S(2)}, u32[]{:S(2)}) collective-permute-start(bf16[128,256]{1,0:T(8,128)(2,1)S(1)} %slice.28), channel_id=1, source_target_pairs={{0,2},{1,3},{2,0},{3,1},{4,6},{5,7},{6,4},{7,5},{8,10},{9,11},{10,... | collective-permute-start | bytes 196616 | tf_op jit(solution)/shard_map/ppermute | solution.py:39
  139.6 21.5 %all-to-all-start.3 = ((bf16[8,16,4096]{2,1,0:T(8,128)(2,1)}), bf16[8,16,4096]{2,1,0:T(8,128)(2,1)}, u32[]{:S(2)}, u32[]{:S(2)}) async-start(bf16[8,16,4096]{2,1,0:T(8,128)(2,1)} %bitcast.34), calls=%async_computation.3 | async-start | bytes 2097152 | tf_op jit(solution)/shard_map/all_to_all | solution.py:67
  145.8 0.9 copy-start.10
  145.8 0.9 copy-start.28
  145.8 1.1 copy-start.12
  145.8 1.1 copy-start.29
  145.9 2.9 %copy-start.6 = (bf16[2,128,512]{2,1,0:T(8,128)(2,1)S(1)}, bf16[2,128,512]{2,1,0:T(8,128)(2,1)}, u32[]{:S(2)}) copy-start(bf16[2,128,512]{2,1,0:T(8,128)(2,1)} %copy-done.5) | copy-start | bytes 786436
  145.9 15.2 %copy-start.8 = (bf16[16,4096]{1,0:T(8,128)(2,1)S(1)}, bf16[16,4096]{1,0:T(8,128)(2,1)}, u32[]{:S(2)}) copy-start(bf16[16,4096]{1,0:T(8,128)(2,1)} %copy-done.7) | copy-start | bytes 393220
  145.9 15.2 %copy-start.16 = (bf16[16,16,256]{2,1,0:T(8,128)(2,1)S(1)}, bf16[16,16,256]{2,1,0:T(8,128)(2,1)}, u32[]{:S(2)}) copy-start(bf16[16,16,256]{2,1,0:T(8,128)(2,1)} %copy-done.15) | copy-start | bytes 393220
  146.0 17.4 %copy-start.19 = (bf16[16,16,2048]{2,1,0:T(8,128)(2,1)}, bf16[16,16,2048]{2,1,0:T(8,128)(2,1)S(1)}, u32[]{:S(2)}) copy-start(bf16[16,16,2048]{2,1,0:T(8,128)(2,1)S(1)} %pad_maximum_fusion) | copy-start | bytes 3145732
  146.0 4.1 %collective-permute-start.12 = (bf16[256,2048]{1,0:T(8,128)(2,1)S(1)}, bf16[256,2048]{1,0:T(8,128)(2,1)}, u32[]{:S(2)}, u32[]{:S(2)}) collective-permute-start(bf16[256,2048]{1,0:T(8,128)(2,1)S(1)} %bitcast.40), channel_id=1, source_target_pairs={{0,1},{1,0},{2,3},{3,2},{4,5},{5,4},{6,7},{7,6},{8,9},{9,8},{10,11... | collective-permute-start | bytes 3145736 | tf_op jit(solution)/shard_map/ppermute | solution.py:35
  147.7 18.7 %collective-permute-start.13 = (bf16[2,384,256]{2,1,0:T(8,128)(2,1)}, bf16[2,384,256]{2,1,0:T(8,128)(2,1)}, u32[]{:S(2)}, u32[]{:S(2)}) collective-permute-start(bf16[2,384,256]{2,1,0:T(8,128)(2,1)} %pad_maximum_fusion.1.here_ref), channel_id=1, source_target_pairs={{0,240},{16,224},{32,208},{48,192},{64,176},{80,160},{96,144},{112... | collective-permute-start | bytes 1179656 | tf_op jit(solution)/shard_map/ppermute | solution.py:47
  149.4 18.1 %copy-start.21 = (bf16[2,128,512]{2,1,0:T(8,128)(2,1)S(1)}, bf16[2,128,512]{2,1,0:T(8,128)(2,1)}, u32[]{:S(2)}) copy-start(bf16[2,128,512]{2,1,0:T(8,128)(2,1)} %copy-done.20) | copy-start | bytes 786436
  150.2 27.4 %copy-start.23 = (bf16[1,2,128,256]{3,2,1,0:T(8,128)(2,1)S(1)}, bf16[1,2,128,256]{3,2,1,0:T(8,128)(2,1)}, u32[]{:S(2)}) copy-start(bf16[1,2,128,256]{3,2,1,0:T(8,128)(2,1)} %slice_bitcast_fusion.1) | copy-start | bytes 393220
  150.2 27.7 %collective-permute-start.14 = (bf16[2,256,256]{2,1,0:T(8,128)(2,1)}, bf16[2,256,256]{2,1,0:T(8,128)(2,1)S(1)}, u32[]{:S(2)}, u32[]{:S(2)}) collective-permute-start(bf16[2,256,256]{2,1,0:T(8,128)(2,1)} %fusion), channel_id=1, source_target_pairs={{0,1},{1,0},{2,3},{3,2},{4,5},{5,4},{6,7},{7,6},{8,9},{9,8},{10,11... | collective-permute-start | bytes 786440 | tf_op jit(solution)/shard_map/ppermute | solution.py:35
  167.4 10.4 %collective-permute-start.15 = (bf16[2,256,256]{2,1,0:T(8,128)(2,1)S(1)}, bf16[2,256,256]{2,1,0:T(8,128)(2,1)S(1)}, u32[]{:S(2)}, u32[]{:S(2)}) collective-permute-start(bf16[2,256,256]{2,1,0:T(8,128)(2,1)S(1)} %slice.33), channel_id=1, source_target_pairs={{0,1},{1,0},{2,3},{3,2},{4,5},{5,4},{6,7},{7,6},{8,9},{9,8},{10,11... | collective-permute-start | bytes 786440 | tf_op jit(solution)/shard_map/ppermute | solution.py:35
  167.6 26.2 %all-to-all-start.4 = ((bf16[16,32,256]{2,1,0:T(8,128)(2,1)}), bf16[16,32,256]{2,1,0:T(8,128)(2,1)S(1)}, u32[]{:S(2)}, u32[]{:S(2)}) async-start(bf16[16,32,256]{2,1,0:T(8,128)(2,1)} %get-tuple-element.73), calls=%async_computation.4 | async-start | bytes 524288 | tf_op jit(solution)/shard_map/all_to_all | solution.py:71
  177.6 9.8 %collective-permute-start.17 = (bf16[2,2,128,256]{3,2,1,0:T(8,128)(2,1)S(1)}, bf16[2,2,128,256]{3,2,1,0:T(8,128)(2,1)S(1)}, u32[]{:S(2)}, u32[]{:S(2)}) collective-permute-start(bf16[2,2,128,256]{3,2,1,0:T(8,128)(2,1)S(1)} %pad_maximum_fusion.4), channel_id=1, source_target_pairs={{0,1},{1,0},{2,3},{3,2},{4,5},{5,4},{6,7},{7,6},{8,9},{9,8},{10,11... | collective-permute-start | bytes 786440 | tf_op jit(solution)/shard_map/ppermute | solution.py:35
  177.9 0.8 copy-start.26
  186.1 14.7 %collective-permute-start.16 = (bf16[512,256]{1,0:T(8,128)(2,1)S(1)}, bf16[512,256]{1,0:T(8,128)(2,1)S(1)}, u32[]{:S(2)}, u32[]{:S(2)}) collective-permute-start(bf16[512,256]{1,0:T(8,128)(2,1)S(1)} %constant_dynamic-slice_fusion), channel_id=1, source_target_pairs={{0,240},{1,241},{4,244},{5,245},{8,248},{9,249},{12,252},{13,253},... | collective-permute-start | bytes 786440 | tf_op jit(solution)/shard_map/ppermute | solution.py:31
  187.4 13.4 %copy-start.22 = (bf16[1024,256]{1,0:T(8,128)(2,1)S(1)}, bf16[1024,256]{1,0:T(8,128)(2,1)}, u32[]{:S(2)}) copy-start(bf16[1024,256]{1,0:T(8,128)(2,1)} %get-tuple-element.83) | copy-start | bytes 1572868
  (5 other events, 3.4 us)
Sparse Core Ops, SparseCore 0:
  91.9 57.1 all-gather.1

commit v4 on v3

--- a/solution.py
+++ b/solution.py
@@ -221,6 +221,9 @@
     )(grads, wo_own, wo_far, wq_own, wq_far, w_kv, queries, pairs, attention)
 
 
+LAST_ROWS = 64
+
+
 def finish_kernel(first, tick, chip_ref, terms_ref, rows_ref, grad_ref, before_ref, out_ref, blocks_ref, kept):
     x_at = TOK + 16 * tick
     here = pl.ds(pl.multiple_of(chip_ref[0] * 16, 16), 16)
@@ -248,7 +251,8 @@
             blocks_ref[j] = out
         else:
             blocks_ref[j, :16] = before_ref[j]
-            blocks_ref[j, 16:] = out
+            for copy in range(1, blocks_ref.shape[1] // 16):
+                blocks_ref[j, copy * 16:copy * 16 + 16] = out
 
 
 def finish(tick, chip, terms, rows, grad_rows=None, blocks=None):
@@ -265,7 +269,7 @@
         kernel,
         out_shape=(
             jax.ShapeDtypeStruct((16, WIDTH), BF),
-            jax.ShapeDtypeStruct((16, 16 if first else 32, 256), BF),
+            jax.ShapeDtypeStruct((16, 16 if first else LAST_ROWS, 256), BF),
         ),
         in_specs=[pl.BlockSpec(memory_space=pltpu.SMEM)] + [VMEM] * (len(operands) - 1),
         out_specs=(VMEM, VMEM),
@@ -500,12 +504,13 @@
     terms_1, x_all, g_far = together(terms_1, x_all, g_far)
 
     after, blocks_1 = finish(1, chip, terms_1, rows, grad_rows, blocks_0)
-    out = exchange16(blocks_1)
-    after, x_all, late_m = together(after, x_all, late_m)
+    out = exchange16(blocks_1)[:, :TICKS * 16]
+    after, x_all = together(after, x_all)
+    x_all = x_all.reshape(16, 96, HALF)
+    grad_output = output_columns(core, x_all, g_near, g_far, [attended, att_m, att_far])
+    grad_output, late_m = together(grad_output, late_m)
     far_late = swap_core(late_m[:, TOK:])
-    x_all = x_all.reshape(16, 96, HALF)
     grad_query, acc_kv = columns(core, x_all, after, [here, late_m, far_here, far_late])
-    grad_output = output_columns(core, x_all, g_near, g_far, [attended, att_m, att_far])
     kept = lax.dynamic_slice_in_dim(acc_kv, half * 512, 512, 0)
     given = lax.dynamic_slice_in_dim(acc_kv, (1 - half) * 512, 512, 0)
     taken = send(given, lambda s, c: (15 - s, c) if c // 2 % 2 == s // 8 else None)

time: 210 us -> 213 us (1.014)
  waiting for transfers between devices: 56.6 us -> 62.6 us
    ppermute x3, waiting for transfers between devices: 11.6 us -> 18.7 us  [send(): return lax.ppermute(x, ('section', 'tensor'), pairs)]
    all_to_all x2, starting transfers between devices: 15.9 us -> 13.4 us  [exchange16(): return lax.all_to_all(x, 'tensor', 0, 0, tiled=True)]
    ppermute x3, waiting for transfers between devices: 5.17 us -> 2.74 us  [mirror(): return lax.ppermute(x, 'section', [(i, 15 - i) for i in range(16)])]
    unnamed x60 -> x54, local copies, waits for them, and re-layouts: 8.72 us -> 8.1 us
where the time goes in v4:
time: 213 us; the launch traced here: 212 us
  waiting for transfers between devices  62.6 us (29%)
  starting transfers between devices  53.5 us (25%)
  Pallas kernels  33.4 us (16%)
  blocking collectives  29.7 us (14%)
  between operations  14.4 us (7%)
  local copies, waits for them, and re-layouts  12.3 us (6%)
  other arithmetic  6.41 us (3%)
    all_to_all x1, blocking collectives, exchange8(): lax.all_to_all(x, 'tensor', 0, 0, axis_index_groups=SAME_CORE, tiled=True)  29.7 us
    ppermute x3, waiting for transfers between devices, send(): return lax.ppermute(x, ('section', 'tensor'), pairs)  18.7 us
    ppermute x2, waiting for transfers between devices, swap_z(): return lax.ppermute(x, 'tensor', [(i, i ^ 2) for i in range(16)])  17.4 us
    pallas_call x2, Pallas kernels, back(): pl.pallas_call(functools.partial(back_kernel, tick), out_shape=(jax.Shape...  14.7 us
    all_to_all x2, starting transfers between devices, exchange8(): lax.all_to_all(x, 'tensor', 0, 0, axis_index_groups=SAME_CORE, tiled=True)  13.6 us
    all_to_all x2, starting transfers between devices, exchange16(): return lax.all_to_all(x, 'tensor', 0, 0, tiled=True)  13.4 us
    all_to_all x2, waiting for transfers between devices, exchange8(): lax.all_to_all(x, 'tensor', 0, 0, axis_index_groups=SAME_CORE, tiled=True)  11.1 us
    ppermute x3, starting transfers between devices, mirror(): return lax.ppermute(x, 'section', [(i, 15 - i) for i in range(16)])  10.3 us
  transfers between devices with their start and end apart: 23, of which 9 were waited for; matrix products, arithmetic and copies ran while one was open for 4% of the time, Pallas kernels for 16%

profile of v4, /device:TPU:96, one launch (start us, length us, event | category | flops | bytes accessed | tf_op | source)
XLA Modules:
  0.0 212.3 jit_solution(15022962517831354810)
XLA Ops:
  7.8 0.9 copy-done.13
  8.7 0.9 copy-done.17
  9.6 1.2 shard_map.102
  10.8 5.9 %all-to-all-start = ((bf16[16,160,256]{2,1,0:T(8,128)(2,1)}), bf16[16,160,256]{2,1,0:T(8,128)(2,1)S(1)}, u32[]{:S(2)}, u32[]{:S(2)}) async-start(bf16[16,160,256]{2,1,0:T(8,128)(2,1)} %shard_map.102), calls=%async_computation | async-start | bytes 2621440 | tf_op jit(solution)/shard_map/all_to_all | solution.py:71
  17.9 3.4 %collective-permute-done.5 = bf16[2,128,256]{2,1,0:T(8,128)(2,1)S(1)} collective-permute-done((bf16[2,128,256]{2,1,0:T(8,128)(2,1)S(1)}, bf16[2,128,256]{2,1,0:T(8,128)(2,1)S(1)}, u32[]{:S(2)}, u32[]{:S(2)}) %collective-permute-start.5) | collective-permute-done | bytes 131104 | tf_op jit(solution)/shard_map/ppermute | solution.py:35
  21.3 2.7 %shard_map.104 = (f32[2,4,128,128]{3,2,1,0:T(8,128)S(1)}, bf16[2,128,512]{2,1,0:T(8,128)(2,1)S(1)}) custom-call(bf16[2,128,512]{2,1,0:T(8,128)(2,1)S(1)} %pad_maximum_fusion.3.q_ref, bf16[2,128,256]{2,1,0:T(8,128)(2,1)S(1)} %dynamic-slice_bitcast_fusion.kv_ref), custom_call_target="tpu_custom_call" | custom-call | tf_op jit(solution)/shard_map/pallas_call | solution.py:134
  24.0 5.9 %collective-permute-start.6 = (bf16[2,128,512]{2,1,0:T(8,128)(2,1)S(1)}, bf16[2,128,512]{2,1,0:T(8,128)(2,1)S(1)}, u32[]{:S(2)}, u32[]{:S(2)}) collective-permute-start(bf16[2,128,512]{2,1,0:T(8,128)(2,1)S(1)} %get-tuple-element.57.here), channel_id=1, source_target_pairs={{0,240},{16,224},{32,208},{48,192},{64,176},{80,160},{96,144},{112... | collective-permute-start | bytes 786440 | tf_op jit(solution)/shard_map/ppermute | solution.py:47
  29.9 8.0 %all-to-all-done.rows_ref.g_hbm.refs_2_ = bf16[16,160,256]{2,1,0:T(8,128)(2,1)S(1)} async-done(((bf16[16,160,256]{2,1,0:T(8,128)(2,1)}), bf16[16,160,256]{2,1,0:T(8,128)(2,1)S(1)}, u32[]{:S(2)}, u32[]{:S(2)}) %all-to-all-start) | async-done | bytes 1310752 | tf_op jit(solution)/shard_map/all_to_all | solution.py:71
  38.1 0.6 copy-done.18
  38.7 7.2 %shard_map.105 = (bf16[128,4096]{1,0:T(8,128)(2,1)S(1)}, bf16[384,256]{1,0:T(8,128)(2,1)S(1)}) custom-call(bf16[16,160,256]{2,1,0:T(8,128)(2,1)S(1)} %all-to-all-done.rows_ref.g_hbm.refs_2_, bf16[4096,256]{1,0:T(8,128)(2,1)} %collective-permute-done.2.wo_own_ref, bf16[4096,256]{1,0:T(8,128)(2,1)} %collective-permute-done.wo_far_ref, ...), custom_call_target="tpu_custom_call" | custom-call | tf_op jit(solution)/shard_map/pallas_call | solution.py:206
  46.0 1.0 copy-done.4
  47.0 0.7 copy-done.20
  47.7 7.4 %all-to-all-start.1 = ((bf16[8,16,4096]{2,1,0:T(8,128)(2,1)}), bf16[8,16,4096]{2,1,0:T(8,128)(2,1)S(1)}, u32[]{:S(2)}, u32[]{:S(2)}) async-start(bf16[8,16,4096]{2,1,0:T(8,128)(2,1)} %bitcast.35), calls=%async_computation.1 | async-start | bytes 2097152 | tf_op jit(solution)/shard_map/all_to_all | solution.py:67
  55.4 3.1 %collective-permute-start.7 = (bf16[48,2048]{1,0:T(8,128)(2,1)}, bf16[48,2048]{1,0:T(8,128)(2,1)}, u32[]{:S(2)}, u32[]{:S(2)}) collective-permute-start(bf16[48,2048]{1,0:T(8,128)(2,1)} %copy-done.18), channel_id=1, source_target_pairs={{0,240},{16,224},{32,208},{48,192},{64,176},{80,160},{96,144},{112... | collective-permute-start | bytes 589832 | tf_op jit(solution)/shard_map/ppermute | solution.py:47
  58.5 13.5 %collective-permute-done.10 = bf16[128,256]{1,0:T(8,128)(2,1)S(1)} collective-permute-done((bf16[128,256]{1,0:T(8,128)(2,1)S(1)}, bf16[128,256]{1,0:T(8,128)(2,1)S(1)}, u32[]{:S(2)}, u32[]{:S(2)}) %collective-permute-start.10) | collective-permute-done | bytes 65568 | tf_op jit(solution)/shard_map/ppermute | solution.py:39
  72.0 0.7 add_convert_fusion.1
  72.6 2.7 %collective-permute-done.7 = bf16[48,2048]{1,0:T(8,128)(2,1)} collective-permute-done((bf16[48,2048]{1,0:T(8,128)(2,1)}, bf16[48,2048]{1,0:T(8,128)(2,1)}, u32[]{:S(2)}, u32[]{:S(2)}) %collective-permute-start.7) | collective-permute-done | bytes 196640 | tf_op jit(solution)/shard_map/ppermute | solution.py:47
  75.7 0.6 copy-done.15
  76.3 1.9 collective-permute-start.8
  78.3 5.1 %collective-permute-start.9 = (bf16[16,2048]{1,0:T(8,128)(2,1)S(1)}, bf16[16,2048]{1,0:T(8,128)(2,1)S(1)}, u32[]{:S(2)}, u32[]{:S(2)}) collective-permute-start(bf16[16,2048]{1,0:T(8,128)(2,1)S(1)} %constant_dynamic-slice_fusion.2), channel_id=1, source_target_pairs={{1,225},{3,227},{5,229},{7,231},{9,233},{11,235},{13,237},{15,239}... | collective-permute-start | bytes 196616 | tf_op jit(solution)/shard_map/ppermute | solution.py:31
  83.4 1.7 pad_maximum_fusion.2
  85.1 5.4 %collective-permute-done.9 = bf16[16,2048]{1,0:T(8,128)(2,1)S(1)} collective-permute-done((bf16[16,2048]{1,0:T(8,128)(2,1)S(1)}, bf16[16,2048]{1,0:T(8,128)(2,1)S(1)}, u32[]{:S(2)}, u32[]{:S(2)}) %collective-permute-start.9) | collective-permute-done | bytes 65568 | tf_op jit(solution)/shard_map/ppermute | solution.py:31
  90.5 1.4 broadcast_in_dim.15
  91.8 29.7 %all_to_all.25.g_hbm = bf16[8,16,6144]{2,1,0:T(8,128)(2,1)S(1)} all-to-all(bf16[8,16,6144]{2,1,0:T(8,128)(2,1)} %broadcast_in_dim.15), channel_id=1, replica_groups={{0,2,4,6,8,10,12,14},{1,3,5,7,9,11,13,15},{16,18,20,22,24,26,28,30},{17..., dimensions={0} | all-to-all | bytes 3145728 | tf_op jit(solution)/shard_map/all_to_all | solution.py:67
  121.6 7.5 %shard_map.107 = (bf16[128,4096]{1,0:T(8,128)(2,1)S(1)}, bf16[384,256]{1,0:T(8,128)(2,1)S(1)}) custom-call(bf16[8,16,6144]{2,1,0:T(8,128)(2,1)S(1)} %all_to_all.25.g_hbm, bf16[4096,256]{1,0:T(8,128)(2,1)} %collective-permute-done.2.wo_own_ref, bf16[4096,256]{1,0:T(8,128)(2,1)} %collective-permute-done.wo_far_ref, ...), custom_call_target="tpu_custom_call" | custom-call | tf_op jit(solution)/shard_map/pallas_call | solution.py:206
  129.1 1.0 copy-done.3
  130.0 5.1 %collective-permute-start.11 = (bf16[128,256]{1,0:T(8,128)(2,1)S(1)}, bf16[128,256]{1,0:T(8,128)(2,1)S(1)}, u32[]{:S(2)}, u32[]{:S(2)}) collective-permute-start(bf16[128,256]{1,0:T(8,128)(2,1)S(1)} %slice.31), channel_id=1, source_target_pairs={{0,2},{1,3},{2,0},{3,1},{4,6},{5,7},{6,4},{7,5},{8,10},{9,11},{10,... | collective-permute-start | bytes 196616 | tf_op jit(solution)/shard_map/ppermute | solution.py:39
  135.1 3.9 %collective-permute-done.11 = bf16[128,256]{1,0:T(8,128)(2,1)S(1)} collective-permute-done((bf16[128,256]{1,0:T(8,128)(2,1)S(1)}, bf16[128,256]{1,0:T(8,128)(2,1)S(1)}, u32[]{:S(2)}, u32[]{:S(2)}) %collective-permute-start.11) | collective-permute-done | bytes 65568 | tf_op jit(solution)/shard_map/ppermute | solution.py:39
  139.0 0.6 add_convert_fusion
  139.6 6.2 %all-to-all-start.3 = ((bf16[8,16,4096]{2,1,0:T(8,128)(2,1)}), bf16[8,16,4096]{2,1,0:T(8,128)(2,1)}, u32[]{:S(2)}, u32[]{:S(2)}) async-start(bf16[8,16,4096]{2,1,0:T(8,128)(2,1)} %bitcast.34), calls=%async_computation.3 | async-start | bytes 2097152 | tf_op jit(solution)/shard_map/all_to_all | solution.py:67
  146.2 0.6 copy-done.6
  147.1 0.8 pad_maximum_fusion.1.here_ref
  147.9 1.4 collective-permute-start.14
  149.3 0.7 pad_maximum_fusion.4
  150.1 11.1 %all-to-all-done.3.refs_1_ = bf16[8,16,4096]{2,1,0:T(8,128)(2,1)} async-done(((bf16[8,16,4096]{2,1,0:T(8,128)(2,1)}), bf16[8,16,4096]{2,1,0:T(8,128)(2,1)}, u32[]{:S(2)}, u32[]{:S(2)}) %all-to-all-start.3) | async-done | bytes 1048608 | tf_op jit(solution)/shard_map/all_to_all | solution.py:67
  161.2 2.3 %shard_map.108 = (bf16[16,4096]{1,0:T(8,128)(2,1)S(1)}, bf16[16,64,256]{2,1,0:T(8,128)(2,1)}) custom-call(s32[1]{0:T(128)} %bitcast.chip_ref.refs_0_, bf16[8,16,4096]{2,1,0:T(8,128)(2,1)} %all-to-all-done.3.refs_1_, bf16[16,160,256]{2,1,0:T(8,128)(2,1)S(1)} %all-to-all-done.rows_ref.g_hbm.refs_2_, bf16[16,4096]{1,0:T(8,128)(2,1)S(1)} %copy-done.8, ...), custom_call_target="tpu_custom_call" | custom-call | tf_op jit(solution)/shard_map/pallas_call | solution.py:268
  163.5 0.7 copy-done.14
  164.2 7.5 %all-to-all-start.4 = ((bf16[16,64,256]{2,1,0:T(8,128)(2,1)}), bf16[16,64,256]{2,1,0:T(8,128)(2,1)S(1)}, u32[]{:S(2)}, u32[]{:S(2)}) async-start(bf16[16,64,256]{2,1,0:T(8,128)(2,1)} %get-tuple-element.74), calls=%async_computation.4 | async-start | bytes 1048576 | tf_op jit(solution)/shard_map/all_to_all | solution.py:71
  171.9 5.6 %shard_map.109 = bf16[2048,256]{1,0:T(8,128)(2,1)} custom-call(s32[1]{0:T(128)} %bitcast.16.core_ref, bf16[16,96,2048]{2,1,0:T(8,128)(2,1)} %bitcast.38, bf16[256,2048]{1,0:T(8,128)(2,1)} %bitcast.41, bf16[256,2048]{1,0:T(8,128)(2,1)} %collective-permute-done.12.far_hbm, bf16[2,128,512]{2,1,0:T(8,128)(2,1)} %copy-done.5, bf16[2,128,512]{2,1,0:T(8,128)(2,1)} %copy-done.20, ...), custom_call_target="tpu_custom_call" | custom-call | flops 1000 | bytes 1000 | tf_op jit(solution)/shard_map/pallas_call | solution.py:404
  177.5 1.0 slice.39
  179.0 1.2 collective-permute-done.16.far_got_ref
  180.1 0.7 copy-done.23
  180.8 6.5 %shard_map.110 = (bf16[2048,256]{1,0:T(8,128)(2,1)}, bf16[1024,256]{1,0:T(8,128)(2,1)}) custom-call(s32[1]{0:T(128)} %bitcast.16.core_ref, bf16[16,96,2048]{2,1,0:T(8,128)(2,1)} %bitcast.39, bf16[16,4096]{1,0:T(8,128)(2,1)} %copy-done.14, bf16[2,384,256]{2,1,0:T(8,128)(2,1)} %pad_maximum_fusion.1.here_ref, ...), custom_call_target="tpu_custom_call" | custom-call | flops 1000 | bytes 1000 | tf_op jit(solution)/shard_map/pallas_call | solution.py:356
  187.3 1.0 constant_dynamic-slice_fusion
  188.3 1.3 collective-permute-start.17
  189.6 13.4 %collective-permute-done.17 = bf16[512,256]{1,0:T(8,128)(2,1)S(1)} collective-permute-done((bf16[512,256]{1,0:T(8,128)(2,1)S(1)}, bf16[512,256]{1,0:T(8,128)(2,1)S(1)}, u32[]{:S(2)}, u32[]{:S(2)}) %collective-permute-start.17) | collective-permute-done | bytes 262176 | tf_op jit(solution)/shard_map/ppermute | solution.py:31
  203.0 1.7 select_bitcast_fusion
  204.7 0.7 copy.11
  (90 shorter events, 3.9 us)
Async XLA Ops:
  7.2 10.7 %copy-start = (bf16[2,2,1,128,256]{4,3,2,1,0:T(8,128)(2,1)S(1)}, bf16[2,2,1,128,256]{4,3,2,1,0:T(8,128)(2,1)}, u32[]{:S(2)}) copy-start(bf16[2,2,1,128,256]{4,3,2,1,0:T(8,128)(2,1)} %param.12) | copy-start | bytes 786436
  7.2 9.7 %collective-permute-start = (bf16[4096,256]{1,0:T(8,128)(2,1)}, bf16[4096,256]{1,0:T(8,128)(2,1)}, u32[]{:S(2)}, u32[]{:S(2)}) collective-permute-start(bf16[4096,256]{1,0:T(8,128)(2,1)} %bitcast.45), channel_id=1, source_target_pairs={{0,1},{1,0},{2,3},{3,2},{4,5},{5,4},{6,7},{7,6},{8,9},{9,8},{10,11... | collective-permute-start | bytes 6291464 | tf_op jit(solution)/shard_map/ppermute | solution.py:35
  7.3 10.0 %collective-permute-start.1 = (bf16[4096,256]{1,0:T(8,128)(2,1)}, bf16[4096,256]{1,0:T(8,128)(2,1)}, u32[]{:S(2)}, u32[]{:S(2)}) collective-permute-start(bf16[4096,256]{1,0:T(8,128)(2,1)} %bitcast.46), channel_id=1, source_target_pairs={{0,1},{1,0},{2,3},{3,2},{4,5},{5,4},{6,7},{7,6},{8,9},{9,8},{10,11... | collective-permute-start | bytes 6291464 | tf_op jit(solution)/shard_map/ppermute | solution.py:35
  7.8 0.9 copy-start.13
  8.7 0.9 copy-start.17
  9.6 7.8 %copy-start.24 = (bf16[2,2,1,128,256]{4,3,2,1,0:T(8,128)(2,1)S(1)}, bf16[2,2,1,128,256]{4,3,2,1,0:T(8,128)(2,1)}, u32[]{:S(2)}) copy-start(bf16[2,2,1,128,256]{4,3,2,1,0:T(8,128)(2,1)} %param.11) | copy-start | bytes 786436
  10.8 27.1 %all-to-all-start = ((bf16[16,160,256]{2,1,0:T(8,128)(2,1)}), bf16[16,160,256]{2,1,0:T(8,128)(2,1)S(1)}, u32[]{:S(2)}, u32[]{:S(2)}) async-start(bf16[16,160,256]{2,1,0:T(8,128)(2,1)} %shard_map.102), calls=%async_computation | async-start | bytes 2621440 | tf_op jit(solution)/shard_map/all_to_all | solution.py:71
  16.8 21.3 %collective-permute-start.4 = (bf16[4096,256]{1,0:T(8,128)(2,1)}, bf16[4096,256]{1,0:T(8,128)(2,1)}, u32[]{:S(2)}, u32[]{:S(2)}) collective-permute-start(bf16[4096,256]{1,0:T(8,128)(2,1)} %bitcast.47), channel_id=1, source_target_pairs={{0,1},{1,0},{2,3},{3,2},{4,5},{5,4},{6,7},{7,6},{8,9},{9,8},{10,11... | collective-permute-start | bytes 6291464 | tf_op jit(solution)/shard_map/ppermute | solution.py:35
  16.9 21.2 %collective-permute-start.2 = (bf16[4096,256]{1,0:T(8,128)(2,1)}, bf16[4096,256]{1,0:T(8,128)(2,1)}, u32[]{:S(2)}, u32[]{:S(2)}) collective-permute-start(bf16[4096,256]{1,0:T(8,128)(2,1)} %collective-permute-done.wo_far_ref), channel_id=1, source_target_pairs={{0,1},{1,0},{2,3},{3,2},{4,5},{5,4},{6,7},{7,6},{8,9},{9,8},{10,11... | collective-permute-start | bytes 6291464 | tf_op jit(solution)/shard_map/ppermute | solution.py:35
  17.3 20.8 %collective-permute-start.3 = (bf16[4096,256]{1,0:T(8,128)(2,1)}, bf16[4096,256]{1,0:T(8,128)(2,1)}, u32[]{:S(2)}, u32[]{:S(2)}) collective-permute-start(bf16[4096,256]{1,0:T(8,128)(2,1)} %collective-permute-done.1.wq_far_ref), channel_id=1, source_target_pairs={{0,1},{1,0},{2,3},{3,2},{4,5},{5,4},{6,7},{7,6},{8,9},{9,8},{10,11... | collective-permute-start | bytes 6291464 | tf_op jit(solution)/shard_map/ppermute | solution.py:35
  17.4 3.8 %collective-permute-start.5 = (bf16[2,128,256]{2,1,0:T(8,128)(2,1)S(1)}, bf16[2,128,256]{2,1,0:T(8,128)(2,1)S(1)}, u32[]{:S(2)}, u32[]{:S(2)}) collective-permute-start(bf16[2,128,256]{2,1,0:T(8,128)(2,1)S(1)} %get-tuple-element.91), channel_id=1, source_target_pairs={{0,1},{1,0},{2,3},{3,2},{4,5},{5,4},{6,7},{7,6},{8,9},{9,8},{10,11... | collective-permute-start | bytes 393224 | tf_op jit(solution)/shard_map/ppermute | solution.py:35
  24.0 22.0 %copy-start.1 = (f32[2,4,128,128]{3,2,1,0:T(8,128)}, f32[2,4,128,128]{3,2,1,0:T(8,128)S(1)}, u32[]{:S(2)}) copy-start(f32[2,4,128,128]{3,2,1,0:T(8,128)S(1)} %get-tuple-element.55.attention_ref) | copy-start | bytes 1572868
  24.0 22.0 %copy-start.5 = (bf16[2,128,512]{2,1,0:T(8,128)(2,1)}, bf16[2,128,512]{2,1,0:T(8,128)(2,1)S(1)}, u32[]{:S(2)}) copy-start(bf16[2,128,512]{2,1,0:T(8,128)(2,1)S(1)} %get-tuple-element.57.here) | copy-start | bytes 786436
  24.0 23.0 %collective-permute-start.6 = (bf16[2,128,512]{2,1,0:T(8,128)(2,1)S(1)}, bf16[2,128,512]{2,1,0:T(8,128)(2,1)S(1)}, u32[]{:S(2)}, u32[]{:S(2)}) collective-permute-start(bf16[2,128,512]{2,1,0:T(8,128)(2,1)S(1)} %get-tuple-element.57.here), channel_id=1, source_target_pairs={{0,240},{16,224},{32,208},{48,192},{64,176},{80,160},{96,144},{112... | collective-permute-start | bytes 786440 | tf_op jit(solution)/shard_map/ppermute | solution.py:47
  38.1 0.7 copy-start.18
  46.0 1.0 copy-start.4
  47.0 28.7 %copy-start.9 = (bf16[384,256]{1,0:T(8,128)(2,1)}, bf16[384,256]{1,0:T(8,128)(2,1)S(1)}, u32[]{:S(2)}) copy-start(bf16[384,256]{1,0:T(8,128)(2,1)S(1)} %get-tuple-element.79) | copy-start | bytes 589828
  47.0 0.7 copy-start.20
  47.7 27.6 %all-to-all-start.1 = ((bf16[8,16,4096]{2,1,0:T(8,128)(2,1)}), bf16[8,16,4096]{2,1,0:T(8,128)(2,1)S(1)}, u32[]{:S(2)}, u32[]{:S(2)}) async-start(bf16[8,16,4096]{2,1,0:T(8,128)(2,1)} %bitcast.35), calls=%async_computation.1 | async-start | bytes 2097152 | tf_op jit(solution)/shard_map/all_to_all | solution.py:67
  55.2 106.0 %all-gather.2.cloned.1.call-start = ((), (), s32[]{:S(2)}) async-start(), calls=%async_computation.5 | async-start | bytes 6684672 | tf_op jit(solution)/shard_map/all_gather | solution.py:75
  55.2 16.8 %collective-permute-start.10 = (bf16[128,256]{1,0:T(8,128)(2,1)S(1)}, bf16[128,256]{1,0:T(8,128)(2,1)S(1)}, u32[]{:S(2)}, u32[]{:S(2)}) collective-permute-start(bf16[128,256]{1,0:T(8,128)(2,1)S(1)} %slice.30), channel_id=1, source_target_pairs={{0,2},{1,3},{2,0},{3,1},{4,6},{5,7},{6,4},{7,5},{8,10},{9,11},{10,... | collective-permute-start | bytes 196616 | tf_op jit(solution)/shard_map/ppermute | solution.py:39
  55.4 19.9 %collective-permute-start.7 = (bf16[48,2048]{1,0:T(8,128)(2,1)}, bf16[48,2048]{1,0:T(8,128)(2,1)}, u32[]{:S(2)}, u32[]{:S(2)}) collective-permute-start(bf16[48,2048]{1,0:T(8,128)(2,1)} %copy-done.18), channel_id=1, source_target_pairs={{0,240},{16,224},{32,208},{48,192},{64,176},{80,160},{96,144},{112... | collective-permute-start | bytes 589832 | tf_op jit(solution)/shard_map/ppermute | solution.py:47
  76.3 14.1 %collective-permute-start.8 = (bf16[16,4096]{1,0:T(8,128)(2,1)S(1)}, bf16[16,4096]{1,0:T(8,128)(2,1)S(1)}, u32[]{:S(2)}, u32[]{:S(2)}) collective-permute-start(bf16[16,4096]{1,0:T(8,128)(2,1)S(1)} %get-tuple-element.63), channel_id=1, source_target_pairs={{1,17},{3,19},{5,21},{7,23},{9,25},{11,27},{13,29},{15,31},{16,0},... | collective-permute-start | bytes 393224 | tf_op jit(solution)/shard_map/ppermute | solution.py:31
  78.3 12.2 %collective-permute-start.9 = (bf16[16,2048]{1,0:T(8,128)(2,1)S(1)}, bf16[16,2048]{1,0:T(8,128)(2,1)S(1)}, u32[]{:S(2)}, u32[]{:S(2)}) collective-permute-start(bf16[16,2048]{1,0:T(8,128)(2,1)S(1)} %constant_dynamic-slice_fusion.2), channel_id=1, source_target_pairs={{1,225},{3,227},{5,229},{7,231},{9,233},{11,235},{13,237},{15,239}... | collective-permute-start | bytes 196616 | tf_op jit(solution)/shard_map/ppermute | solution.py:31
  90.4 1.4 copy-start.7
  91.8 29.8 %copy-start.2 = (f32[2,4,128,128]{3,2,1,0:T(8,128)S(1)}, f32[2,4,128,128]{3,2,1,0:T(8,128)}, u32[]{:S(2)}) copy-start(f32[2,4,128,128]{3,2,1,0:T(8,128)} %copy-done.1) | copy-start | bytes 1572868
  129.0 1.0 copy-start.3
  130.0 9.0 %copy-start.11 = (bf16[384,256]{1,0:T(8,128)(2,1)}, bf16[384,256]{1,0:T(8,128)(2,1)S(1)}, u32[]{:S(2)}) copy-start(bf16[384,256]{1,0:T(8,128)(2,1)S(1)} %get-tuple-element.69) | copy-start | bytes 589828
  130.0 9.0 %collective-permute-start.11 = (bf16[128,256]{1,0:T(8,128)(2,1)S(1)}, bf16[128,256]{1,0:T(8,128)(2,1)S(1)}, u32[]{:S(2)}, u32[]{:S(2)}) collective-permute-start(bf16[128,256]{1,0:T(8,128)(2,1)S(1)} %slice.31), channel_id=1, source_target_pairs={{0,2},{1,3},{2,0},{3,1},{4,6},{5,7},{6,4},{7,5},{8,10},{9,11},{10,... | collective-permute-start | bytes 196616 | tf_op jit(solution)/shard_map/ppermute | solution.py:39
  139.6 21.5 %all-to-all-start.3 = ((bf16[8,16,4096]{2,1,0:T(8,128)(2,1)}), bf16[8,16,4096]{2,1,0:T(8,128)(2,1)}, u32[]{:S(2)}, u32[]{:S(2)}) async-start(bf16[8,16,4096]{2,1,0:T(8,128)(2,1)} %bitcast.34), calls=%async_computation.3 | async-start | bytes 2097152 | tf_op jit(solution)/shard_map/all_to_all | solution.py:67
  145.8 0.9 copy-start.6
  145.8 1.0 copy-start.10
  145.8 1.0 copy-start.25
  145.8 1.2 copy-start.12
  145.9 1.2 copy-start.26
  145.9 3.4 %copy-start.21 = (bf16[2,128,512]{2,1,0:T(8,128)(2,1)S(1)}, bf16[2,128,512]{2,1,0:T(8,128)(2,1)}, u32[]{:S(2)}) copy-start(bf16[2,128,512]{2,1,0:T(8,128)(2,1)} %copy-done.20) | copy-start | bytes 786436
  146.0 17.5 %copy-start.19 = (bf16[16,16,2048]{2,1,0:T(8,128)(2,1)}, bf16[16,16,2048]{2,1,0:T(8,128)(2,1)S(1)}, u32[]{:S(2)}) copy-start(bf16[16,16,2048]{2,1,0:T(8,128)(2,1)S(1)} %pad_maximum_fusion) | copy-start | bytes 3145732
  146.0 15.1 %copy-start.8 = (bf16[16,4096]{1,0:T(8,128)(2,1)S(1)}, bf16[16,4096]{1,0:T(8,128)(2,1)}, u32[]{:S(2)}) copy-start(bf16[16,4096]{1,0:T(8,128)(2,1)} %copy-done.7) | copy-start | bytes 393220
  146.1 15.1 %copy-start.16 = (bf16[16,16,256]{2,1,0:T(8,128)(2,1)S(1)}, bf16[16,16,256]{2,1,0:T(8,128)(2,1)}, u32[]{:S(2)}) copy-start(bf16[16,16,256]{2,1,0:T(8,128)(2,1)} %copy-done.15) | copy-start | bytes 393220
  146.1 4.0 %collective-permute-start.12 = (bf16[256,2048]{1,0:T(8,128)(2,1)S(1)}, bf16[256,2048]{1,0:T(8,128)(2,1)}, u32[]{:S(2)}, u32[]{:S(2)}) collective-permute-start(bf16[256,2048]{1,0:T(8,128)(2,1)S(1)} %bitcast.40), channel_id=1, source_target_pairs={{0,1},{1,0},{2,3},{3,2},{4,5},{5,4},{6,7},{7,6},{8,9},{9,8},{10,11... | collective-permute-start | bytes 3145736 | tf_op jit(solution)/shard_map/ppermute | solution.py:35
  147.9 29.7 %collective-permute-start.14 = (bf16[2,384,256]{2,1,0:T(8,128)(2,1)}, bf16[2,384,256]{2,1,0:T(8,128)(2,1)}, u32[]{:S(2)}, u32[]{:S(2)}) collective-permute-start(bf16[2,384,256]{2,1,0:T(8,128)(2,1)} %pad_maximum_fusion.1.here_ref), channel_id=1, source_target_pairs={{0,240},{16,224},{32,208},{48,192},{64,176},{80,160},{96,144},{112... | collective-permute-start | bytes 1179656 | tf_op jit(solution)/shard_map/ppermute | solution.py:47
  150.0 21.9 %collective-permute-start.13 = (bf16[2,2,128,256]{3,2,1,0:T(8,128)(2,1)}, bf16[2,2,128,256]{3,2,1,0:T(8,128)(2,1)}, u32[]{:S(2)}, u32[]{:S(2)}) collective-permute-start(bf16[2,2,128,256]{3,2,1,0:T(8,128)(2,1)} %pad_maximum_fusion.4), channel_id=1, source_target_pairs={{0,1},{1,0},{2,3},{3,2},{4,5},{5,4},{6,7},{7,6},{8,9},{9,8},{10,11... | collective-permute-start | bytes 786440 | tf_op jit(solution)/shard_map/ppermute | solution.py:35
  164.2 40.5 %all-to-all-start.4 = ((bf16[16,64,256]{2,1,0:T(8,128)(2,1)}), bf16[16,64,256]{2,1,0:T(8,128)(2,1)S(1)}, u32[]{:S(2)}, u32[]{:S(2)}) async-start(bf16[16,64,256]{2,1,0:T(8,128)(2,1)} %get-tuple-element.74), calls=%async_computation.4 | async-start | bytes 1048576 | tf_op jit(solution)/shard_map/all_to_all | solution.py:71
  171.7 7.3 %collective-permute-start.15 = (bf16[2,256,256]{2,1,0:T(8,128)(2,1)S(1)}, bf16[2,256,256]{2,1,0:T(8,128)(2,1)S(1)}, u32[]{:S(2)}, u32[]{:S(2)}) collective-permute-start(bf16[2,256,256]{2,1,0:T(8,128)(2,1)S(1)} %fusion), channel_id=1, source_target_pairs={{0,1},{1,0},{2,3},{3,2},{4,5},{5,4},{6,7},{7,6},{8,9},{9,8},{10,11... | collective-permute-start | bytes 786440 | tf_op jit(solution)/shard_map/ppermute | solution.py:35
  178.5 1.6 collective-permute-start.16
  179.0 1.2 copy-start.22
  180.1 0.7 copy-start.23
  188.3 14.7 %collective-permute-start.17 = (bf16[512,256]{1,0:T(8,128)(2,1)S(1)}, bf16[512,256]{1,0:T(8,128)(2,1)S(1)}, u32[]{:S(2)}, u32[]{:S(2)}) collective-permute-start(bf16[512,256]{1,0:T(8,128)(2,1)S(1)} %constant_dynamic-slice_fusion), channel_id=1, source_target_pairs={{0,240},{1,241},{4,244},{5,245},{8,248},{9,249},{12,252},{13,253},... | collective-permute-start | bytes 786440 | tf_op jit(solution)/shard_map/ppermute | solution.py:31
  (2 other events, 1.3 us)
Sparse Core Ops, SparseCore 0:
  92.0 57.1 all-gather.1

commit v5 on v3

--- a/solution.py
+++ b/solution.py
@@ -501,11 +501,12 @@
 
     after, blocks_1 = finish(1, chip, terms_1, rows, grad_rows, blocks_0)
     out = exchange16(blocks_1)
-    after, x_all, late_m = together(after, x_all, late_m)
+    after, x_all = together(after, x_all)
+    x_all = x_all.reshape(16, 96, HALF)
+    grad_output = output_columns(core, x_all, g_near, g_far, [attended, att_m, att_far])
+    grad_output, late_m = together(grad_output, late_m)
     far_late = swap_core(late_m[:, TOK:])
-    x_all = x_all.reshape(16, 96, HALF)
     grad_query, acc_kv = columns(core, x_all, after, [here, late_m, far_here, far_late])
-    grad_output = output_columns(core, x_all, g_near, g_far, [attended, att_m, att_far])
     kept = lax.dynamic_slice_in_dim(acc_kv, half * 512, 512, 0)
     given = lax.dynamic_slice_in_dim(acc_kv, (1 - half) * 512, 512, 0)
     taken = send(given, lambda s, c: (15 - s, c) if c // 2 % 2 == s // 8 else None)

time: 210 us -> 213 us (1.014)
  starting transfers between devices: 55.3 us -> 53.1 us
  waiting for transfers between devices: 56.6 us -> 58.8 us
    ppermute x3, waiting for transfers between devices: 11.6 us -> 17.8 us  [send(): return lax.ppermute(x, ('section', 'tensor'), pairs)]
    all_to_all x2, starting transfers between devices: 15.9 us -> 13.5 us  [exchange16(): return lax.all_to_all(x, 'tensor', 0, 0, tiled=True)]
    ppermute x3, waiting for transfers between devices: 5.17 us -> 2.75 us  [mirror(): return lax.ppermute(x, 'section', [(i, 15 - i) for i in range(16)])]
    unnamed x60 -> x52, local copies, waits for them, and re-layouts: 8.72 us -> 8.55 us
  transfers between devices with their start and end apart: 23 -> 23, of which waited for: 9 -> 8; matrix products, arithmetic and copies ran while one was open for 4% -> 5% of each run, Pallas kernels for 16% -> 16%
where the time goes in v5:
time: 213 us; the launch traced here: 211 us
  waiting for transfers between devices  58.8 us (28%)
  starting transfers between devices  53.1 us (25%)
  Pallas kernels  33.3 us (16%)
  blocking collectives  29.7 us (14%)
  local copies, waits for them, and re-layouts  14.5 us (7%)
  between operations  14.5 us (7%)
  other arithmetic  7.2 us (3%)
    all_to_all x1, blocking collectives, exchange8(): lax.all_to_all(x, 'tensor', 0, 0, axis_index_groups=SAME_CORE, tiled=True)  29.7 us
    ppermute x2, waiting for transfers between devices, swap_z(): return lax.ppermute(x, 'tensor', [(i, i ^ 2) for i in range(16)])  17.8 us
    ppermute x3, waiting for transfers between devices, send(): return lax.ppermute(x, ('section', 'tensor'), pairs)  17.8 us
    pallas_call x2, Pallas kernels, back(): pl.pallas_call(functools.partial(back_kernel, tick), out_shape=(jax.Shape...  14.7 us
    all_to_all x2, starting transfers between devices, exchange16(): return lax.all_to_all(x, 'tensor', 0, 0, tiled=True)  13.5 us
    all_to_all x2, starting transfers between devices, exchange8(): lax.all_to_all(x, 'tensor', 0, 0, axis_index_groups=SAME_CORE, tiled=True)  13.2 us
    ppermute x3, starting transfers between devices, mirror(): return lax.ppermute(x, 'section', [(i, 15 - i) for i in range(16)])  10.5 us
    all_to_all x2, waiting for transfers between devices, exchange8(): lax.all_to_all(x, 'tensor', 0, 0, axis_index_groups=SAME_CORE, tiled=True)  9.06 us
  transfers between devices with their start and end apart: 23, of which 8 were waited for; matrix products, arithmetic and copies ran while one was open for 5% of the time, Pallas kernels for 16%

profile of v5, /device:TPU:96, one launch (start us, length us, event | category | flops | bytes accessed | tf_op | source)
XLA Modules:
  0.0 211.1 jit_solution(6658255271689259065)
XLA Ops:
  7.8 0.9 copy-done.11
  8.7 0.9 copy-done.15
  9.6 1.2 shard_map.102
  10.8 5.9 %all-to-all-start = ((bf16[16,160,256]{2,1,0:T(8,128)(2,1)}), bf16[16,160,256]{2,1,0:T(8,128)(2,1)S(1)}, u32[]{:S(2)}, u32[]{:S(2)}) async-start(bf16[16,160,256]{2,1,0:T(8,128)(2,1)} %shard_map.102), calls=%async_computation | async-start | bytes 2621440 | tf_op jit(solution)/shard_map/all_to_all | solution.py:71
  17.9 3.4 %collective-permute-done.5 = bf16[2,128,256]{2,1,0:T(8,128)(2,1)S(1)} collective-permute-done((bf16[2,128,256]{2,1,0:T(8,128)(2,1)S(1)}, bf16[2,128,256]{2,1,0:T(8,128)(2,1)S(1)}, u32[]{:S(2)}, u32[]{:S(2)}) %collective-permute-start.5) | collective-permute-done | bytes 131104 | tf_op jit(solution)/shard_map/ppermute | solution.py:35
  21.3 2.7 %shard_map.104 = (f32[2,4,128,128]{3,2,1,0:T(8,128)S(1)}, bf16[2,128,512]{2,1,0:T(8,128)(2,1)S(1)}) custom-call(bf16[2,128,512]{2,1,0:T(8,128)(2,1)S(1)} %pad_maximum_fusion.3.q_ref, bf16[2,128,256]{2,1,0:T(8,128)(2,1)S(1)} %dynamic-slice_bitcast_fusion.kv_ref), custom_call_target="tpu_custom_call" | custom-call | tf_op jit(solution)/shard_map/pallas_call | solution.py:134
  24.0 5.9 %collective-permute-start.6 = (bf16[2,128,512]{2,1,0:T(8,128)(2,1)S(1)}, bf16[2,128,512]{2,1,0:T(8,128)(2,1)S(1)}, u32[]{:S(2)}, u32[]{:S(2)}) collective-permute-start(bf16[2,128,512]{2,1,0:T(8,128)(2,1)S(1)} %get-tuple-element.57.here), channel_id=1, source_target_pairs={{0,240},{16,224},{32,208},{48,192},{64,176},{80,160},{96,144},{112... | collective-permute-start | bytes 786440 | tf_op jit(solution)/shard_map/ppermute | solution.py:47
  29.9 8.0 %all-to-all-done.rows_ref.g_hbm.refs_2_ = bf16[16,160,256]{2,1,0:T(8,128)(2,1)S(1)} async-done(((bf16[16,160,256]{2,1,0:T(8,128)(2,1)}), bf16[16,160,256]{2,1,0:T(8,128)(2,1)S(1)}, u32[]{:S(2)}, u32[]{:S(2)}) %all-to-all-start) | async-done | bytes 1310752 | tf_op jit(solution)/shard_map/all_to_all | solution.py:71
  38.1 0.6 copy-done.16
  38.7 7.2 %shard_map.105 = (bf16[128,4096]{1,0:T(8,128)(2,1)S(1)}, bf16[384,256]{1,0:T(8,128)(2,1)S(1)}) custom-call(bf16[16,160,256]{2,1,0:T(8,128)(2,1)S(1)} %all-to-all-done.rows_ref.g_hbm.refs_2_, bf16[4096,256]{1,0:T(8,128)(2,1)} %collective-permute-done.2.wo_own_ref, bf16[4096,256]{1,0:T(8,128)(2,1)} %collective-permute-done.wo_far_ref, ...), custom_call_target="tpu_custom_call" | custom-call | tf_op jit(solution)/shard_map/pallas_call | solution.py:206
  46.0 1.0 copy-done.4
  47.0 0.7 copy-done.19
  47.7 7.4 %all-to-all-start.1 = ((bf16[8,16,4096]{2,1,0:T(8,128)(2,1)}), bf16[8,16,4096]{2,1,0:T(8,128)(2,1)S(1)}, u32[]{:S(2)}, u32[]{:S(2)}) async-start(bf16[8,16,4096]{2,1,0:T(8,128)(2,1)} %bitcast.35), calls=%async_computation.1 | async-start | bytes 2097152 | tf_op jit(solution)/shard_map/all_to_all | solution.py:67
  55.4 3.1 %collective-permute-start.7 = (bf16[48,2048]{1,0:T(8,128)(2,1)}, bf16[48,2048]{1,0:T(8,128)(2,1)}, u32[]{:S(2)}, u32[]{:S(2)}) collective-permute-start(bf16[48,2048]{1,0:T(8,128)(2,1)} %copy-done.16), channel_id=1, source_target_pairs={{0,240},{16,224},{32,208},{48,192},{64,176},{80,160},{96,144},{112... | collective-permute-start | bytes 589832 | tf_op jit(solution)/shard_map/ppermute | solution.py:47
  58.5 13.5 %collective-permute-done.10 = bf16[128,256]{1,0:T(8,128)(2,1)S(1)} collective-permute-done((bf16[128,256]{1,0:T(8,128)(2,1)S(1)}, bf16[128,256]{1,0:T(8,128)(2,1)S(1)}, u32[]{:S(2)}, u32[]{:S(2)}) %collective-permute-start.10) | collective-permute-done | bytes 65568 | tf_op jit(solution)/shard_map/ppermute | solution.py:39
  72.0 0.6 add_convert_fusion.1
  72.6 2.7 %collective-permute-done.7 = bf16[48,2048]{1,0:T(8,128)(2,1)} collective-permute-done((bf16[48,2048]{1,0:T(8,128)(2,1)}, bf16[48,2048]{1,0:T(8,128)(2,1)}, u32[]{:S(2)}, u32[]{:S(2)}) %collective-permute-start.7) | collective-permute-done | bytes 196640 | tf_op jit(solution)/shard_map/ppermute | solution.py:47
  76.3 1.9 collective-permute-start.8
  78.2 5.1 %collective-permute-start.9 = (bf16[16,2048]{1,0:T(8,128)(2,1)S(1)}, bf16[16,2048]{1,0:T(8,128)(2,1)S(1)}, u32[]{:S(2)}, u32[]{:S(2)}) collective-permute-start(bf16[16,2048]{1,0:T(8,128)(2,1)S(1)} %constant_dynamic-slice_fusion.2), channel_id=1, source_target_pairs={{1,225},{3,227},{5,229},{7,231},{9,233},{11,235},{13,237},{15,239}... | collective-permute-start | bytes 196616 | tf_op jit(solution)/shard_map/ppermute | solution.py:31
  83.3 1.7 pad_maximum_fusion.2
  85.0 5.4 %collective-permute-done.9 = bf16[16,2048]{1,0:T(8,128)(2,1)S(1)} collective-permute-done((bf16[16,2048]{1,0:T(8,128)(2,1)S(1)}, bf16[16,2048]{1,0:T(8,128)(2,1)S(1)}, u32[]{:S(2)}, u32[]{:S(2)}) %collective-permute-start.9) | collective-permute-done | bytes 65568 | tf_op jit(solution)/shard_map/ppermute | solution.py:31
  90.4 1.3 broadcast_in_dim.15
  91.8 29.7 %all_to_all.25.g_hbm = bf16[8,16,6144]{2,1,0:T(8,128)(2,1)S(1)} all-to-all(bf16[8,16,6144]{2,1,0:T(8,128)(2,1)} %broadcast_in_dim.15), channel_id=1, replica_groups={{0,2,4,6,8,10,12,14},{1,3,5,7,9,11,13,15},{16,18,20,22,24,26,28,30},{17..., dimensions={0} | all-to-all | bytes 3145728 | tf_op jit(solution)/shard_map/all_to_all | solution.py:67
  121.5 7.5 %shard_map.107 = (bf16[128,4096]{1,0:T(8,128)(2,1)S(1)}, bf16[384,256]{1,0:T(8,128)(2,1)}) custom-call(bf16[8,16,6144]{2,1,0:T(8,128)(2,1)S(1)} %all_to_all.25.g_hbm, bf16[4096,256]{1,0:T(8,128)(2,1)} %collective-permute-done.2.wo_own_ref, bf16[4096,256]{1,0:T(8,128)(2,1)} %collective-permute-done.wo_far_ref, ...), custom_call_target="tpu_custom_call" | custom-call | tf_op jit(solution)/shard_map/pallas_call | solution.py:206
  129.0 1.0 copy-done.3
  130.0 0.8 slice.28
  130.8 5.0 %collective-permute-start.11 = (bf16[128,256]{1,0:T(8,128)(2,1)S(1)}, bf16[128,256]{1,0:T(8,128)(2,1)S(1)}, u32[]{:S(2)}, u32[]{:S(2)}) collective-permute-start(bf16[128,256]{1,0:T(8,128)(2,1)S(1)} %slice.28), channel_id=1, source_target_pairs={{0,2},{1,3},{2,0},{3,1},{4,6},{5,7},{6,4},{7,5},{8,10},{9,11},{10,... | collective-permute-start | bytes 196616 | tf_op jit(solution)/shard_map/ppermute | solution.py:39
  135.8 4.3 %collective-permute-done.11 = bf16[128,256]{1,0:T(8,128)(2,1)S(1)} collective-permute-done((bf16[128,256]{1,0:T(8,128)(2,1)S(1)}, bf16[128,256]{1,0:T(8,128)(2,1)S(1)}, u32[]{:S(2)}, u32[]{:S(2)}) %collective-permute-start.11) | collective-permute-done | bytes 65568 | tf_op jit(solution)/shard_map/ppermute | solution.py:39
  140.1 1.5 add_convert_fusion
  141.6 5.8 %all-to-all-start.3 = ((bf16[8,16,4096]{2,1,0:T(8,128)(2,1)}), bf16[8,16,4096]{2,1,0:T(8,128)(2,1)}, u32[]{:S(2)}, u32[]{:S(2)}) async-start(bf16[8,16,4096]{2,1,0:T(8,128)(2,1)} %bitcast.34), calls=%async_computation.3 | async-start | bytes 2097152 | tf_op jit(solution)/shard_map/all_to_all | solution.py:67
  148.4 0.9 slice.31
  149.4 1.6 collective-permute-start.14
  151.0 0.7 pad_maximum_fusion.4
  151.8 0.7 fusion
  153.0 9.1 %all-to-all-done.3.refs_1_ = bf16[8,16,4096]{2,1,0:T(8,128)(2,1)} async-done(((bf16[8,16,4096]{2,1,0:T(8,128)(2,1)}), bf16[8,16,4096]{2,1,0:T(8,128)(2,1)}, u32[]{:S(2)}, u32[]{:S(2)}) %all-to-all-start.3) | async-done | bytes 1048608 | tf_op jit(solution)/shard_map/all_to_all | solution.py:67
  162.1 2.2 %shard_map.108 = (bf16[16,4096]{1,0:T(8,128)(2,1)S(1)}, bf16[16,32,256]{2,1,0:T(8,128)(2,1)}) custom-call(s32[1]{0:T(128)} %bitcast.chip_ref.refs_0_, bf16[8,16,4096]{2,1,0:T(8,128)(2,1)} %all-to-all-done.3.refs_1_, bf16[16,160,256]{2,1,0:T(8,128)(2,1)S(1)} %all-to-all-done.rows_ref.g_hbm.refs_2_, bf16[16,4096]{1,0:T(8,128)(2,1)S(1)} %copy-done.8, ...), custom_call_target="tpu_custom_call" | custom-call | tf_op jit(solution)/shard_map/pallas_call | solution.py:264
  164.3 0.7 copy-done.12
  164.9 5.6 %shard_map.109 = bf16[2048,256]{1,0:T(8,128)(2,1)} custom-call(s32[1]{0:T(128)} %bitcast.16.core_ref, bf16[16,96,2048]{2,1,0:T(8,128)(2,1)} %bitcast.38, bf16[256,2048]{1,0:T(8,128)(2,1)} %bitcast.41, bf16[256,2048]{1,0:T(8,128)(2,1)} %collective-permute-done.12.far_hbm, bf16[2,128,512]{2,1,0:T(8,128)(2,1)} %copy-done.5, bf16[2,128,512]{2,1,0:T(8,128)(2,1)} %copy-done.19, ...), custom_call_target="tpu_custom_call" | custom-call | flops 1000 | bytes 1000 | tf_op jit(solution)/shard_map/pallas_call | solution.py:400
  170.6 1.0 slice.35
  171.7 7.5 %all-to-all-start.4 = ((bf16[16,32,256]{2,1,0:T(8,128)(2,1)}), bf16[16,32,256]{2,1,0:T(8,128)(2,1)S(1)}, u32[]{:S(2)}, u32[]{:S(2)}) async-start(bf16[16,32,256]{2,1,0:T(8,128)(2,1)} %get-tuple-element.74), calls=%async_computation.4 | async-start | bytes 524288 | tf_op jit(solution)/shard_map/all_to_all | solution.py:71
  179.2 0.7 copy-done.21
  179.9 0.7 copy-done.22
  180.6 6.5 %shard_map.110 = (bf16[2048,256]{1,0:T(8,128)(2,1)}, bf16[1024,256]{1,0:T(8,128)(2,1)}) custom-call(s32[1]{0:T(128)} %bitcast.16.core_ref, bf16[16,96,2048]{2,1,0:T(8,128)(2,1)} %bitcast.39, bf16[16,4096]{1,0:T(8,128)(2,1)} %copy-done.12, bf16[2,384,256]{2,1,0:T(8,128)(2,1)} %copy-done.18, bf16[2,384,256]{2,1,0:T(8,128)(2,1)} %collective-permute-done.14.got_ref, ...), custom_call_target="tpu_custom_call" | custom-call | flops 1000 | bytes 1000 | tf_op jit(solution)/shard_map/pallas_call | solution.py:352
  187.1 1.0 constant_dynamic-slice_fusion
  188.1 1.3 collective-permute-start.17
  189.4 0.7 copy.11
  190.1 12.4 %collective-permute-done.17 = bf16[512,256]{1,0:T(8,128)(2,1)S(1)} collective-permute-done((bf16[512,256]{1,0:T(8,128)(2,1)S(1)}, bf16[512,256]{1,0:T(8,128)(2,1)S(1)}, u32[]{:S(2)}, u32[]{:S(2)}) %collective-permute-start.17) | collective-permute-done | bytes 262176 | tf_op jit(solution)/shard_map/ppermute | solution.py:31
  202.6 1.7 select_bitcast_fusion
  (87 shorter events, 4.9 us)
Async XLA Ops:
  7.2 10.7 %copy-start = (bf16[2,2,1,128,256]{4,3,2,1,0:T(8,128)(2,1)S(1)}, bf16[2,2,1,128,256]{4,3,2,1,0:T(8,128)(2,1)}, u32[]{:S(2)}) copy-start(bf16[2,2,1,128,256]{4,3,2,1,0:T(8,128)(2,1)} %param.12) | copy-start | bytes 786436
  7.2 9.7 %collective-permute-start = (bf16[4096,256]{1,0:T(8,128)(2,1)}, bf16[4096,256]{1,0:T(8,128)(2,1)}, u32[]{:S(2)}, u32[]{:S(2)}) collective-permute-start(bf16[4096,256]{1,0:T(8,128)(2,1)} %bitcast.45), channel_id=1, source_target_pairs={{0,1},{1,0},{2,3},{3,2},{4,5},{5,4},{6,7},{7,6},{8,9},{9,8},{10,11... | collective-permute-start | bytes 6291464 | tf_op jit(solution)/shard_map/ppermute | solution.py:35
  7.3 10.0 %collective-permute-start.1 = (bf16[4096,256]{1,0:T(8,128)(2,1)}, bf16[4096,256]{1,0:T(8,128)(2,1)}, u32[]{:S(2)}, u32[]{:S(2)}) collective-permute-start(bf16[4096,256]{1,0:T(8,128)(2,1)} %bitcast.46), channel_id=1, source_target_pairs={{0,1},{1,0},{2,3},{3,2},{4,5},{5,4},{6,7},{7,6},{8,9},{9,8},{10,11... | collective-permute-start | bytes 6291464 | tf_op jit(solution)/shard_map/ppermute | solution.py:35
  7.8 0.9 copy-start.11
  8.7 0.9 copy-start.15
  9.6 7.8 %copy-start.23 = (bf16[2,2,1,128,256]{4,3,2,1,0:T(8,128)(2,1)S(1)}, bf16[2,2,1,128,256]{4,3,2,1,0:T(8,128)(2,1)}, u32[]{:S(2)}) copy-start(bf16[2,2,1,128,256]{4,3,2,1,0:T(8,128)(2,1)} %param.11) | copy-start | bytes 786436
  10.8 27.1 %all-to-all-start = ((bf16[16,160,256]{2,1,0:T(8,128)(2,1)}), bf16[16,160,256]{2,1,0:T(8,128)(2,1)S(1)}, u32[]{:S(2)}, u32[]{:S(2)}) async-start(bf16[16,160,256]{2,1,0:T(8,128)(2,1)} %shard_map.102), calls=%async_computation | async-start | bytes 2621440 | tf_op jit(solution)/shard_map/all_to_all | solution.py:71
  16.8 21.3 %collective-permute-start.4 = (bf16[4096,256]{1,0:T(8,128)(2,1)}, bf16[4096,256]{1,0:T(8,128)(2,1)}, u32[]{:S(2)}, u32[]{:S(2)}) collective-permute-start(bf16[4096,256]{1,0:T(8,128)(2,1)} %bitcast.47), channel_id=1, source_target_pairs={{0,1},{1,0},{2,3},{3,2},{4,5},{5,4},{6,7},{7,6},{8,9},{9,8},{10,11... | collective-permute-start | bytes 6291464 | tf_op jit(solution)/shard_map/ppermute | solution.py:35
  16.9 21.2 %collective-permute-start.2 = (bf16[4096,256]{1,0:T(8,128)(2,1)}, bf16[4096,256]{1,0:T(8,128)(2,1)}, u32[]{:S(2)}, u32[]{:S(2)}) collective-permute-start(bf16[4096,256]{1,0:T(8,128)(2,1)} %collective-permute-done.wo_far_ref), channel_id=1, source_target_pairs={{0,1},{1,0},{2,3},{3,2},{4,5},{5,4},{6,7},{7,6},{8,9},{9,8},{10,11... | collective-permute-start | bytes 6291464 | tf_op jit(solution)/shard_map/ppermute | solution.py:35
  17.3 20.8 %collective-permute-start.3 = (bf16[4096,256]{1,0:T(8,128)(2,1)}, bf16[4096,256]{1,0:T(8,128)(2,1)}, u32[]{:S(2)}, u32[]{:S(2)}) collective-permute-start(bf16[4096,256]{1,0:T(8,128)(2,1)} %collective-permute-done.1.wq_far_ref), channel_id=1, source_target_pairs={{0,1},{1,0},{2,3},{3,2},{4,5},{5,4},{6,7},{7,6},{8,9},{9,8},{10,11... | collective-permute-start | bytes 6291464 | tf_op jit(solution)/shard_map/ppermute | solution.py:35
  17.4 3.8 %collective-permute-start.5 = (bf16[2,128,256]{2,1,0:T(8,128)(2,1)S(1)}, bf16[2,128,256]{2,1,0:T(8,128)(2,1)S(1)}, u32[]{:S(2)}, u32[]{:S(2)}) collective-permute-start(bf16[2,128,256]{2,1,0:T(8,128)(2,1)S(1)} %get-tuple-element.91), channel_id=1, source_target_pairs={{0,1},{1,0},{2,3},{3,2},{4,5},{5,4},{6,7},{7,6},{8,9},{9,8},{10,11... | collective-permute-start | bytes 393224 | tf_op jit(solution)/shard_map/ppermute | solution.py:35
  24.0 22.0 %copy-start.1 = (f32[2,4,128,128]{3,2,1,0:T(8,128)}, f32[2,4,128,128]{3,2,1,0:T(8,128)S(1)}, u32[]{:S(2)}) copy-start(f32[2,4,128,128]{3,2,1,0:T(8,128)S(1)} %get-tuple-element.55.attention_ref) | copy-start | bytes 1572868
  24.0 22.0 %copy-start.5 = (bf16[2,128,512]{2,1,0:T(8,128)(2,1)}, bf16[2,128,512]{2,1,0:T(8,128)(2,1)S(1)}, u32[]{:S(2)}) copy-start(bf16[2,128,512]{2,1,0:T(8,128)(2,1)S(1)} %get-tuple-element.57.here) | copy-start | bytes 786436
  24.0 23.0 %collective-permute-start.6 = (bf16[2,128,512]{2,1,0:T(8,128)(2,1)S(1)}, bf16[2,128,512]{2,1,0:T(8,128)(2,1)S(1)}, u32[]{:S(2)}, u32[]{:S(2)}) collective-permute-start(bf16[2,128,512]{2,1,0:T(8,128)(2,1)S(1)} %get-tuple-element.57.here), channel_id=1, source_target_pairs={{0,240},{16,224},{32,208},{48,192},{64,176},{80,160},{96,144},{112... | collective-permute-start | bytes 786440 | tf_op jit(solution)/shard_map/ppermute | solution.py:47
  38.1 0.7 copy-start.16
  46.0 1.0 copy-start.4
  47.0 28.7 %copy-start.9 = (bf16[384,256]{1,0:T(8,128)(2,1)}, bf16[384,256]{1,0:T(8,128)(2,1)S(1)}, u32[]{:S(2)}) copy-start(bf16[384,256]{1,0:T(8,128)(2,1)S(1)} %get-tuple-element.79) | copy-start | bytes 589828
  47.0 0.7 copy-start.19
  47.7 27.6 %all-to-all-start.1 = ((bf16[8,16,4096]{2,1,0:T(8,128)(2,1)}), bf16[8,16,4096]{2,1,0:T(8,128)(2,1)S(1)}, u32[]{:S(2)}, u32[]{:S(2)}) async-start(bf16[8,16,4096]{2,1,0:T(8,128)(2,1)} %bitcast.35), calls=%async_computation.1 | async-start | bytes 2097152 | tf_op jit(solution)/shard_map/all_to_all | solution.py:67
  55.1 106.9 %all-gather.2.cloned.1.call-start = ((), (), s32[]{:S(2)}) async-start(), calls=%async_computation.5 | async-start | bytes 6684672 | tf_op jit(solution)/shard_map/all_gather | solution.py:75
  55.2 16.8 %collective-permute-start.10 = (bf16[128,256]{1,0:T(8,128)(2,1)S(1)}, bf16[128,256]{1,0:T(8,128)(2,1)S(1)}, u32[]{:S(2)}, u32[]{:S(2)}) collective-permute-start(bf16[128,256]{1,0:T(8,128)(2,1)S(1)} %slice.27), channel_id=1, source_target_pairs={{0,2},{1,3},{2,0},{3,1},{4,6},{5,7},{6,4},{7,5},{8,10},{9,11},{10,... | collective-permute-start | bytes 196616 | tf_op jit(solution)/shard_map/ppermute | solution.py:39
  55.4 19.9 %collective-permute-start.7 = (bf16[48,2048]{1,0:T(8,128)(2,1)}, bf16[48,2048]{1,0:T(8,128)(2,1)}, u32[]{:S(2)}, u32[]{:S(2)}) collective-permute-start(bf16[48,2048]{1,0:T(8,128)(2,1)} %copy-done.16), channel_id=1, source_target_pairs={{0,240},{16,224},{32,208},{48,192},{64,176},{80,160},{96,144},{112... | collective-permute-start | bytes 589832 | tf_op jit(solution)/shard_map/ppermute | solution.py:47
  76.3 14.1 %collective-permute-start.8 = (bf16[16,4096]{1,0:T(8,128)(2,1)S(1)}, bf16[16,4096]{1,0:T(8,128)(2,1)S(1)}, u32[]{:S(2)}, u32[]{:S(2)}) collective-permute-start(bf16[16,4096]{1,0:T(8,128)(2,1)S(1)} %get-tuple-element.63), channel_id=1, source_target_pairs={{1,17},{3,19},{5,21},{7,23},{9,25},{11,27},{13,29},{15,31},{16,0},... | collective-permute-start | bytes 393224 | tf_op jit(solution)/shard_map/ppermute | solution.py:31
  78.2 12.2 %collective-permute-start.9 = (bf16[16,2048]{1,0:T(8,128)(2,1)S(1)}, bf16[16,2048]{1,0:T(8,128)(2,1)S(1)}, u32[]{:S(2)}, u32[]{:S(2)}) collective-permute-start(bf16[16,2048]{1,0:T(8,128)(2,1)S(1)} %constant_dynamic-slice_fusion.2), channel_id=1, source_target_pairs={{1,225},{3,227},{5,229},{7,231},{9,233},{11,235},{13,237},{15,239}... | collective-permute-start | bytes 196616 | tf_op jit(solution)/shard_map/ppermute | solution.py:31
  90.4 1.4 copy-start.7
  91.8 29.7 %copy-start.2 = (f32[2,4,128,128]{3,2,1,0:T(8,128)S(1)}, f32[2,4,128,128]{3,2,1,0:T(8,128)}, u32[]{:S(2)}) copy-start(f32[2,4,128,128]{3,2,1,0:T(8,128)} %copy-done.1) | copy-start | bytes 1572868
  129.0 1.0 copy-start.3
  130.8 9.3 %collective-permute-start.11 = (bf16[128,256]{1,0:T(8,128)(2,1)S(1)}, bf16[128,256]{1,0:T(8,128)(2,1)S(1)}, u32[]{:S(2)}, u32[]{:S(2)}) collective-permute-start(bf16[128,256]{1,0:T(8,128)(2,1)S(1)} %slice.28), channel_id=1, source_target_pairs={{0,2},{1,3},{2,0},{3,1},{4,6},{5,7},{6,4},{7,5},{8,10},{9,11},{10,... | collective-permute-start | bytes 196616 | tf_op jit(solution)/shard_map/ppermute | solution.py:39
  141.6 20.5 %all-to-all-start.3 = ((bf16[8,16,4096]{2,1,0:T(8,128)(2,1)}), bf16[8,16,4096]{2,1,0:T(8,128)(2,1)}, u32[]{:S(2)}, u32[]{:S(2)}) async-start(bf16[8,16,4096]{2,1,0:T(8,128)(2,1)} %bitcast.34), calls=%async_computation.3 | async-start | bytes 2097152 | tf_op jit(solution)/shard_map/all_to_all | solution.py:67
  147.3 1.0 copy-start.6
  147.3 1.0 copy-start.10
  147.4 1.0 copy-start.24
  147.4 1.9 copy-start.25
  147.4 3.6 %copy-start.20 = (bf16[2,128,512]{2,1,0:T(8,128)(2,1)S(1)}, bf16[2,128,512]{2,1,0:T(8,128)(2,1)}, u32[]{:S(2)}) copy-start(bf16[2,128,512]{2,1,0:T(8,128)(2,1)} %copy-done.19) | copy-start | bytes 786436
  147.6 16.7 %copy-start.17 = (bf16[16,16,2048]{2,1,0:T(8,128)(2,1)}, bf16[16,16,2048]{2,1,0:T(8,128)(2,1)S(1)}, u32[]{:S(2)}) copy-start(bf16[16,16,2048]{2,1,0:T(8,128)(2,1)S(1)} %pad_maximum_fusion) | copy-start | bytes 3145732
  147.6 14.5 %copy-start.8 = (bf16[16,4096]{1,0:T(8,128)(2,1)S(1)}, bf16[16,4096]{1,0:T(8,128)(2,1)}, u32[]{:S(2)}) copy-start(bf16[16,4096]{1,0:T(8,128)(2,1)} %copy-done.7) | copy-start | bytes 393220
  147.6 14.5 %copy-start.14 = (bf16[16,16,256]{2,1,0:T(8,128)(2,1)S(1)}, bf16[16,16,256]{2,1,0:T(8,128)(2,1)}, u32[]{:S(2)}) copy-start(bf16[16,16,256]{2,1,0:T(8,128)(2,1)} %copy-done.13) | copy-start | bytes 393220
  147.6 5.4 %collective-permute-start.12 = (bf16[256,2048]{1,0:T(8,128)(2,1)S(1)}, bf16[256,2048]{1,0:T(8,128)(2,1)}, u32[]{:S(2)}, u32[]{:S(2)}) collective-permute-start(bf16[256,2048]{1,0:T(8,128)(2,1)S(1)} %bitcast.40), channel_id=1, source_target_pairs={{0,1},{1,0},{2,3},{3,2},{4,5},{5,4},{6,7},{7,6},{8,9},{9,8},{10,11... | collective-permute-start | bytes 3145736 | tf_op jit(solution)/shard_map/ppermute | solution.py:35
  149.4 21.2 %copy-start.18 = (bf16[2,384,256]{2,1,0:T(8,128)(2,1)}, bf16[2,384,256]{2,1,0:T(8,128)(2,1)S(1)}, u32[]{:S(2)}) copy-start(bf16[2,384,256]{2,1,0:T(8,128)(2,1)S(1)} %pad_maximum_fusion.1.here_ref) | copy-start | bytes 1179652
  149.4 21.2 %collective-permute-start.14 = (bf16[2,384,256]{2,1,0:T(8,128)(2,1)S(1)}, bf16[2,384,256]{2,1,0:T(8,128)(2,1)}, u32[]{:S(2)}, u32[]{:S(2)}) collective-permute-start(bf16[2,384,256]{2,1,0:T(8,128)(2,1)S(1)} %pad_maximum_fusion.1.here_ref), channel_id=1, source_target_pairs={{0,240},{16,224},{32,208},{48,192},{64,176},{80,160},{96,144},{112... | collective-permute-start | bytes 1179656 | tf_op jit(solution)/shard_map/ppermute | solution.py:47
  151.8 13.2 %collective-permute-start.13 = (bf16[2,2,128,256]{3,2,1,0:T(8,128)(2,1)}, bf16[2,2,128,256]{3,2,1,0:T(8,128)(2,1)}, u32[]{:S(2)}, u32[]{:S(2)}) collective-permute-start(bf16[2,2,128,256]{3,2,1,0:T(8,128)(2,1)} %pad_maximum_fusion.4), channel_id=1, source_target_pairs={{0,1},{1,0},{2,3},{3,2},{4,5},{5,4},{6,7},{7,6},{8,9},{9,8},{10,11... | collective-permute-start | bytes 786440 | tf_op jit(solution)/shard_map/ppermute | solution.py:35
  152.5 26.7 %collective-permute-start.15 = (bf16[2,256,256]{2,1,0:T(8,128)(2,1)}, bf16[2,256,256]{2,1,0:T(8,128)(2,1)S(1)}, u32[]{:S(2)}, u32[]{:S(2)}) collective-permute-start(bf16[2,256,256]{2,1,0:T(8,128)(2,1)} %fusion), channel_id=1, source_target_pairs={{0,1},{1,0},{2,3},{3,2},{4,5},{5,4},{6,7},{7,6},{8,9},{9,8},{10,11... | collective-permute-start | bytes 786440 | tf_op jit(solution)/shard_map/ppermute | solution.py:35
  164.3 0.7 copy-start.12
  171.6 7.7 %collective-permute-start.16 = (bf16[2,256,256]{2,1,0:T(8,128)(2,1)S(1)}, bf16[2,256,256]{2,1,0:T(8,128)(2,1)S(1)}, u32[]{:S(2)}, u32[]{:S(2)}) collective-permute-start(bf16[2,256,256]{2,1,0:T(8,128)(2,1)S(1)} %slice.35), channel_id=1, source_target_pairs={{0,1},{1,0},{2,3},{3,2},{4,5},{5,4},{6,7},{7,6},{8,9},{9,8},{10,11... | collective-permute-start | bytes 786440 | tf_op jit(solution)/shard_map/ppermute | solution.py:35
  171.7 17.7 %all-to-all-start.4 = ((bf16[16,32,256]{2,1,0:T(8,128)(2,1)}), bf16[16,32,256]{2,1,0:T(8,128)(2,1)S(1)}, u32[]{:S(2)}, u32[]{:S(2)}) async-start(bf16[16,32,256]{2,1,0:T(8,128)(2,1)} %get-tuple-element.74), calls=%async_computation.4 | async-start | bytes 524288 | tf_op jit(solution)/shard_map/all_to_all | solution.py:71
  179.2 0.7 copy-start.21
  179.9 0.7 copy-start.22
  188.1 14.5 %collective-permute-start.17 = (bf16[512,256]{1,0:T(8,128)(2,1)S(1)}, bf16[512,256]{1,0:T(8,128)(2,1)S(1)}, u32[]{:S(2)}, u32[]{:S(2)}) collective-permute-start(bf16[512,256]{1,0:T(8,128)(2,1)S(1)} %constant_dynamic-slice_fusion), channel_id=1, source_target_pairs={{0,240},{1,241},{4,244},{5,245},{8,248},{9,249},{12,252},{13,253},... | collective-permute-start | bytes 786440 | tf_op jit(solution)/shard_map/ppermute | solution.py:31
  (1 other events, 0.6 us)
Sparse Core Ops, SparseCore 0:
  91.9 56.7 all-gather.1
